TPU v7x, 32 devices: a whole 2x2x4 slice. The times are simulated.
32 devices in a mesh: row: 4 (over y, core), seq: 8 (over z, x).
Axes of the slice: x: 2, y: 2, z: 4, core: 2. Of those that a mesh axis runs over, the one named last changes fastest.
Arguments:
- tokens: bfloat16 [16, 1024, 512], P('row', 'seq'), may hold values from -6 to 6
- first_len: int32 [16], P('row'), may hold values from 512 to 1024, as said below
- gain_one: float32 [512], replicated, may hold values from 0.5 to 1.5
- conv_weight: float32 [4, 512], replicated, may hold values from -3 to 3
- w_z: bfloat16 [512, 1024], replicated, may hold values from -0.25 to 0.25
- bias_z: float32 [1024], replicated, may hold values from -12 to -3
- w_h: bfloat16 [512, 1024], replicated, may hold values from -0.25 to 0.25
- w_out: bfloat16 [1024, 512], replicated, may hold values from -0.1875 to 0.1875
- gain_two: float32 [512], replicated, may hold values from 0.5 to 1.5
- w_up: bfloat16 [512, 2048], replicated, may hold values from -0.25 to 0.25
- w_down: bfloat16 [2048, 512], replicated, may hold values from -0.125 to 0.125
- cotangent: bfloat16 [16, 1024, 512], P('row', 'seq'), may hold values from -6 to 6
Outputs:
- output: bfloat16 [16, 1024, 512], P('row', 'seq')
- grad_tokens: bfloat16 [16, 1024, 512], P('row', 'seq')
- grad_gain_one: float32 [512], replicated
- grad_conv: float32 [4, 512], replicated
- grad_w_z: float32 [512, 1024], replicated
- grad_bias_z: float32 [1024], replicated
- grad_w_h: float32 [512, 1024], replicated
- grad_w_out: float32 [1024, 512], replicated
- grad_gain_two: float32 [512], replicated
- grad_w_up: float32 [512, 2048], replicated
- grad_w_down: float32 [2048, 512], replicated
Inputs may be any that keep to these rules, and one draw needn't show every extreme that they name: `first_len`: each entry is 1024 // 2 (a row of two documents) or 1024 (one document); in every aligned block of 4 rows both occur.
All inputs are finite; a program needn't handle non-finite values.
Results may differ from a plain program's by a relative error of at most 0.0075.
The roundings to bfloat16 on the way count: a program that leaves them out, or rounds other values in their place, can miss the bound.
Values sent between devices are 32-bit elements; how exact they have to be, the bound alone decides.
No kernel may reach another device: no remote copies, remote signals or barrier semaphores. Data moves between devices by JAX's collectives and lax.ppermute only.
A program may use at most 128 MiB of HBM per device.

v0:
```python
import functools

import jax
import jax.numpy as jnp
from jax import lax
from jax.experimental import pallas as pl
from jax.experimental.pallas import tpu as pltpu
from jax.sharding import PartitionSpec as P

F32, BF16 = jnp.float32, jnp.bfloat16
EPS = 1e-06
VMEM = pl.BlockSpec(memory_space=pltpu.VMEM)
SMEM = pl.BlockSpec(memory_space=pltpu.SMEM)
SUB = 8


def dot(left, right):
    return jnp.dot(left, right, preferred_element_type=F32)


def dot_lt(left, right):
    return lax.dot_general(left, right, (((0,), (0,)), ((), ())), preferred_element_type=F32)


def dot_rt(left, right):
    return lax.dot_general(left, right, (((1,), (1,)), ((), ())), preferred_element_type=F32)


def segment_order(tokens):
    steps = tokens // SUB
    to = lax.broadcasted_iota(jnp.int32, (tokens, tokens), 0)
    source = lax.broadcasted_iota(jnp.int32, (tokens, tokens), 1)
    return jnp.where(source == (to % SUB) * steps + to // SUB, 1.0, 0.0).astype(BF16)


def opened(first_len, seq_start, shape):
    sub = lax.broadcasted_iota(jnp.int32, shape, 0)
    rows = first_len.shape[0]
    result = jnp.ones(shape, F32)
    for r in range(rows):
        factor = jnp.where(first_len[r] == seq_start, 0.0, 1.0)
        result = jnp.where(sub == r * (SUB // rows), factor, result)
    return result


def at_row_start(shape, rows):
    return lax.broadcasted_iota(jnp.int32, shape, 0) % (SUB // rows) == 0


def at_row_end(shape, rows):
    parts = SUB // rows
    return lax.broadcasted_iota(jnp.int32, shape, 0) % parts == parts - 1


def rms(values):
    return lax.rsqrt(jnp.mean(values * values, axis=-1, keepdims=True) + EPS)


def fill_extended(ext, rim, first_len, seq_start, xhat_rim):
    lag, rows = rim.shape[1], rim.shape[0]
    width = ext.shape[-1]
    mask = opened(first_len, seq_start, (SUB, width))
    start = at_row_start((SUB, width), rows)
    total = ext.shape[0]
    for k in range(lag):
        near = pltpu.roll(ext[total - lag * SUB + k * SUB : total - lag * SUB + (k + 1) * SUB, :], 1, 0)
        ext[k * SUB : (k + 1) * SUB, :] = jnp.where(start, xhat_rim[k] * mask, near)


def rim_tiles(rim, spread):
    rows, lag, _ = rim.shape
    parts = SUB // rows
    spread[...] = jnp.zeros_like(spread)
    for k in range(lag):
        for r in range(rows):
            spread[k, r * parts : r * parts + 1, :] = rim[r, k : k + 1, :]
    return [spread[k] for k in range(lag)]


def gates_kernel(
    first_len, tokens, cotangent, rim, gain_one, conv_weight, w_z, bias_z, w_h,
    x_out, up_out, conv_out, keep_out, drive_out, cand_out, gate_out, pass_out, subk, subs, totals,
    ext, spread, lag_order,
):
    rows, group_len, width = tokens.shape
    count, lag = rows * group_len, rim.shape[1]
    hidden = w_z.shape[1]
    seq_start = lax.axis_index("seq") * group_len
    order = segment_order(count)
    x = dot(order, tokens[...].reshape(count, width))
    x_out[...] = x.astype(BF16)
    up_out[...] = dot(order, cotangent[...].reshape(count, width)).astype(BF16)
    normed = x * rms(x) * gain_one[...]
    ext[lag * SUB :, :] = normed
    rim_x = rim_tiles(rim, spread)
    fill_extended(ext, rim, first_len, seq_start, [v * rms(v) * gain_one[...] for v in rim_x])
    mixed = jnp.zeros((count, width), F32)
    for j in range(lag + 1):
        begin = (lag - j) * SUB
        mixed = mixed + conv_weight[j : j + 1, :] * ext[begin : begin + count, :]
    conv_low = mixed.astype(BF16)
    conv_out[...] = conv_low
    block = 256
    for b in range(hidden // block):
        cols = slice(b * block, (b + 1) * block)
        g = dot(conv_out[...], w_z[:, cols]) + bias_z[:, cols]
        c = dot(conv_out[...], w_h[:, cols])
        small = jnp.exp(-jnp.abs(g))
        large = 1.0 / (1.0 + small)
        small = small * large
        zeta = jnp.where(g >= 0, large, small)
        keep = jnp.where(g >= 0, small, large)
        sig = 1.0 / (1.0 + jnp.exp(-c))
        cand = jnp.where(c >= 0, c + 0.5, sig)
        keep_out[:, cols] = keep
        drive_out[:, cols] = zeta * cand
        cand_out[:, cols] = cand
        gate_out[:, cols] = small * large
        pass_out[:, cols] = zeta * jnp.where(c >= 0, 1.0, sig * (1.0 - sig))
    keep_out[0:SUB, :] = keep_out[0:SUB, :] * opened(first_len, seq_start, (SUB, hidden))

    def step(i, carry):
        total, state = carry
        at = pl.ds(pl.multiple_of(i * SUB, SUB), SUB)
        keep = keep_out[at, :]
        return total * keep, keep * state + drive_out[at, :]

    total, state = lax.fori_loop(
        0, count // SUB, step, (jnp.ones((SUB, hidden), F32), jnp.zeros((SUB, hidden), F32)), unroll=8
    )
    subk[...] = total
    subs[...] = state
    parts = SUB // rows
    for r in range(rows):
        at = slice(r * parts, r * parts + 1)
        k, s = subk[at, :], subs[at, :]
        for h in range(1, parts):
            at = slice(r * parts + h, r * parts + h + 1)
            s = subs[at, :] + subk[at, :] * s
            k = k * subk[at, :]
        totals[0, r : r + 1, :] = k
        totals[1, r : r + 1, :] = s


def mlp_kernel(
    first_len, carried, subk, subs, keep, drive, x, up, w_out, gain_two, w_up, w_down,
    state_out, before_out, low_out, middle_out, output, second_grad, grad_up, grad_down,
    second_low, tail,
):
    count, width = x.shape
    hidden, ff = keep.shape[1], w_up.shape[1]
    rows = carried.shape[0]
    group_len = count // rows
    parts = SUB // rows
    seq_start = lax.axis_index("seq") * group_len
    mask = opened(first_len, seq_start, (SUB, hidden))
    for r in range(rows):
        s = carried[r : r + 1, :]
        before_out[r * parts : r * parts + 1, :] = s
        for h in range(1, parts):
            at = slice(r * parts + h - 1, r * parts + h)
            s = subs[at, :] + subk[at, :] * s
            before_out[r * parts + h : r * parts + h + 1, :] = s
    before_out[...] = before_out[...] * mask

    def step(i, state):
        at = pl.ds(pl.multiple_of(i * SUB, SUB), SUB)
        state = keep[at, :] * state + drive[at, :]
        state_out[at, :] = state
        return state

    lax.fori_loop(0, count // SUB, step, before_out[...], unroll=8)
    low_out[...] = state_out[...].astype(BF16)
    middle = x[...].astype(F32) + dot(low_out[...], w_out[...])
    middle_out[...] = middle
    second_low[...] = (middle * rms(middle) * gain_two[...]).astype(BF16)
    block = 256

    def part(b, carry):
        cols = pl.ds(pl.multiple_of(b * block, block), block)
        pre = dot(second_low[...], w_up[:, cols])
        back = dot_rt(up[...], w_down[cols, :])
        scaled = pre * 0.7071067811865476
        phi = 0.5 + 0.5 * lax.erf(scaled)
        active = (pre * phi).astype(BF16)
        slope = phi + pre * (0.3989422804014327 * jnp.exp(-scaled * scaled))
        up_low = (slope * back).astype(BF16)
        grad_down[cols, :] = dot_lt(active, up[...])
        grad_up[:, cols] = dot_lt(second_low[...], up_low)
        out_part = dot(active, w_down[cols, :])
        grad_part = dot_rt(up_low, w_up[:, cols])

        @pl.when(b == 0)
        def _():
            tail[...] = out_part
            second_grad[...] = grad_part

        @pl.when(b > 0)
        def _():
            tail[...] += out_part
            second_grad[...] += grad_part

        return carry

    lax.fori_loop(0, ff // block, part, 0)
    order = segment_order(count)
    result = (middle_out[...] + tail[...]).astype(BF16)
    output[...] = dot_lt(order, result).astype(BF16).reshape(output.shape)


def middle_kernel(
    middle_ref, second_grad, up, gain_two, state_low, w_out, keep, subk,
    grad_middle_out, grad_gain_two, grad_out, grad_state, subb, totals,
):
    count, width = middle_ref.shape
    hidden = keep.shape[1]
    rows = totals.shape[0]
    middle = middle_ref[...]
    scale = rms(middle)
    unit = middle * scale
    grad = second_grad[...]
    grad_gain_two[...] = jnp.sum(grad * unit, axis=0, keepdims=True)
    grad = grad * gain_two[...]
    grad_middle = up[...].astype(F32) + scale * (grad - unit * jnp.mean(grad * unit, axis=-1, keepdims=True))
    grad_middle_out[...] = grad_middle
    middle_low = grad_middle.astype(BF16)
    grad_state[...] = dot_rt(middle_low, w_out[...])
    grad_out[...] = dot_lt(state_low[...], middle_low)
    steps = count // SUB

    def step(i, passed):
        at = pl.ds(pl.multiple_of((steps - 1 - i) * SUB, SUB), SUB)
        return keep[at, :] * (grad_state[at, :] + passed)

    subb[...] = lax.fori_loop(0, steps, step, jnp.zeros((SUB, hidden), F32), unroll=8)
    parts = SUB // rows
    for r in range(rows):
        end = r * parts + parts - 1
        b = subb[end : end + 1, :]
        for h in range(parts - 2, -1, -1):
            at = slice(r * parts + h, r * parts + h + 1)
            b = subb[at, :] + subk[at, :] * b
        totals[r : r + 1, :] = b


def first_kernel(
    first_len, returned, subk, subb, keep, grad_state, state, before, cand, gate, passing, conv_low,
    x_ref, rim, gain_one, conv_weight, w_z, w_h, grad_middle, grad_gain_two,
    grad_z, grad_h, small, grad_tokens, sent, tail_normed, tail_middle,
    incoming, gate_low, cand_low, ext, spread, grad_ext, bias_sum,
):
    count, width = x_ref.shape
    hidden = keep.shape[1]
    rows, lag = rim.shape[0], rim.shape[1]
    parts = SUB // rows
    steps = count // SUB
    seq_start = lax.axis_index("seq") * (count // rows)
    for r in range(rows):
        b = returned[r : r + 1, :]
        incoming[r * parts + parts - 1 : (r + 1) * parts, :] = b
        for h in range(parts - 2, -1, -1):
            at = slice(r * parts + h + 1, r * parts + h + 2)
            b = subb[at, :] + subk[at, :] * b
            incoming[r * parts + h : r * parts + h + 1, :] = b
    def one(step_at, passed, bias):
        at = pl.ds(pl.multiple_of(step_at * SUB, SUB), SUB)
        prior = pl.ds(pl.multiple_of(jnp.maximum(step_at - 1, 0) * SUB, SUB), SUB)
        adjoint = grad_state[at, :] + passed
        earlier = jnp.where(step_at > 0, state[prior, :], before[...])
        grad_g = adjoint * (cand[at, :] - earlier) * gate[at, :]
        return keep[at, :] * adjoint, bias + grad_g, grad_g, adjoint * passing[at, :]

    def two(i, carry):
        pair = steps // 2 - 1 - i
        passed, bias, late_g, late_c = one(2 * pair + 1, *carry)
        passed, bias, early_g, early_c = one(2 * pair, passed, bias)
        at = pl.ds(pl.multiple_of(pair * 2 * SUB, 2 * SUB), 2 * SUB)
        gate_low[at, :] = jnp.concatenate([early_g, late_g], axis=0).astype(BF16)
        cand_low[at, :] = jnp.concatenate([early_c, late_c], axis=0).astype(BF16)
        return passed, bias

    _, bias = lax.fori_loop(
        0, steps // 2, two, (incoming[...], jnp.zeros((SUB, hidden), F32)), unroll=2
    )
    bias_sum[...] = jnp.sum(bias, axis=0, keepdims=True)
    grad_z[...] = dot_lt(conv_low[...], gate_low[...])
    grad_h[...] = dot_lt(conv_low[...], cand_low[...])
    grad_mixed = dot_rt(gate_low[...], w_z[...]) + dot_rt(cand_low[...], w_h[...])

    x = x_ref[...].astype(F32)
    scale = rms(x)
    unit = x * scale
    gain = gain_one[...]
    ext[lag * SUB :, :] = unit * gain
    rim_x = rim_tiles(rim, spread)
    rim_unit = [v * rms(v) for v in rim_x]
    fill_extended(ext, rim, first_len, seq_start, [v * gain for v in rim_unit])
    small[0:1, :] = jnp.zeros((1, width), F32)
    for j in range(lag + 1):
        begin = (lag - j) * SUB
        small[1 + j : 2 + j, :] = jnp.sum(grad_mixed * ext[begin : begin + count, :], axis=0, keepdims=True)
    for j in range(hidden // width):
        at = 2 + lag + j
        small[at : at + 1, :] = bias_sum[:, j * width : (j + 1) * width]
    last = 2 + lag + hidden // width
    small[last : last + 1, :] = grad_gain_two[...]
    grad_ext[...] = jnp.zeros_like(grad_ext)
    for j in range(lag + 1):
        begin = (lag - j) * SUB
        grad_ext[begin : begin + count, :] += conv_weight[j : j + 1, :] * grad_mixed
    mask = opened(first_len, seq_start, (SUB, width))
    start = at_row_start((SUB, width), rows)
    end = at_row_end((SUB, width), rows)
    grad_gain = jnp.zeros((SUB, width), F32)
    for k in range(lag):
        head = grad_ext[k * SUB : (k + 1) * SUB, :]
        tail_at = pl.ds(count + k * SUB, SUB)
        near = pltpu.roll(head, SUB - 1, 0)
        grad_ext[tail_at, :] = grad_ext[tail_at, :] + jnp.where(end, 0.0, near)
        to_rim = jnp.where(start, head * mask, 0.0)
        grad_gain = grad_gain + to_rim * rim_unit[k]
        spread[k] = to_rim
        for r in range(rows):
            sent[r, k : k + 1, :] = spread[k, r * parts : r * parts + 1, :]
    grad_normed = grad_ext[lag * SUB :, :]
    small[0:1, :] = jnp.sum(grad_normed * unit, axis=0, keepdims=True) + jnp.sum(
        grad_gain, axis=0, keepdims=True
    )
    for k in range(lag):
        at = count - lag * SUB + k * SUB
        for r in range(rows):
            row = at + r * parts + parts - 1
            to = tail_normed.shape[1] - lag + k
            tail_normed[r, to : to + 1, :] = grad_ext[lag * SUB + row : lag * SUB + row + 1, :]
            tail_middle[r, to : to + 1, :] = grad_middle[row : row + 1, :]
    grad = grad_normed * gain
    grad_x = grad_middle[...] + scale * (grad - unit * jnp.mean(grad * unit, axis=-1, keepdims=True))
    order = segment_order(count)
    grad_tokens[...] = dot_lt(order, grad_x.astype(BF16)).astype(BF16).reshape(grad_tokens.shape)


def tail_kernel(tokens, tail_normed, tail_middle, received, gain_one, _, grad_tokens, spread):
    rows, tile, width = tokens.shape
    lag = received.shape[1]
    for r in range(rows):
        spread[tile - lag :, :] = tail_normed[r, tile - lag :, :] + received[r]
        x = tokens[r].astype(F32)
        scale = rms(x)
        unit = x * scale
        grad = spread[...] * gain_one[...]
        fixed = tail_middle[r] + scale * (grad - unit * jnp.mean(grad * unit, axis=-1, keepdims=True))
        changed = lax.broadcasted_iota(jnp.int32, (tile, width), 0) >= tile - lag
        grad_tokens[r] = jnp.where(changed, fixed, _[r].astype(F32)).astype(BF16)


def shaped(*shapes):
    return tuple(jax.ShapeDtypeStruct(shape, kind) for shape, kind in shapes)


def call(kernel, in_specs, outs, scratch, flops, **more):
    return pl.pallas_call(
        kernel,
        in_specs=in_specs,
        out_specs=(VMEM,) * len(outs),
        out_shape=shaped(*outs),
        scratch_shapes=[pltpu.VMEM(shape, kind) for shape, kind in scratch],
        compiler_params=pltpu.CompilerParams(vmem_limit_bytes=40 << 20),
        cost_estimate=pl.CostEstimate(flops=flops, bytes_accessed=1 << 20, transcendentals=0),
        **more,
    )


def swapped(array, axis, bit):
    return lax.ppermute(array, axis, [(i, i ^ bit) for i in range(lax.axis_size(axis))])


def bits_of(axis):
    bit, result = 1, []
    while bit < lax.axis_size(axis):
        result.append(bit)
        bit *= 2
    return result


def upper(axis, bit):
    return (lax.axis_index(axis) // bit) % 2 == 1


def carry_forward(totals):
    keep, state = totals[0], totals[1]
    before_k, before_s = jnp.ones_like(keep), jnp.zeros_like(state)
    levels = []
    for bit in bits_of("seq"):
        other = swapped(jnp.stack([keep, state]), "seq", bit)
        other_k, other_s = other[0], other[1]
        late = upper("seq", bit)
        levels.append((keep, other_k))
        before_s = jnp.where(late, before_s + before_k * other_s, before_s)
        before_k = jnp.where(late, before_k * other_k, before_k)
        state = jnp.where(late, state + keep * other_s, other_s + other_k * state)
        keep = keep * other_k
    return before_s, levels


def carry_backward(passed, levels):
    after_b, after_k = jnp.zeros_like(passed), jnp.ones_like(passed)
    for bit, (keep, other_k) in zip(bits_of("seq"), levels):
        other_b = swapped(passed, "seq", bit)
        late = upper("seq", bit)
        after_b = jnp.where(late, after_b, after_b + after_k * other_b)
        after_k = jnp.where(late, after_k, after_k * other_k)
        passed = jnp.where(late, other_b + other_k * passed, passed + keep * other_b)
    return after_b


def per_device(
    tokens, first_len, gain_one, conv_weight, w_z, bias_z, w_h, w_out, gain_two, w_up, w_down, cotangent
):
    rows, group_len, width = tokens.shape
    hidden, ff = w_z.shape[1], w_up.shape[1]
    lag = conv_weight.shape[0] - 1
    count = rows * group_len
    devices = lax.axis_size("seq")
    gain_one, gain_two, bias_z = gain_one[None], gain_two[None], bias_z[None]
    rim = lax.ppermute(
        tokens[:, group_len - lag :].astype(F32), "seq", [(i, i + 1) for i in range(devices - 1)]
    )
    th, tw = (count, hidden), (count, width)
    x, up, conv_low, keep, drive, cand, gate, passing, subk, subs, totals = call(
        gates_kernel,
        [SMEM] + [VMEM] * 8,
        [(tw, BF16), (tw, BF16), (tw, BF16)] + [(th, F32)] * 5
        + [((SUB, hidden), F32)] * 2 + [((2, rows, hidden), F32)],
        [((count + lag * SUB, width), F32), ((lag, SUB, width), F32), ((8, 128), F32)],
        4 * count * width * hidden,
    )(first_len, tokens, cotangent, rim, gain_one, conv_weight, w_z, bias_z, w_h)
    carried, levels = carry_forward(totals)
    state, before, state_low, middle, output, second_grad, grad_up, grad_down = call(
        mlp_kernel,
        [SMEM] + [VMEM] * 11,
        [(th, F32), ((SUB, hidden), F32), (th, BF16), (tw, F32), (tokens.shape, BF16), (tw, F32),
         ((width, ff), F32), ((ff, width), F32)],
        [(tw, BF16), (tw, F32)],
        12 * count * width * ff,
    )(first_len, carried, subk, subs, keep, drive, x, up, w_out, gain_two, w_up, w_down)
    grad_middle, grad_gain_two, grad_out, grad_state, subb, passed = call(
        middle_kernel,
        [VMEM] * 8,
        [(tw, F32), ((1, width), F32), ((hidden, width), F32), (th, F32), ((SUB, hidden), F32),
         ((rows, hidden), F32)],
        [],
        4 * count * width * hidden,
    )(middle, second_grad, up, gain_two, state_low, w_out, keep, subk)
    returned = carry_backward(passed, levels)
    tile = 16
    grad_z, grad_h, small, grad_tokens, sent, tail_normed, tail_middle = call(
        first_kernel,
        [SMEM] + [VMEM] * 19,
        [((width, hidden), F32)] * 2 + [((SUB, width), F32), (tokens.shape, BF16),
         ((rows, lag, width), F32)] + [((rows, tile, width), F32)] * 2,
        [((SUB, hidden), F32), (th, BF16), (th, BF16), ((count + lag * SUB, width), F32),
         ((lag, SUB, width), F32), ((count + lag * SUB, width), F32), ((1, hidden), F32)],
        8 * count * width * hidden,
    )(first_len, returned, subk, subb, keep, grad_state, state, before, cand, gate, passing, conv_low,
      x, rim, gain_one, conv_weight, w_z, w_h, grad_middle, grad_gain_two)
    received = lax.ppermute(sent, "seq", [(i + 1, i) for i in range(devices - 1)])
    at_tail = pl.BlockSpec((rows, tile, width), lambda i: (0, group_len // tile - 1, 0))
    whole = lambda *shape: pl.BlockSpec(shape, lambda i: (0,) * len(shape))
    grad_tokens = pl.pallas_call(
        tail_kernel,
        grid=(1,),
        in_specs=[at_tail, whole(rows, tile, width), whole(rows, tile, width), whole(rows, lag, width),
                  whole(1, width), at_tail],
        out_specs=at_tail,
        out_shape=jax.ShapeDtypeStruct(tokens.shape, BF16),
        scratch_shapes=[pltpu.VMEM((tile, width), F32)],
        input_output_aliases={5: 0},
    )(tokens, tail_normed, tail_middle, received, gain_one, grad_tokens)
    axes = ("row", "seq")
    grad_down, grad_up, grad_out, grad_z, grad_h, small = lax.psum(
        (grad_down, grad_up, grad_out, grad_z, grad_h, small), axes
    )
    bias_at = 2 + lag
    gain_at = bias_at + hidden // width
    return (
        output,
        grad_tokens,
        small[0],
        small[1:bias_at],
        grad_z,
        small[bias_at:gain_at].reshape(hidden),
        grad_h,
        grad_out,
        small[gain_at],
        grad_up,
        grad_down,
    )


def solution(mesh):
    block, copied = P("row", "seq", None), P()
    return jax.shard_map(
        per_device,
        mesh=mesh,
        in_specs=(block, P("row")) + (copied,) * 9 + (block,),
        out_specs=(block, block) + (copied,) * 9,
        check_vma=False,
    )
```

profile of v0, /device:TPU:0, one launch (start us, length us, event | category | flops | bytes accessed | tf_op | source)
XLA Modules:
  0.0 380.8 jit_solution(15369508994119536303)
XLA Ops:
  8.0 4.8 %collective-permute-start = (f32[4,3,512]{2,1,0:T(4,128)S(1)}, f32[4,3,512]{2,1,0:T(4,128)S(1)}, u32[]{:S(2)}, u32[]{:S(2)}) collective-permute-start(f32[4,3,512]{2,1,0:T(4,128)S(1)} %slice_convert_fusion), channel_id=1, source_target_pairs={{0,1},{1,2},{2,3},{3,4},{4,5},{5,6},{6,7},{8,9},{9,10},{10,11},{11... | collective-permute-start | bytes 73736 | tf_op jit(solution)/shard_map/ppermute | solution.py:425
  12.8 1.6 collective-permute-done.rim
  14.4 1.2 copy-done.7
  15.6 1.2 copy-done.9
  16.9 1.0 copy-done.11
  19.9 1.0 copy-done.30
  21.7 5.3 %shard_map.203 = (bf16[512,512]{1,0:T(8,128)(2,1)S(1)}, bf16[512,512]{1,0:T(8,128)(2,1)S(1)}, bf16[512,512]{1,0:T(8,128)(2,1)S(1)}, f32[512,1024]{1,0:T(8,128)S(...) custom-call(s32[4]{0:T(128)S(1)} %copy-done.27, ...), custom_call_target="tpu_custom_call" | custom-call | flops 1073741824 | bytes 1048576 | tf_op jit(solution)/shard_map/pallas_call | solution.py:429
  26.9 1.3 copy-done
  28.3 1.3 copy-done.1
  29.6 0.8 copy-done.12
  30.4 0.8 copy-done.15
  31.2 0.8 copy-done.17
  32.0 1.3 copy-done.32
  33.3 2.3 collective-permute-start.1
  35.6 1.9 collective-permute-done.1
  37.5 3.1 collective-permute-start.2
  40.6 1.9 collective-permute-done.2
  42.5 3.1 collective-permute-start.3
  45.6 1.9 collective-permute-done.3
  47.6 1.0 copy-done.13
  48.6 1.0 copy-done.18
  49.6 1.6 copy-done.29
  51.2 1.6 copy-done.33
  52.8 17.8 %shard_map.204 = (f32[512,1024]{1,0:T(8,128)S(1)}, f32[8,1024]{1,0:T(8,128)S(1)}, bf16[512,1024]{1,0:T(8,128)(2,1)S(1)}, f32[512,512]{1,0:T(8,128)S(1)}, bf16[4,...) custom-call(s32[4]{0:T(128)S(1)} %copy-done.27, ...), custom_call_target="tpu_custom_call" | custom-call | flops 6442450944 | bytes 1048576 | tf_op jit(solution)/shard_map/pallas_call | solution.py:438
  70.6 1.3 copy-done.3
  72.0 1.9 shard_map.205
  73.9 1.3 copy-done.2
  75.2 0.9 collective-permute-start.4
  76.2 2.8 collective-permute-done.4
  79.0 2.0 collective-permute-start.5
  80.9 1.8 collective-permute-done.5
  82.8 3.0 collective-permute-start.6
  85.8 1.7 collective-permute-done.6
  87.6 9.0 %shard_map.206 = (f32[512,1024]{1,0:T(8,128)S(1)}, f32[512,1024]{1,0:T(8,128)S(1)}, f32[8,512]{1,0:T(8,128)S(1)}, bf16[4,128,512]{2,1,0:T(8,128)(2,1)}, f32[4,3,...) custom-call(s32[4]{0:T(128)S(1)} %copy-done.28, f32[4,1024]{1,0:T(4,128)S(1)} %add_select_fusion.returned, ...), custom_call_target="tpu_custom_call" | custom-call | flops 2147483648 | bytes 1048576 | tf_op jit(solution)/shard_map/pallas_call | solution.py:456
  96.7 1.3 copy-done.4
  98.0 1.3 copy-done.5
  100.6 1.3 collective-permute-start.7
  101.9 43.8 %psum.42 = f32[8,512]{1,0:T(8,128)S(1)} all-reduce(f32[8,512]{1,0:T(8,128)S(1)} %get-tuple-element.69), channel_id=1, replica_groups=mesh['row'=4,'seq'=8] {'row','seq'}, use_global_device_ids=true, to_apply=%region_0.1 | all-reduce | flops 4096 | bytes 32768 | tf_op jit(solution)/shard_map/psum | solution.py:480
  148.1 1.9 shard_map.207
  150.0 209.6 %all-reduce.3.cloned.1.call-done = (f32[512,1024]{1,0:T(8,128)}, f32[512,1024]{1,0:T(8,128)}, f32[1024,512]{1,0:T(8,128)}, f32[512,2048]{1,0:T(8,128)}, f32[2048,512]{1,0:T(8,128)}) async-done(((f32[512,1024]{1,0:T(8,128)}, f32[512,1024]{1,0:T(8,128)}, f32[1024,512]{1,0:T(8,128)}, f32[512,2048]{1,0:T(8,128)}, f32[2048,512]{1,0:T(8,128)}), (f32[512,1024]{1,0:T(8,128)}, f32[512,1024]{1,0:T(8,128)}, ...) | async-done | bytes 14680080 | tf_op jit(solution)/shard_map/psum | solution.py:480
  359.6 3.3 copy.31
  362.9 1.3 copy.32
  364.3 1.0 copy-done.36
  365.3 1.3 copy.33
  366.6 1.6 copy-done.35
  368.2 2.1 copy.34
  370.4 1.6 copy-done.34
  371.9 2.0 copy.35
  (73 shorter events, 7.4 us)
Async XLA Ops:
  7.2 352.4 %all-reduce.3.cloned.1.call-start = ((), (), s32[]{:S(2)}) async-start(), calls=%async_computation | async-start | bytes 29360128 | tf_op jit(solution)/shard_map/psum | solution.py:480
  8.0 6.4 %collective-permute-start = (f32[4,3,512]{2,1,0:T(4,128)S(1)}, f32[4,3,512]{2,1,0:T(4,128)S(1)}, u32[]{:S(2)}, u32[]{:S(2)}) collective-permute-start(f32[4,3,512]{2,1,0:T(4,128)S(1)} %slice_convert_fusion), channel_id=1, source_target_pairs={{0,1},{1,2},{2,3},{3,4},{4,5},{5,6},{6,7},{8,9},{9,10},{10,11},{11... | collective-permute-start | bytes 73736 | tf_op jit(solution)/shard_map/ppermute | solution.py:425
  14.4 1.2 copy-start.7
  15.6 1.2 copy-start.9
  16.9 1.0 copy-start.11
  17.9 0.7 copy-start.22
  18.6 0.7 copy-start.24
  19.3 0.7 copy-start.27
  19.9 1.0 copy-start.30
  21.0 0.7 copy-start.31
  21.7 25.9 %copy-start.6 = (bf16[1024,512]{1,0:T(8,128)(2,1)S(1)}, bf16[1024,512]{1,0:T(8,128)(2,1)}, u32[]{:S(2)}) copy-start(bf16[1024,512]{1,0:T(8,128)(2,1)} %w_out.3) | copy-start | bytes 3145732
  21.7 25.9 %copy-start.26 = (f32[512]{0:T(512)S(1)}, f32[512]{0:T(512)}, u32[]{:S(2)}) copy-start(f32[512]{0:T(512)} %param.20) | copy-start | bytes 6148
  26.9 1.3 copy-start
  28.3 1.3 copy-start.1
  29.6 0.8 copy-start.12
  30.4 0.8 copy-start.15
  31.2 0.8 copy-start.17
  32.0 1.3 copy-start.32
  33.3 4.2 %collective-permute-start.1 = (f32[2,4,1024]{2,1,0:T(4,128)S(1)}, f32[2,4,1024]{2,1,0:T(4,128)S(1)}, u32[]{:S(2)}, u32[]{:S(2)}) collective-permute-start(f32[2,4,1024]{2,1,0:T(4,128)S(1)} %get-tuple-element.43), channel_id=1, source_target_pairs={{0,1},{1,0},{2,3},{3,2},{4,5},{5,4},{6,7},{7,6},{8,9},{9,8},{10,11... | collective-permute-start | bytes 98312 | tf_op jit(solution)/shard_map/ppermute | solution.py:374
  37.5 5.0 %collective-permute-start.2 = (f32[2,4,1024]{2,1,0:T(4,128)S(1)}, f32[2,4,1024]{2,1,0:T(4,128)S(1)}, u32[]{:S(2)}, u32[]{:S(2)}) collective-permute-start(f32[2,4,1024]{2,1,0:T(4,128)S(1)} %pad_maximum_fusion), channel_id=1, source_target_pairs={{0,2},{1,3},{2,0},{3,1},{4,6},{5,7},{6,4},{7,5},{8,10},{9,11},{10,... | collective-permute-start | bytes 98312 | tf_op jit(solution)/shard_map/ppermute | solution.py:374
  42.5 5.0 %collective-permute-start.3 = (f32[2,4,1024]{2,1,0:T(4,128)S(1)}, f32[2,4,1024]{2,1,0:T(4,128)S(1)}, u32[]{:S(2)}, u32[]{:S(2)}) collective-permute-start(f32[2,4,1024]{2,1,0:T(4,128)S(1)} %pad_maximum_fusion.1), channel_id=1, source_target_pairs={{0,4},{1,5},{2,6},{3,7},{4,0},{5,1},{6,2},{7,3},{8,12},{9,13},{10,... | collective-permute-start | bytes 98312 | tf_op jit(solution)/shard_map/ppermute | solution.py:374
  47.6 1.0 copy-start.13
  48.6 1.0 copy-start.18
  49.6 1.6 copy-start.29
  51.2 1.6 copy-start.33
  52.8 19.1 %copy-start.19 = (bf16[512,512]{1,0:T(8,128)(2,1)S(1)}, bf16[512,512]{1,0:T(8,128)(2,1)}, u32[]{:S(2)}) copy-start(bf16[512,512]{1,0:T(8,128)(2,1)} %copy-done.17) | copy-start | bytes 1572868
  70.6 1.3 copy-start.3
  72.0 15.6 %copy-start.8 = (bf16[512,1024]{1,0:T(8,128)(2,1)S(1)}, bf16[512,1024]{1,0:T(8,128)(2,1)}, u32[]{:S(2)}) copy-start(bf16[512,1024]{1,0:T(8,128)(2,1)} %w_z.3) | copy-start | bytes 3145732
  72.0 15.6 %copy-start.10 = (bf16[512,1024]{1,0:T(8,128)(2,1)S(1)}, bf16[512,1024]{1,0:T(8,128)(2,1)}, u32[]{:S(2)}) copy-start(bf16[512,1024]{1,0:T(8,128)(2,1)} %w_h.3) | copy-start | bytes 3145732
  72.0 15.6 %copy-start.14 = (bf16[512,512]{1,0:T(8,128)(2,1)S(1)}, bf16[512,512]{1,0:T(8,128)(2,1)}, u32[]{:S(2)}) copy-start(bf16[512,512]{1,0:T(8,128)(2,1)} %copy-done.12) | copy-start | bytes 1572868
  72.0 15.6 %copy-start.16 = (bf16[512,512]{1,0:T(8,128)(2,1)S(1)}, bf16[512,512]{1,0:T(8,128)(2,1)}, u32[]{:S(2)}) copy-start(bf16[512,512]{1,0:T(8,128)(2,1)} %copy-done.15) | copy-start | bytes 1572868
  72.0 15.6 %copy-start.23 = (f32[4,512]{1,0:T(4,128)S(1)}, f32[4,512]{1,0:T(4,128)}, u32[]{:S(2)}) copy-start(f32[4,512]{1,0:T(4,128)} %conv_weight.3) | copy-start | bytes 24580
  72.0 15.6 %copy-start.25 = (f32[512]{0:T(512)S(1)}, f32[512]{0:T(512)}, u32[]{:S(2)}) copy-start(f32[512]{0:T(512)} %param.14) | copy-start | bytes 6148
  72.0 15.6 %copy-start.28 = (s32[4]{0:T(128)S(1)}, s32[4]{0:T(128)}, u32[]{:S(2)}) copy-start(s32[4]{0:T(128)} %first_len.5) | copy-start | bytes 52
  73.9 1.3 copy-start.2
  75.2 3.7 collective-permute-start.4
  79.0 3.8 collective-permute-start.5
  82.8 4.7 %collective-permute-start.6 = (f32[4,1024]{1,0:T(4,128)S(1)}, f32[4,1024]{1,0:T(4,128)S(1)}, u32[]{:S(2)}, u32[]{:S(2)}) collective-permute-start(f32[4,1024]{1,0:T(4,128)S(1)} %fusion.6), channel_id=1, source_target_pairs={{0,4},{1,5},{2,6},{3,7},{4,0},{5,1},{6,2},{7,3},{8,12},{9,13},{10,... | collective-permute-start | bytes 49160 | tf_op jit(solution)/shard_map/ppermute | solution.py:374
  96.7 1.3 copy-start.4
  98.0 1.3 copy-start.5
  99.3 0.7 copy-start.20
  100.0 0.7 copy-start.21
  100.6 46.9 %collective-permute-start.7 = (f32[4,3,512]{2,1,0:T(4,128)S(1)}, f32[4,3,512]{2,1,0:T(4,128)S(1)}, u32[]{:S(2)}, u32[]{:S(2)}) collective-permute-start(f32[4,3,512]{2,1,0:T(4,128)S(1)} %get-tuple-element.67), channel_id=1, source_target_pairs={{1,0},{2,1},{3,2},{4,3},{5,4},{6,5},{7,6},{9,8},{10,9},{11,10},{12... | collective-permute-start | bytes 73736 | tf_op jit(solution)/shard_map/ppermute | solution.py:466
  147.5 0.6 copy-start.38
  359.6 3.3 copy-start.37
  362.9 2.3 copy-start.36
  365.3 2.9 copy-start.35
  368.2 3.7 copy-start.34
Sparse Core Ops, SparseCore 0:
  100.8 258.8 all-reduce.2
where the time goes:
time: 382 us; the launch traced here: 381 us
  waiting for transfers between devices  223 us (58%)
  blocking collectives  43.8 us (11%)
  local copies, waits for them, and re-layouts  42.2 us (11%)
  Pallas kernels  35.9 us (9%)
  starting transfers between devices  20.6 us (5%)
  between operations  14.3 us (4%)
    psum x1, waiting for transfers between devices, per_device(): lax.psum((grad_down, grad_up, grad_out, grad_z, grad_h, small), axes)  210 us
    psum x1, blocking collectives, per_device(): lax.psum((grad_down, grad_up, grad_out, grad_z, grad_h, small), axes)  43.8 us
    unnamed x85, local copies, waits for them, and re-layouts  41 us
    pallas_call x1, Pallas kernels, per_device(): call(mlp_kernel, [SMEM] + [VMEM] * 11, [(th, F32), ((SUB, hidden), F32),...  17.8 us
    ppermute x6, starting transfers between devices, swapped(): lax.ppermute(array, axis, [(i, i ^ bit) for i in range(lax.axis_size(axis...  14.4 us
    ppermute x6, waiting for transfers between devices, swapped(): lax.ppermute(array, axis, [(i, i ^ bit) for i in range(lax.axis_size(axis...  12 us
    pallas_call x1, Pallas kernels, per_device(): call(first_kernel, [SMEM] + [VMEM] * 19, [((width, hidden), F32)] * 2 + [...  9.05 us
  transfers between devices with their start and end apart: 9, of which 8 were waited for; matrix products, arithmetic and copies ran while one was open for 0% of the time, Pallas kernels for 0%

commit v1 on v0

--- a/solution.py
+++ b/solution.py
@@ -11,6 +11,8 @@
 EPS = 1e-06
 VMEM = pl.BlockSpec(memory_space=pltpu.VMEM)
 SMEM = pl.BlockSpec(memory_space=pltpu.SMEM)
+KINDS = "TSST"
+EARLY = (0, 1, 0, 1)
 SUB = 8
 
 
@@ -142,17 +144,32 @@
         totals[1, r : r + 1, :] = s
 
 
+def by_core(first, mine, other, at, for_even, for_odd):
+    @pl.when(first)
+    def _():
+        mine[at, :] = for_even
+        other[at, :] = for_odd
+
+    @pl.when(jnp.logical_not(first))
+    def _():
+        mine[at, :] = for_odd
+        other[at, :] = for_even
+
+
 def mlp_kernel(
     first_len, carried, subk, subs, keep, drive, x, up, w_out, gain_two, w_up, w_down,
-    state_out, before_out, low_out, middle_out, output, second_grad, grad_up, grad_down,
-    second_low, tail,
+    state_out, before_out, output, mine_a, other_a, mine_b, other_b,
+    grad_middle_out, grad_gain_two, grad_state, subb, totals,
+    low, second_low, tail, second_grad, middle_ref,
 ):
     count, width = x.shape
     hidden, ff = keep.shape[1], w_up.shape[1]
     rows = carried.shape[0]
     group_len = count // rows
     parts = SUB // rows
+    steps = count // SUB
     seq_start = lax.axis_index("seq") * group_len
+    even = lax.axis_index("row") % 2 == 0
     mask = opened(first_len, seq_start, (SUB, hidden))
     for r in range(rows):
         s = carried[r : r + 1, :]
@@ -169,52 +186,37 @@
         state_out[at, :] = state
         return state
 
-    lax.fori_loop(0, count // SUB, step, before_out[...], unroll=8)
-    low_out[...] = state_out[...].astype(BF16)
-    middle = x[...].astype(F32) + dot(low_out[...], w_out[...])
-    middle_out[...] = middle
+    lax.fori_loop(0, steps, step, before_out[...], unroll=8)
+    low[...] = state_out[...].astype(BF16)
+    middle = x[...].astype(F32) + dot(low[...], w_out[...])
+    middle_ref[...] = middle
     second_low[...] = (middle * rms(middle) * gain_two[...]).astype(BF16)
-    block = 256
-
-    def part(b, carry):
-        cols = pl.ds(pl.multiple_of(b * block, block), block)
-        pre = dot(second_low[...], w_up[:, cols])
-        back = dot_rt(up[...], w_down[cols, :])
-        scaled = pre * 0.7071067811865476
-        phi = 0.5 + 0.5 * lax.erf(scaled)
-        active = (pre * phi).astype(BF16)
-        slope = phi + pre * (0.3989422804014327 * jnp.exp(-scaled * scaled))
-        up_low = (slope * back).astype(BF16)
-        grad_down[cols, :] = dot_lt(active, up[...])
-        grad_up[:, cols] = dot_lt(second_low[...], up_low)
-        out_part = dot(active, w_down[cols, :])
-        grad_part = dot_rt(up_low, w_up[:, cols])
-
-        @pl.when(b == 0)
-        def _():
-            tail[...] = out_part
-            second_grad[...] = grad_part
-
-        @pl.when(b > 0)
-        def _():
-            tail[...] += out_part
-            second_grad[...] += grad_part
-
-        return carry
-
-    lax.fori_loop(0, ff // block, part, 0)
+    tail[...] = jnp.zeros_like(tail)
+    second_grad[...] = jnp.zeros_like(second_grad)
+    block = width
+    half = ff // block // 2
+    for mine, other, begin in ((mine_a, other_a, 0), (mine_b, other_b, half)):
+
+        def part(b, carry):
+            cols = pl.ds(pl.multiple_of((b + begin) * block, block), block)
+            at = pl.ds(pl.multiple_of(b * block, block), block)
+            pre = dot(second_low[...], w_up[:, cols])
+            back = dot_rt(up[...], w_down[cols, :])
+            scaled = pre * 0.7071067811865476
+            phi = 0.5 + 0.5 * lax.erf(scaled)
+            active = (pre * phi).astype(BF16)
+            slope = phi + pre * (0.3989422804014327 * jnp.exp(-scaled * scaled))
+            up_low = (slope * back).astype(BF16)
+            by_core(even, mine, other, at, dot_lt(active, up[...]), dot_lt(second_low[...], up_low))
+            tail[...] += dot(active, w_down[cols, :])
+            second_grad[...] += dot_rt(up_low, w_up[:, cols])
+            return carry
+
+        lax.fori_loop(0, half, part, 0)
     order = segment_order(count)
-    result = (middle_out[...] + tail[...]).astype(BF16)
+    result = (middle_ref[...] + tail[...]).astype(BF16)
     output[...] = dot_lt(order, result).astype(BF16).reshape(output.shape)
 
-
-def middle_kernel(
-    middle_ref, second_grad, up, gain_two, state_low, w_out, keep, subk,
-    grad_middle_out, grad_gain_two, grad_out, grad_state, subb, totals,
-):
-    count, width = middle_ref.shape
-    hidden = keep.shape[1]
-    rows = totals.shape[0]
     middle = middle_ref[...]
     scale = rms(middle)
     unit = middle * scale
@@ -225,15 +227,17 @@
     grad_middle_out[...] = grad_middle
     middle_low = grad_middle.astype(BF16)
     grad_state[...] = dot_rt(middle_low, w_out[...])
-    grad_out[...] = dot_lt(state_low[...], middle_low)
-    steps = count // SUB
-
-    def step(i, passed):
+    half_h = hidden // 2
+    by_core(
+        even, mine_b, other_b, slice(half * block, half * block + half_h),
+        dot_lt(low[:, :half_h], middle_low), dot_lt(low[:, half_h:], middle_low),
+    )
+
+    def back_step(i, passed):
         at = pl.ds(pl.multiple_of((steps - 1 - i) * SUB, SUB), SUB)
         return keep[at, :] * (grad_state[at, :] + passed)
 
-    subb[...] = lax.fori_loop(0, steps, step, jnp.zeros((SUB, hidden), F32), unroll=8)
-    parts = SUB // rows
+    subb[...] = lax.fori_loop(0, steps, back_step, jnp.zeros((SUB, hidden), F32), unroll=8)
     for r in range(rows):
         end = r * parts + parts - 1
         b = subb[end : end + 1, :]
@@ -245,9 +249,9 @@
 
 def first_kernel(
     first_len, returned, subk, subb, keep, grad_state, state, before, cand, gate, passing, conv_low,
-    x_ref, rim, gain_one, conv_weight, w_z, w_h, grad_middle, grad_gain_two,
-    grad_z, grad_h, small, grad_tokens, sent, tail_normed, tail_middle,
-    incoming, gate_low, cand_low, ext, spread, grad_ext, bias_sum,
+    x_ref, rim, gain_one, conv_weight, w_z, w_h, grad_middle, grad_gain_two, token,
+    mine_a, other_a, mine_b, other_b, grad_tokens, sent, tail_normed, tail_middle,
+    incoming, gate_low, cand_low, ext, spread, grad_ext, bias_sum, small,
 ):
     count, width = x_ref.shape
     hidden = keep.shape[1]
@@ -283,8 +287,14 @@
         0, steps // 2, two, (incoming[...], jnp.zeros((SUB, hidden), F32)), unroll=2
     )
     bias_sum[...] = jnp.sum(bias, axis=0, keepdims=True)
-    grad_z[...] = dot_lt(conv_low[...], gate_low[...])
-    grad_h[...] = dot_lt(conv_low[...], cand_low[...])
+    even = lax.axis_index("row") % 2 == 0
+    half = width // 2
+    for k, (mine, other) in enumerate(((mine_a, other_a), (mine_b, other_b))):
+        cols = slice(k * half, (k + 1) * half)
+        by_core(
+            even, mine.at[:, :hidden], other.at[:, :hidden], slice(0, half),
+            dot_lt(conv_low[:, cols], gate_low[...]), dot_lt(conv_low[:, cols], cand_low[...]),
+        )
     grad_mixed = dot_rt(gate_low[...], w_z[...]) + dot_rt(cand_low[...], w_h[...])
 
     x = x_ref[...].astype(F32)
@@ -326,6 +336,14 @@
     small[0:1, :] = jnp.sum(grad_normed * unit, axis=0, keepdims=True) + jnp.sum(
         grad_gain, axis=0, keepdims=True
     )
+    for mine, keeps in ((mine_b, even), (other_b, jnp.logical_not(even))):
+
+        @pl.when(keeps)
+        def _():
+            mine[:, hidden:] = jnp.zeros((half, 128), F32)
+            for j in range(width // 128):
+                mine[j * SUB : (j + 1) * SUB, hidden:] = small[:, j * 128 : (j + 1) * 128]
+
     for k in range(lag):
         at = count - lag * SUB + k * SUB
         for r in range(rows):
@@ -364,7 +382,7 @@
         out_specs=(VMEM,) * len(outs),
         out_shape=shaped(*outs),
         scratch_shapes=[pltpu.VMEM(shape, kind) for shape, kind in scratch],
-        compiler_params=pltpu.CompilerParams(vmem_limit_bytes=40 << 20),
+        compiler_params=pltpu.CompilerParams(vmem_limit_bytes=20 << 20),
         cost_estimate=pl.CostEstimate(flops=flops, bytes_accessed=1 << 20, transcendentals=0),
         **more,
     )
@@ -411,6 +429,185 @@
         after_k = jnp.where(late, after_k, after_k * other_k)
         passed = jnp.where(late, other_b + other_k * passed, passed + keep * other_b)
     return after_b
+
+
+BOTH = ("row", "seq")
+
+
+def axis_steps(kind):
+    row = [("row", bit) for bit in bits_of("row")[1:]]
+    seq = [("seq", bit) for bit in bits_of("seq")]
+    near, far = seq[:1], seq[1:]
+    even = {"P": near + row + far, "S": near + far + row, "T": far + near + row}[kind]
+    return list(zip(even, row + near + far))
+
+
+def exchanged(array, even, odd):
+    rows, devices = lax.axis_size("row"), lax.axis_size("seq")
+    pairs = []
+    for r in range(rows):
+        for s in range(devices):
+            axis, bit = odd if r & 1 else even
+            to = ((r ^ bit) * devices + s) if axis == "row" else (r * devices + (s ^ bit))
+            pairs.append((r * devices + s, to))
+    return lax.ppermute(array, BOTH, pairs)
+
+
+def place_bit(even, odd):
+    one, two = [lax.axis_index(axis) // bit % 2 for axis, bit in (even, odd)]
+    return jnp.where(lax.axis_index("row") % 2 == 0, one, two).astype(jnp.int32).reshape(1)
+
+
+def by_rows(total, body):
+    chunk = next((c for c in (64, 32, 16, 8) if total % c == 0), total)
+    if chunk == total:
+        body(0, chunk)
+        return
+
+    def turn(i, carry):
+        body(pl.multiple_of(i * chunk, chunk), chunk)
+        return carry
+
+    lax.fori_loop(0, total // chunk, turn, 0)
+
+
+def aligned(at, half):
+    return pl.multiple_of(at, SUB) if half % SUB == 0 else at
+
+
+def split_kernel(_, bit, mine, received, send, keep):
+    half = send.shape[0]
+    if half % SUB:
+        first = mine[:half, :] + received[:half, :]
+        second = mine[half:, :] + received[half:, :]
+        lower = jnp.broadcast_to(bit[0] == 0, first.shape)
+        send[...] = jnp.where(lower, second, first)
+        keep[...] = jnp.where(lower, first, second)
+        return
+
+    def body(i, chunk):
+        to = pl.ds(i, chunk)
+        for out, begin in ((send, (1 - bit[0]) * half), (keep, bit[0] * half)):
+            at = pl.ds(pl.multiple_of(i + begin, SUB), chunk)
+            out[to, :] = mine[at, :] + received[at, :]
+
+    by_rows(half, body)
+
+
+def add_kernel(_, mine, received, out):
+    def body(i, chunk):
+        at = pl.ds(i, chunk)
+        out[at, :] = mine[at, :] + received[at, :]
+
+    by_rows(mine.shape[0], body)
+
+
+def join_kernel(_, bit, mine, received, out):
+    half = mine.shape[0]
+    if half % SUB:
+        lower = jnp.broadcast_to(bit[0] == 0, mine.shape)
+        out[:half, :] = jnp.where(lower, mine[...], received[...])
+        out[half:, :] = jnp.where(lower, received[...], mine[...])
+        return
+
+    def body(i, chunk):
+        at = pl.ds(i, chunk)
+        for source, begin in ((mine, bit[0] * half), (received, (1 - bit[0]) * half)):
+            out[pl.ds(pl.multiple_of(i + begin, SUB), chunk), :] = source[at, :]
+
+    by_rows(half, body)
+
+
+def piece_call(kernel, specs, outs, *operands):
+    return pl.pallas_call(
+        kernel,
+        in_specs=[pl.BlockSpec(memory_space=pl.ANY)] + specs,
+        out_specs=(VMEM,) * len(outs),
+        out_shape=shaped(*[(shape, F32) for shape in outs]),
+        compiler_params=pltpu.CompilerParams(vmem_limit_bytes=16 << 20),
+        cost_estimate=pl.CostEstimate(flops=1, bytes_accessed=1, transcendentals=0),
+    )(*operands)
+
+
+class Summed:
+    def __init__(self, mine, other, kind):
+        self.steps = axis_steps(kind)
+        self.core = (("row", 1),) * 2
+        self.mine, self.other, self.at = mine, other, 0
+        self.width = mine.shape[1]
+
+    def advance(self, token):
+        count, at = len(self.steps), self.at
+        self.at += 1
+        if at == 0:
+            self.received = exchanged(self.other, *self.core)
+            return token
+        rows = self.mine.shape[0]
+        if at <= count:
+            step = self.steps[at - 1]
+            half = (rows // 2, self.width)
+            send, self.mine = piece_call(
+                split_kernel, [SMEM, VMEM, VMEM], [half, half], token, place_bit(*step), self.mine, self.received
+            )
+            self.received = exchanged(send, *step)
+            return self.mine
+        if at == count + 1:
+            (self.mine,) = piece_call(add_kernel, [VMEM] * 2, [self.mine.shape], token, self.mine, self.received)
+        else:
+            step = self.steps[2 * count + 1 - at]
+            (self.mine,) = piece_call(
+                join_kernel, [SMEM, VMEM, VMEM], [(2 * rows, self.width)], token, place_bit(*step), self.mine,
+                self.received,
+            )
+        step = self.steps[2 * count - at] if at <= 2 * count else self.core
+        self.received = exchanged(self.mine, *step)
+        return self.mine
+
+    def turns(self):
+        return 2 * len(self.steps) + 2
+
+
+def finish_kernel(
+    mine_a, got_a, mine_b, got_b, mine_c, got_c, mine_d, got_d,
+    grad_down, grad_up, grad_out, grad_z, grad_h, small, sems,
+):
+    block = mine_a.shape[1]
+    width, hidden = grad_z.shape
+    half = width // 2
+    even = lax.axis_index("row") % 2 == 0
+
+    def run(a_even, a_odd, b_even, b_odd, c_even, c_odd, d_even, d_odd):
+        rows = mine_a.shape[0]
+        copies = [
+            (a_even, grad_down.at[pl.ds(0, rows), :]),
+            (b_even.at[pl.ds(0, rows), :], grad_down.at[pl.ds(rows, rows), :]),
+            (b_even.at[pl.ds(rows, hidden // 2), :], grad_out.at[pl.ds(0, hidden // 2), :]),
+            (b_odd.at[pl.ds(rows, hidden // 2), :], grad_out.at[pl.ds(hidden // 2, hidden // 2), :]),
+        ]
+        for k in range(rows // block):
+            at = pl.ds(k * block, block)
+            copies.append((a_odd.at[at, :], grad_up.at[:, at]))
+            copies.append((b_odd.at[at, :], grad_up.at[:, pl.ds(rows + k * block, block)]))
+        for k, (one, two) in enumerate(((c_even, c_odd), (d_even, d_odd))):
+            to = pl.ds(k * half, half)
+            copies.append((one.at[:, pl.ds(0, hidden)], grad_z.at[to, :]))
+            copies.append((two.at[:, pl.ds(0, hidden)], grad_h.at[to, :]))
+        copies.append((d_even.at[pl.ds(0, small.shape[0]), pl.ds(hidden, 128)], small))
+        started = [pltpu.make_async_copy(*pair, sems.at[i]) for i, pair in enumerate(copies)]
+        for copy in started:
+            copy.start()
+        for copy in started:
+            copy.wait()
+
+    pairs = ((mine_a, got_a), (mine_b, got_b), (mine_c, got_c), (mine_d, got_d))
+
+    @pl.when(even)
+    def _():
+        run(*[ref for pair in pairs for ref in pair])
+
+    @pl.when(jnp.logical_not(even))
+    def _():
+        run(*[ref for pair in pairs for ref in pair[::-1]])
 
 
 def per_device(
@@ -435,34 +632,34 @@
         4 * count * width * hidden,
     )(first_len, tokens, cotangent, rim, gain_one, conv_weight, w_z, bias_z, w_h)
     carried, levels = carry_forward(totals)
-    state, before, state_low, middle, output, second_grad, grad_up, grad_down = call(
+    pairs_a = ((ff // 2, width), F32)
+    pairs_b = ((ff // 2 + hidden // 2, width), F32)
+    state, before, output, mine_a, other_a, mine_b, other_b, grad_middle, grad_gain_two, grad_state, subb, passed = call(
         mlp_kernel,
         [SMEM] + [VMEM] * 11,
-        [(th, F32), ((SUB, hidden), F32), (th, BF16), (tw, F32), (tokens.shape, BF16), (tw, F32),
-         ((width, ff), F32), ((ff, width), F32)],
-        [(tw, BF16), (tw, F32)],
+        [(th, F32), ((SUB, hidden), F32), (tokens.shape, BF16), pairs_a, pairs_a, pairs_b, pairs_b,
+         (tw, F32), ((1, width), F32), (th, F32), ((SUB, hidden), F32), ((rows, hidden), F32)],
+        [(th, BF16), (tw, BF16), (tw, F32), (tw, F32), (tw, F32)],
         12 * count * width * ff,
     )(first_len, carried, subk, subs, keep, drive, x, up, w_out, gain_two, w_up, w_down)
-    grad_middle, grad_gain_two, grad_out, grad_state, subb, passed = call(
-        middle_kernel,
-        [VMEM] * 8,
-        [(tw, F32), ((1, width), F32), ((hidden, width), F32), (th, F32), ((SUB, hidden), F32),
-         ((rows, hidden), F32)],
-        [],
-        4 * count * width * hidden,
-    )(middle, second_grad, up, gain_two, state_low, w_out, keep, subk)
     returned = carry_backward(passed, levels)
+    sums = [Summed(mine_a, other_a, KINDS[0]), Summed(mine_b, other_b, KINDS[1])]
+    token = grad_gain_two
+    for turn in EARLY:
+        token = sums[turn].advance(token)
     tile = 16
-    grad_z, grad_h, small, grad_tokens, sent, tail_normed, tail_middle = call(
+    pair = ((width // 2, hidden), F32)
+    pair_small = ((width // 2, hidden + 128), F32)
+    mine_c, other_c, mine_d, other_d, grad_tokens, sent, tail_normed, tail_middle = call(
         first_kernel,
-        [SMEM] + [VMEM] * 19,
-        [((width, hidden), F32)] * 2 + [((SUB, width), F32), (tokens.shape, BF16),
+        [SMEM] + [VMEM] * 19 + [pl.BlockSpec(memory_space=pl.ANY)],
+        [pair, pair, pair_small, pair_small, (tokens.shape, BF16),
          ((rows, lag, width), F32)] + [((rows, tile, width), F32)] * 2,
         [((SUB, hidden), F32), (th, BF16), (th, BF16), ((count + lag * SUB, width), F32),
-         ((lag, SUB, width), F32), ((count + lag * SUB, width), F32), ((1, hidden), F32)],
+         ((lag, SUB, width), F32), ((count + lag * SUB, width), F32), ((1, hidden), F32), ((SUB, width), F32)],
         8 * count * width * hidden,
     )(first_len, returned, subk, subb, keep, grad_state, state, before, cand, gate, passing, conv_low,
-      x, rim, gain_one, conv_weight, w_z, w_h, grad_middle, grad_gain_two)
+      x, rim, gain_one, conv_weight, w_z, w_h, grad_middle, grad_gain_two, token)
     received = lax.ppermute(sent, "seq", [(i + 1, i) for i in range(devices - 1)])
     at_tail = pl.BlockSpec((rows, tile, width), lambda i: (0, group_len // tile - 1, 0))
     whole = lambda *shape: pl.BlockSpec(shape, lambda i: (0,) * len(shape))
@@ -476,10 +673,24 @@
         scratch_shapes=[pltpu.VMEM((tile, width), F32)],
         input_output_aliases={5: 0},
     )(tokens, tail_normed, tail_middle, received, gain_one, grad_tokens)
-    axes = ("row", "seq")
-    grad_down, grad_up, grad_out, grad_z, grad_h, small = lax.psum(
-        (grad_down, grad_up, grad_out, grad_z, grad_h, small), axes
-    )
+    sums += [Summed(mine_c, other_c, KINDS[2]), Summed(mine_d, other_d, KINDS[3])]
+    token = tail_normed
+    while any(one.at < one.turns() for one in sums):
+        for one in sums:
+            if one.at < one.turns():
+                token = one.advance(token)
+    anywhere = pl.BlockSpec(memory_space=pl.ANY)
+    grad_down, grad_up, grad_out, grad_z, grad_h, small = pl.pallas_call(
+        finish_kernel,
+        in_specs=[anywhere] * 8,
+        out_specs=(anywhere,) * 6,
+        out_shape=shaped(
+            ((ff, width), F32), ((width, ff), F32), ((hidden, width), F32), ((width, hidden), F32),
+            ((width, hidden), F32), ((SUB * width // 128, 128), F32),
+        ),
+        scratch_shapes=[pltpu.SemaphoreType.DMA((24,))],
+    )(*[array for one in sums for array in (one.mine, one.received)])
+    small = small.reshape(width // 128, SUB, 128).swapaxes(0, 1).reshape(SUB, width)
     bias_at = 2 + lag
     gain_at = bias_at + hidden // width
     return (

time: 382 us -> 806 us (2.11)
  Pallas kernels: 35.9 us -> 496 us
  starting transfers between devices: 20.6 us -> 86.8 us
  waiting for transfers between devices: 223 us -> 173 us
  blocking collectives: 43.8 us -> 0 us
  between operations: 14.3 us -> 1.2 us
    pallas_call x2 -> x38, Pallas kernels: 10.9 us -> 474 us  [the longest x1 447 us: per_device(): pl.pallas_call(finish_kernel, in_specs=[anywhere] * 8, out_specs=(anywher...]
    psum x1 -> x0, waiting for transfers between devices: 210 us -> none  [per_device(): lax.psum((grad_down, grad_up, grad_out, grad_z, grad_h, small), axes)]
    ppermute x0 -> x40, waiting for transfers between devices: none -> 133 us  [exchanged(): return lax.ppermute(array, BOTH, pairs)]
    ppermute x0 -> x40, starting transfers between devices: none -> 66.1 us  [exchanged(): return lax.ppermute(array, BOTH, pairs)]
    psum x1 -> x0, blocking collectives: 43.8 us -> none  [per_device(): lax.psum((grad_down, grad_up, grad_out, grad_z, grad_h, small), axes)]
    ppermute x6, waiting for transfers between devices: 12 us -> 34.3 us  [swapped(): lax.ppermute(array, axis, [(i, i ^ bit) for i in range(lax.axis_size(axis...]
    unnamed x85 -> x104, local copies, waits for them, and re-layouts: 41 us -> 45.2 us
  transfers between devices with their start and end apart: 9 -> 48, of which waited for: 8 -> 24; matrix products, arithmetic and copies ran while one was open for 0% -> 0% of each run, Pallas kernels for 0% -> 3%
where the time goes in v1:
time: 806 us; the launch traced here: 805 us
  Pallas kernels  496 us (62%)
  waiting for transfers between devices  173 us (21%)
  starting transfers between devices  86.8 us (11%)
  local copies, waits for them, and re-layouts  47.1 us (6%)
    pallas_call x1, Pallas kernels, per_device(): pl.pallas_call(finish_kernel, in_specs=[anywhere] * 8, out_specs=(anywher...  447 us
    ppermute x40, waiting for transfers between devices, exchanged(): return lax.ppermute(array, BOTH, pairs)  133 us
    ppermute x40, starting transfers between devices, exchanged(): return lax.ppermute(array, BOTH, pairs)  66.1 us
    unnamed x104, local copies, waits for them, and re-layouts  45.2 us
    ppermute x6, waiting for transfers between devices, swapped(): lax.ppermute(array, axis, [(i, i ^ bit) for i in range(lax.axis_size(axis...  34.3 us
    pallas_call x36, Pallas kernels, piece_call(): pl.pallas_call(kernel, in_specs=[pl.BlockSpec(memory_space=pl.ANY)] + spe...  20.5 us
    pallas_call x1, Pallas kernels, per_device(): call(mlp_kernel, [SMEM] + [VMEM] * 11, [(th, F32), ((SUB, hidden), F32),...  16.3 us
  transfers between devices with their start and end apart: 48, of which 24 were waited for; matrix products, arithmetic and copies ran while one was open for 0% of the time, Pallas kernels for 3%

profile of v1, /device:TPU:0, one launch (start us, length us, event | category | flops | bytes accessed | tf_op | source)
XLA Modules:
  0.0 804.9 jit_solution(13217951487391829998)
XLA Ops:
  1.4 4.8 collective-permute-start
  15.1 4.0 shard_map.203
  25.4 2.3 collective-permute-start.1
  27.7 1.9 collective-permute-done.1
  29.6 3.1 collective-permute-start.2
  32.7 1.9 collective-permute-done.2
  34.6 3.1 collective-permute-start.3
  37.7 1.9 collective-permute-done.3
  41.2 1.6 copy-done.41
  44.0 1.6 copy-done.49
  45.6 16.3 %shard_map.204 = (f32[512,1024]{1,0:T(8,128)S(1)}, f32[8,1024]{1,0:T(8,128)S(1)}, bf16[4,128,512]{2,1,0:T(8,128)(2,1)}, f32[1024,512]{1,0:T(8,128)S(1)}, f32[102...) custom-call(s32[4]{0:T(128)S(1)} %copy-done.39, ...), custom_call_target="tpu_custom_call" | custom-call | flops 6442450944 | bytes 1048576 | tf_op jit(solution)/shard_map/pallas_call | solution.py:637
  62.0 1.7 copy-done.1
  69.1 8.0 collective-permute-done.7.received
  83.9 3.6 shard_map.206
  89.5 19.0 %collective-permute-done.4 = f32[4,1024]{1,0:T(4,128)S(1)} collective-permute-done((f32[4,1024]{1,0:T(4,128)S(1)}, f32[4,1024]{1,0:T(4,128)S(1)}, u32[]{:S(2)}, u32[]{:S(2)}) %collective-permute-start.4) | collective-permute-done | bytes 16416 | tf_op jit(solution)/shard_map/ppermute | solution.py:392
  108.5 2.0 collective-permute-start.5
  110.5 1.7 collective-permute-done.5
  112.3 3.0 collective-permute-start.6
  115.3 8.0 collective-permute-done.6
  131.2 6.8 shard_map.207
  141.8 2.2 shard_map.209
  144.0 2.5 shard_map.210
  146.5 5.2 collective-permute-start.13
  151.6 15.9 %collective-permute-done.12.received = f32[256,512]{1,0:T(8,128)S(1)} collective-permute-done((f32[256,512]{1,0:T(8,128)}, f32[256,512]{1,0:T(8,128)S(1)}, u32[]{:S(2)}, u32[]{:S(2)}) %collective-permute-start.12) | collective-permute-done | bytes 524320 | tf_op jit(solution)/shard_map/ppermute | solution.py:453
  170.5 2.1 shard_map.213
  172.6 2.2 shard_map.214
  175.9 2.3 collective-permute-start.17
  179.6 7.6 collective-permute-done.16.received
  187.2 6.7 collective-permute-done.17.received
  196.2 3.3 collective-permute-start.23
  203.3 9.2 %collective-permute-done.22.received = f32[64,1024]{1,0:T(8,128)S(1)} collective-permute-done((f32[64,1024]{1,0:T(8,128)S(1)}, f32[64,1024]{1,0:T(8,128)S(1)}, u32[]{:S(2)}, u32[]{:S(2)}) %collective-permute-start.22) | collective-permute-done | bytes 262176 | tf_op jit(solution)/shard_map/ppermute | solution.py:453
  214.9 2.8 collective-permute-start.26
  217.7 13.8 %collective-permute-done.26.received = f32[32,1024]{1,0:T(8,128)S(1)} collective-permute-done((f32[32,1024]{1,0:T(8,128)S(1)}, f32[32,1024]{1,0:T(8,128)S(1)}, u32[]{:S(2)}, u32[]{:S(2)}) %collective-permute-start.26) | collective-permute-done | bytes 131104 | tf_op jit(solution)/shard_map/ppermute | solution.py:453
  231.8 3.0 collective-permute-start.32
  236.8 3.6 collective-permute-done.30.received
  240.4 13.6 %collective-permute-done.32.received = f32[256,512]{1,0:T(8,128)S(1)} collective-permute-done((f32[256,512]{1,0:T(8,128)S(1)}, f32[256,512]{1,0:T(8,128)S(1)}, u32[]{:S(2)}, u32[]{:S(2)}) %collective-permute-start.32) | collective-permute-done | bytes 524320 | tf_op jit(solution)/shard_map/ppermute | solution.py:453
  254.1 2.1 collective-permute-done.33.received
  259.3 3.6 collective-permute-done.34.received
  263.0 9.7 %collective-permute-done.36.received = f32[512,512]{1,0:T(8,128)S(1)} collective-permute-done((f32[512,512]{1,0:T(8,128)S(1)}, f32[512,512]{1,0:T(8,128)S(1)}, u32[]{:S(2)}, u32[]{:S(2)}) %collective-permute-start.36) | collective-permute-done | bytes 1048608 | tf_op jit(solution)/shard_map/ppermute | solution.py:453
  274.2 14.2 %collective-permute-done.38.received = f32[768,512]{1,0:T(8,128)S(1)} collective-permute-done((f32[768,512]{1,0:T(8,128)S(1)}, f32[768,512]{1,0:T(8,128)S(1)}, u32[]{:S(2)}, u32[]{:S(2)}) %collective-permute-start.38) | collective-permute-done | bytes 1572896 | tf_op jit(solution)/shard_map/ppermute | solution.py:453
  288.7 27.2 %collective-permute-start.39 = (f32[1536,512]{1,0:T(8,128)S(1)}, f32[1536,512]{1,0:T(8,128)}, u32[]{:S(2)}, u32[]{:S(2)}) collective-permute-start(f32[1536,512]{1,0:T(8,128)S(1)} %shard_map.236._.mine_b), channel_id=1, source_target_pairs={{0,8},{1,9},{2,10},{3,11},{4,12},{5,13},{6,14},{7,15},{8,0},{9,1},... | collective-permute-start | bytes 9437192 | tf_op jit(solution)/shard_map/ppermute | solution.py:453
  317.5 5.5 collective-permute-done.40.received
  324.2 9.3 %collective-permute-done.42.received = f32[64,1024]{1,0:T(8,128)S(1)} collective-permute-done((f32[64,1024]{1,0:T(8,128)S(1)}, f32[64,1024]{1,0:T(8,128)S(1)}, u32[]{:S(2)}, u32[]{:S(2)}) %collective-permute-start.42) | collective-permute-done | bytes 262176 | tf_op jit(solution)/shard_map/ppermute | solution.py:453
  334.7 8.2 %collective-permute-done.44.received = f32[128,1024]{1,0:T(8,128)S(1)} collective-permute-done((f32[128,1024]{1,0:T(8,128)S(1)}, f32[128,1024]{1,0:T(8,128)S(1)}, u32[]{:S(2)}, u32[]{:S(2)}) %collective-permute-start.44) | collective-permute-done | bytes 524320 | tf_op jit(solution)/shard_map/ppermute | solution.py:453
  345.2 2.4 collective-permute-start.47
  348.9 4.5 collective-permute-done.9.received
  354.0 1.9 shard_map.208
  355.9 446.5 %shard_map.243 = (f32[2048,512]{1,0:T(8,128)}, f32[512,2048]{1,0:T(8,128)}, f32[1024,512]{1,0:T(8,128)}, f32[512,1024]{1,0:T(8,128)}, f32[512,1024]{1,0:T(8,128)}, /*index=5*/f32[32,128]{1,0:T(8,128)}) custom-call(f32[1024,512]{1,0:T(8,128)} %shard_map.235._.mine_a, f32[1024,512]{1,0:T(8,128)} %collective-permute-done.37.got_a, f32[1536,512]{1,0:T(8,128)} %copy-done, ...), custom_call_target="tpu_custom_call" | custom-call | tf_op jit(solution)/shard_map/pallas_call | solution.py:683
  (205 shorter events, 76.4 us)
Async XLA Ops:
  1.4 6.4 collective-permute-start
  25.4 4.2 collective-permute-start.1
  29.6 5.0 collective-permute-start.2
  34.6 5.0 collective-permute-start.3
  68.6 14.3 %collective-permute-start.8 = (f32[1536,512]{1,0:T(8,128)}, f32[1536,512]{1,0:T(8,128)}, u32[]{:S(2)}, u32[]{:S(2)}) collective-permute-start(f32[1536,512]{1,0:T(8,128)} %get-tuple-element.103), channel_id=1, source_target_pairs={{0,8},{1,9},{2,10},{3,11},{4,12},{5,13},{6,14},{7,15},{8,0},{9,1},... | collective-permute-start | bytes 9437192 | tf_op jit(solution)/shard_map/ppermute | solution.py:453
  68.6 8.5 %collective-permute-start.7 = (f32[1024,512]{1,0:T(8,128)}, f32[1024,512]{1,0:T(8,128)S(1)}, u32[]{:S(2)}, u32[]{:S(2)}) collective-permute-start(f32[1024,512]{1,0:T(8,128)} %get-tuple-element.100), channel_id=1, source_target_pairs={{0,8},{1,9},{2,10},{3,11},{4,12},{5,13},{6,14},{7,15},{8,0},{9,1},... | collective-permute-start | bytes 6291464 | tf_op jit(solution)/shard_map/ppermute | solution.py:453
  87.5 56.5 %collective-permute-start.11 = (f32[768,512]{1,0:T(8,128)}, f32[768,512]{1,0:T(8,128)}, u32[]{:S(2)}, u32[]{:S(2)}) collective-permute-start(f32[768,512]{1,0:T(8,128)} %get-tuple-element.111), channel_id=1, source_target_pairs={{0,1},{1,0},{2,3},{3,2},{4,5},{5,4},{6,7},{7,6},{8,24},{9,25},{10,... | collective-permute-start | bytes 4718600 | tf_op jit(solution)/shard_map/ppermute | solution.py:453
  88.4 20.1 %collective-permute-start.4 = (f32[4,1024]{1,0:T(4,128)S(1)}, f32[4,1024]{1,0:T(4,128)S(1)}, u32[]{:S(2)}, u32[]{:S(2)}) collective-permute-start(f32[4,1024]{1,0:T(4,128)S(1)} %get-tuple-element.88), channel_id=1, source_target_pairs={{0,1},{1,0},{2,3},{3,2},{4,5},{5,4},{6,7},{7,6},{8,9},{9,8},{10,11... | collective-permute-start | bytes 49160 | tf_op jit(solution)/shard_map/ppermute | solution.py:392
  108.5 3.8 collective-permute-start.5
  110.4 31.4 %collective-permute-start.10 = (f32[512,512]{1,0:T(8,128)}, f32[512,512]{1,0:T(8,128)}, u32[]{:S(2)}, u32[]{:S(2)}) collective-permute-start(f32[512,512]{1,0:T(8,128)} %get-tuple-element.109), channel_id=1, source_target_pairs={{0,2},{1,3},{2,0},{3,1},{4,6},{5,7},{6,4},{7,5},{8,24},{9,25},{10,... | collective-permute-start | bytes 3145736 | tf_op jit(solution)/shard_map/ppermute | solution.py:453
  112.3 11.0 %collective-permute-start.6 = (f32[4,1024]{1,0:T(4,128)S(1)}, f32[4,1024]{1,0:T(4,128)S(1)}, u32[]{:S(2)}, u32[]{:S(2)}) collective-permute-start(f32[4,1024]{1,0:T(4,128)S(1)} %fusion.6), channel_id=1, source_target_pairs={{0,4},{1,5},{2,6},{3,7},{4,0},{5,1},{6,2},{7,3},{8,12},{9,13},{10,... | collective-permute-start | bytes 49160 | tf_op jit(solution)/shard_map/ppermute | solution.py:392
  141.3 31.3 %collective-permute-start.15 = (f32[256,1152]{1,0:T(8,128)}, f32[256,1152]{1,0:T(8,128)}, u32[]{:S(2)}, u32[]{:S(2)}) collective-permute-start(f32[256,1152]{1,0:T(8,128)} %get-tuple-element.121), channel_id=1, source_target_pairs={{0,8},{1,9},{2,10},{3,11},{4,12},{5,13},{6,14},{7,15},{8,0},{9,1},... | collective-permute-start | bytes 3538952 | tf_op jit(solution)/shard_map/ppermute | solution.py:453
  141.3 28.0 %collective-permute-start.14 = (f32[256,1024]{1,0:T(8,128)}, f32[256,1024]{1,0:T(8,128)}, u32[]{:S(2)}, u32[]{:S(2)}) collective-permute-start(f32[256,1024]{1,0:T(8,128)} %get-tuple-element.118), channel_id=1, source_target_pairs={{0,8},{1,9},{2,10},{3,11},{4,12},{5,13},{6,14},{7,15},{8,0},{9,1},... | collective-permute-start | bytes 3145736 | tf_op jit(solution)/shard_map/ppermute | solution.py:453
  146.5 21.9 %collective-permute-start.13 = (f32[384,512]{1,0:T(8,128)}, f32[384,512]{1,0:T(8,128)S(1)}, u32[]{:S(2)}, u32[]{:S(2)}) collective-permute-start(f32[384,512]{1,0:T(8,128)} %get-tuple-element.115), channel_id=1, source_target_pairs={{0,2},{1,3},{2,0},{3,1},{4,6},{5,7},{6,4},{7,5},{8,9},{9,8},{10,11... | collective-permute-start | bytes 2359304 | tf_op jit(solution)/shard_map/ppermute | solution.py:453
  151.6 16.0 %collective-permute-start.12 = (f32[256,512]{1,0:T(8,128)}, f32[256,512]{1,0:T(8,128)S(1)}, u32[]{:S(2)}, u32[]{:S(2)}) collective-permute-start(f32[256,512]{1,0:T(8,128)} %get-tuple-element.113), channel_id=1, source_target_pairs={{0,4},{1,5},{2,6},{3,7},{4,0},{5,1},{6,2},{7,3},{8,9},{9,8},{10,11... | collective-permute-start | bytes 1572872 | tf_op jit(solution)/shard_map/ppermute | solution.py:453
  174.8 21.3 %collective-permute-start.19 = (f32[128,1152]{1,0:T(8,128)}, f32[128,1152]{1,0:T(8,128)S(1)}, u32[]{:S(2)}, u32[]{:S(2)}) collective-permute-start(f32[128,1152]{1,0:T(8,128)} %get-tuple-element.129), channel_id=1, source_target_pairs={{0,2},{1,3},{2,0},{3,1},{4,6},{5,7},{6,4},{7,5},{8,24},{9,25},{10,... | collective-permute-start | bytes 1769480 | tf_op jit(solution)/shard_map/ppermute | solution.py:453
  175.0 21.1 %collective-permute-start.18 = (f32[128,1024]{1,0:T(8,128)}, f32[128,1024]{1,0:T(8,128)S(1)}, u32[]{:S(2)}, u32[]{:S(2)}) collective-permute-start(f32[128,1024]{1,0:T(8,128)} %get-tuple-element.127), channel_id=1, source_target_pairs={{0,1},{1,0},{2,3},{3,2},{4,5},{5,4},{6,7},{7,6},{8,24},{9,25},{10,... | collective-permute-start | bytes 1572872 | tf_op jit(solution)/shard_map/ppermute | solution.py:453
  175.9 18.0 %collective-permute-start.17 = (f32[192,512]{1,0:T(8,128)}, f32[192,512]{1,0:T(8,128)S(1)}, u32[]{:S(2)}, u32[]{:S(2)}) collective-permute-start(f32[192,512]{1,0:T(8,128)} %get-tuple-element.125), channel_id=1, source_target_pairs={{0,4},{1,5},{2,6},{3,7},{4,0},{5,1},{6,2},{7,3},{8,10},{9,11},{10,... | collective-permute-start | bytes 1179656 | tf_op jit(solution)/shard_map/ppermute | solution.py:453
  178.2 9.0 %collective-permute-start.16 = (f32[128,512]{1,0:T(8,128)}, f32[128,512]{1,0:T(8,128)S(1)}, u32[]{:S(2)}, u32[]{:S(2)}) collective-permute-start(f32[128,512]{1,0:T(8,128)} %get-tuple-element.123), channel_id=1, source_target_pairs={{0,1},{1,0},{2,3},{3,2},{4,5},{5,4},{6,7},{7,6},{8,10},{9,11},{10,... | collective-permute-start | bytes 786440 | tf_op jit(solution)/shard_map/ppermute | solution.py:453
  194.0 7.2 collective-permute-start.21
  195.4 5.7 collective-permute-start.20
  196.2 16.3 %collective-permute-start.23 = (f32[64,1152]{1,0:T(8,128)S(1)}, f32[64,1152]{1,0:T(8,128)S(1)}, u32[]{:S(2)}, u32[]{:S(2)}) collective-permute-start(f32[64,1152]{1,0:T(8,128)S(1)} %get-tuple-element.135), channel_id=1, source_target_pairs={{0,4},{1,5},{2,6},{3,7},{4,0},{5,1},{6,2},{7,3},{8,9},{9,8},{10,11... | collective-permute-start | bytes 884744 | tf_op jit(solution)/shard_map/ppermute | solution.py:453
  199.6 12.9 %collective-permute-start.22 = (f32[64,1024]{1,0:T(8,128)S(1)}, f32[64,1024]{1,0:T(8,128)S(1)}, u32[]{:S(2)}, u32[]{:S(2)}) collective-permute-start(f32[64,1024]{1,0:T(8,128)S(1)} %get-tuple-element.133), channel_id=1, source_target_pairs={{0,2},{1,3},{2,0},{3,1},{4,6},{5,7},{6,4},{7,5},{8,9},{9,8},{10,11... | collective-permute-start | bytes 786440 | tf_op jit(solution)/shard_map/ppermute | solution.py:453
  201.2 11.4 %collective-permute-start.25 = (f32[96,512]{1,0:T(8,128)S(1)}, f32[96,512]{1,0:T(8,128)S(1)}, u32[]{:S(2)}, u32[]{:S(2)}) collective-permute-start(f32[96,512]{1,0:T(8,128)S(1)} %shard_map.220._.mine), channel_id=1, source_target_pairs={{0,16},{1,17},{2,18},{3,19},{4,20},{5,21},{6,22},{7,23},{8,12},{9,... | collective-permute-start | bytes 589832 | tf_op jit(solution)/shard_map/ppermute | solution.py:453
  202.6 10.0 %collective-permute-start.24 = (f32[64,512]{1,0:T(8,128)S(1)}, f32[64,512]{1,0:T(8,128)S(1)}, u32[]{:S(2)}, u32[]{:S(2)}) collective-permute-start(f32[64,512]{1,0:T(8,128)S(1)} %shard_map.219._.mine), channel_id=1, source_target_pairs={{0,16},{1,17},{2,18},{3,19},{4,20},{5,21},{6,22},{7,23},{8,12},{9,... | collective-permute-start | bytes 393224 | tf_op jit(solution)/shard_map/ppermute | solution.py:453
  212.7 18.9 %collective-permute-start.29 = (f32[192,512]{1,0:T(8,128)S(1)}, f32[192,512]{1,0:T(8,128)S(1)}, u32[]{:S(2)}, u32[]{:S(2)}) collective-permute-start(f32[192,512]{1,0:T(8,128)S(1)} %shard_map.224._.mine), channel_id=1, source_target_pairs={{0,4},{1,5},{2,6},{3,7},{4,0},{5,1},{6,2},{7,3},{8,10},{9,11},{10,... | collective-permute-start | bytes 1179656 | tf_op jit(solution)/shard_map/ppermute | solution.py:453
  212.8 18.8 %collective-permute-start.28 = (f32[128,512]{1,0:T(8,128)S(1)}, f32[128,512]{1,0:T(8,128)S(1)}, u32[]{:S(2)}, u32[]{:S(2)}) collective-permute-start(f32[128,512]{1,0:T(8,128)S(1)} %shard_map.223._.mine), channel_id=1, source_target_pairs={{0,1},{1,0},{2,3},{3,2},{4,5},{5,4},{6,7},{7,6},{8,10},{9,11},{10,... | collective-permute-start | bytes 786440 | tf_op jit(solution)/shard_map/ppermute | solution.py:453
  213.5 18.0 %collective-permute-start.27 = (f32[32,1152]{1,0:T(8,128)S(1)}, f32[32,1152]{1,0:T(8,128)S(1)}, u32[]{:S(2)}, u32[]{:S(2)}) collective-permute-start(f32[32,1152]{1,0:T(8,128)S(1)} %get-tuple-element.139), channel_id=1, source_target_pairs={{0,1},{1,0},{2,3},{3,2},{4,5},{5,4},{6,7},{7,6},{8,10},{9,11},{10,... | collective-permute-start | bytes 442376 | tf_op jit(solution)/shard_map/ppermute | solution.py:453
  214.9 16.6 %collective-permute-start.26 = (f32[32,1024]{1,0:T(8,128)S(1)}, f32[32,1024]{1,0:T(8,128)S(1)}, u32[]{:S(2)}, u32[]{:S(2)}) collective-permute-start(f32[32,1024]{1,0:T(8,128)S(1)} %get-tuple-element.137), channel_id=1, source_target_pairs={{0,4},{1,5},{2,6},{3,7},{4,0},{5,1},{6,2},{7,3},{8,10},{9,11},{10,... | collective-permute-start | bytes 393224 | tf_op jit(solution)/shard_map/ppermute | solution.py:453
  231.7 24.5 %collective-permute-start.33 = (f32[384,512]{1,0:T(8,128)S(1)}, f32[384,512]{1,0:T(8,128)S(1)}, u32[]{:S(2)}, u32[]{:S(2)}) collective-permute-start(f32[384,512]{1,0:T(8,128)S(1)} %shard_map.228._.mine), channel_id=1, source_target_pairs={{0,2},{1,3},{2,0},{3,1},{4,6},{5,7},{6,4},{7,5},{8,9},{9,8},{10,11... | collective-permute-start | bytes 2359304 | tf_op jit(solution)/shard_map/ppermute | solution.py:453
  231.8 22.2 %collective-permute-start.32 = (f32[256,512]{1,0:T(8,128)S(1)}, f32[256,512]{1,0:T(8,128)S(1)}, u32[]{:S(2)}, u32[]{:S(2)}) collective-permute-start(f32[256,512]{1,0:T(8,128)S(1)} %shard_map.227._.mine), channel_id=1, source_target_pairs={{0,4},{1,5},{2,6},{3,7},{4,0},{5,1},{6,2},{7,3},{8,9},{9,8},{10,11... | collective-permute-start | bytes 1572872 | tf_op jit(solution)/shard_map/ppermute | solution.py:453
  234.8 5.6 collective-permute-start.31
  236.1 4.3 collective-permute-start.30
  256.3 32.1 %collective-permute-start.38 = (f32[768,512]{1,0:T(8,128)S(1)}, f32[768,512]{1,0:T(8,128)S(1)}, u32[]{:S(2)}, u32[]{:S(2)}) collective-permute-start(f32[768,512]{1,0:T(8,128)S(1)} %shard_map.232._.mine), channel_id=1, source_target_pairs={{0,1},{1,0},{2,3},{3,2},{4,5},{5,4},{6,7},{7,6},{8,24},{9,25},{10,... | collective-permute-start | bytes 4718600 | tf_op jit(solution)/shard_map/ppermute | solution.py:453
  257.0 15.6 %collective-permute-start.36 = (f32[512,512]{1,0:T(8,128)S(1)}, f32[512,512]{1,0:T(8,128)S(1)}, u32[]{:S(2)}, u32[]{:S(2)}) collective-permute-start(f32[512,512]{1,0:T(8,128)S(1)} %shard_map.231._.mine), channel_id=1, source_target_pairs={{0,2},{1,3},{2,0},{3,1},{4,6},{5,7},{6,4},{7,5},{8,24},{9,25},{10,... | collective-permute-start | bytes 3145736 | tf_op jit(solution)/shard_map/ppermute | solution.py:453
  257.3 5.6 collective-permute-start.35
  258.6 4.3 collective-permute-start.34
  288.7 67.2 %collective-permute-start.39 = (f32[1536,512]{1,0:T(8,128)S(1)}, f32[1536,512]{1,0:T(8,128)}, u32[]{:S(2)}, u32[]{:S(2)}) collective-permute-start(f32[1536,512]{1,0:T(8,128)S(1)} %shard_map.236._.mine_b), channel_id=1, source_target_pairs={{0,8},{1,9},{2,10},{3,11},{4,12},{5,13},{6,14},{7,15},{8,0},{9,1},... | collective-permute-start | bytes 9437192 | tf_op jit(solution)/shard_map/ppermute | solution.py:453
  315.9 7.1 collective-permute-start.41
  316.6 6.4 collective-permute-start.40
  316.6 39.3 %collective-permute-start.37 = (f32[1024,512]{1,0:T(8,128)}, f32[1024,512]{1,0:T(8,128)}, u32[]{:S(2)}, u32[]{:S(2)}) collective-permute-start(f32[1024,512]{1,0:T(8,128)} %shard_map.235._.mine_a), channel_id=1, source_target_pairs={{0,8},{1,9},{2,10},{3,11},{4,12},{5,13},{6,14},{7,15},{8,0},{9,1},... | collective-permute-start | bytes 6291464 | tf_op jit(solution)/shard_map/ppermute | solution.py:453
  323.1 10.5 %collective-permute-start.43 = (f32[64,1152]{1,0:T(8,128)S(1)}, f32[64,1152]{1,0:T(8,128)S(1)}, u32[]{:S(2)}, u32[]{:S(2)}) collective-permute-start(f32[64,1152]{1,0:T(8,128)S(1)} %shard_map.238._.mine), channel_id=1, source_target_pairs={{0,4},{1,5},{2,6},{3,7},{4,0},{5,1},{6,2},{7,3},{8,9},{9,8},{10,11... | collective-permute-start | bytes 884744 | tf_op jit(solution)/shard_map/ppermute | solution.py:453
  324.0 9.5 %collective-permute-start.42 = (f32[64,1024]{1,0:T(8,128)S(1)}, f32[64,1024]{1,0:T(8,128)S(1)}, u32[]{:S(2)}, u32[]{:S(2)}) collective-permute-start(f32[64,1024]{1,0:T(8,128)S(1)} %shard_map.237._.mine), channel_id=1, source_target_pairs={{0,2},{1,3},{2,0},{3,1},{4,6},{5,7},{6,4},{7,5},{8,9},{9,8},{10,11... | collective-permute-start | bytes 786440 | tf_op jit(solution)/shard_map/ppermute | solution.py:453
  333.6 10.4 %collective-permute-start.46 = (f32[128,1152]{1,0:T(8,128)S(1)}, f32[128,1152]{1,0:T(8,128)S(1)}, u32[]{:S(2)}, u32[]{:S(2)}) collective-permute-start(f32[128,1152]{1,0:T(8,128)S(1)} %shard_map.240._.mine), channel_id=1, source_target_pairs={{0,2},{1,3},{2,0},{3,1},{4,6},{5,7},{6,4},{7,5},{8,24},{9,25},{10,... | collective-permute-start | bytes 1769480 | tf_op jit(solution)/shard_map/ppermute | solution.py:453
  333.8 9.2 %collective-permute-start.44 = (f32[128,1024]{1,0:T(8,128)S(1)}, f32[128,1024]{1,0:T(8,128)S(1)}, u32[]{:S(2)}, u32[]{:S(2)}) collective-permute-start(f32[128,1024]{1,0:T(8,128)S(1)} %shard_map.239._.mine), channel_id=1, source_target_pairs={{0,1},{1,0},{2,3},{3,2},{4,5},{5,4},{6,7},{7,6},{8,24},{9,25},{10,... | collective-permute-start | bytes 1572872 | tf_op jit(solution)/shard_map/ppermute | solution.py:453
  345.2 10.7 %collective-permute-start.47 = (f32[256,1152]{1,0:T(8,128)}, f32[256,1152]{1,0:T(8,128)}, u32[]{:S(2)}, u32[]{:S(2)}) collective-permute-start(f32[256,1152]{1,0:T(8,128)} %shard_map.242.mine_d), channel_id=1, source_target_pairs={{0,8},{1,9},{2,10},{3,11},{4,12},{5,13},{6,14},{7,15},{8,0},{9,1},... | collective-permute-start | bytes 3538952 | tf_op jit(solution)/shard_map/ppermute | solution.py:453
  347.6 8.3 %collective-permute-start.45 = (f32[256,1024]{1,0:T(8,128)}, f32[256,1024]{1,0:T(8,128)}, u32[]{:S(2)}, u32[]{:S(2)}) collective-permute-start(f32[256,1024]{1,0:T(8,128)} %shard_map.241._.mine_c), channel_id=1, source_target_pairs={{0,8},{1,9},{2,10},{3,11},{4,12},{5,13},{6,14},{7,15},{8,0},{9,1},... | collective-permute-start | bytes 3145736 | tf_op jit(solution)/shard_map/ppermute | solution.py:453
  347.6 5.8 collective-permute-start.9
  (51 other events, 417.9 us)

commit v2 on v1

--- a/solution.py
+++ b/solution.py
@@ -12,8 +12,85 @@
 VMEM = pl.BlockSpec(memory_space=pltpu.VMEM)
 SMEM = pl.BlockSpec(memory_space=pltpu.SMEM)
 KINDS = "TSST"
+CHUNKS = 4
 EARLY = (0, 1, 0, 1)
 SUB = 8
+
+
+HBM = pl.BlockSpec(memory_space=pltpu.HBM)
+
+
+class Staged:
+    def __init__(self, sources, buffers, targets, results, sems, chunks):
+        self.ins, self.pending, self.sems, self.next = {}, [], sems, 0
+        self.targets, self.results = targets, results
+        order = []
+        for i, (source, buffer) in enumerate(zip(sources, buffers)):
+            parts = chunks.get(i, 1)
+            rows = source.shape[0] // parts
+            self.ins[i] = []
+            for c in range(parts):
+                at = pl.ds(c * rows, rows)
+                pair = (source, buffer) if parts == 1 else (source.at[at], buffer.at[at])
+                self.ins[i].append(self.copy(*pair))
+                order.append((c, self.ins[i][-1]))
+        for _, copy in sorted(order, key=lambda pair: pair[0]):
+            copy.start()
+
+    def copy(self, source, target):
+        self.next += 1
+        return pltpu.make_async_copy(source, target, self.sems.at[self.next - 1])
+
+    def need(self, *indices):
+        for i in indices:
+            for copy in self.ins[i]:
+                copy.wait()
+
+    def need_chunk(self, c, *indices):
+        for i in indices:
+            self.ins[i][c].wait()
+
+    def done(self, *indices):
+        for i in indices:
+            copy = self.copy(self.results[i], self.targets[i])
+            copy.start()
+            self.pending.append(copy)
+
+    def send(self, source, target):
+        copy = self.copy(source, target)
+        copy.start()
+        self.pending.append(copy)
+
+    def finish(self):
+        for copy in self.pending:
+            copy.wait()
+
+
+def staged_call(kernel, scalars, ins, outs, extra_outs, scratch, flops, copies, chunks=None, reverse=False):
+    n_s, n_i, n_o, n_e = len(scalars), len(ins), len(outs), len(extra_outs)
+
+    def body(*refs):
+        cut = [0]
+        for size in (n_s, n_i, n_o, n_e, n_i, n_o, len(scratch)):
+            cut.append(cut[-1] + size)
+        scalar, source, target, extra, buffer, result, own = [refs[a:b] for a, b in zip(cut, cut[1:])]
+        stage = Staged(source, buffer, target, result, refs[-1], chunks or {})
+        kernel(stage, scalar, buffer, result, extra, own)
+        stage.finish()
+
+    results = pl.pallas_call(
+        body,
+        in_specs=[SMEM] * n_s + [HBM] * n_i,
+        out_specs=(HBM,) * (n_o + n_e),
+        out_shape=shaped(*outs, *extra_outs),
+        scratch_shapes=[pltpu.VMEM(a.shape, a.dtype) for a in ins]
+        + [pltpu.VMEM(shape, kind) for shape, kind in outs]
+        + [pltpu.VMEM(shape, kind) for shape, kind in scratch]
+        + [pltpu.SemaphoreType.DMA((copies,))],
+        compiler_params=pltpu.CompilerParams(vmem_limit_bytes=56 << 20),
+        cost_estimate=pl.CostEstimate(flops=flops, bytes_accessed=8 << 20, transcendentals=0),
+    )(*scalars, *ins)
+    return results
 
 
 def dot(left, right):
@@ -79,19 +156,21 @@
     return [spread[k] for k in range(lag)]
 
 
-def gates_kernel(
-    first_len, tokens, cotangent, rim, gain_one, conv_weight, w_z, bias_z, w_h,
-    x_out, up_out, conv_out, keep_out, drive_out, cand_out, gate_out, pass_out, subk, subs, totals,
-    ext, spread, lag_order,
-):
+def gates_kernel(stage, scalars, ins, outs, extra, scratch):
+    (first_len,) = scalars
+    tokens, rim, gain_one, conv_weight, w_z, bias_z, w_h, cotangent = ins
+    x_out, conv_out, keep_out, drive_out, cand_out, gate_out, pass_out, subk, subs, totals, up_out = outs
+    ext, spread = scratch
     rows, group_len, width = tokens.shape
     count, lag = rows * group_len, rim.shape[1]
     hidden = w_z.shape[1]
     seq_start = lax.axis_index("seq") * group_len
     order = segment_order(count)
+    stage.need(0)
     x = dot(order, tokens[...].reshape(count, width))
     x_out[...] = x.astype(BF16)
-    up_out[...] = dot(order, cotangent[...].reshape(count, width)).astype(BF16)
+    stage.done(0)
+    stage.need(1, 2, 3)
     normed = x * rms(x) * gain_one[...]
     ext[lag * SUB :, :] = normed
     rim_x = rim_tiles(rim, spread)
@@ -100,8 +179,10 @@
     for j in range(lag + 1):
         begin = (lag - j) * SUB
         mixed = mixed + conv_weight[j : j + 1, :] * ext[begin : begin + count, :]
-    conv_low = mixed.astype(BF16)
-    conv_out[...] = conv_low
+    conv_out[...] = mixed.astype(BF16)
+    stage.done(1)
+    stage.need(4, 5, 6)
+    mask = opened(first_len, seq_start, (SUB, hidden))
     block = 256
     for b in range(hidden // block):
         cols = slice(b * block, (b + 1) * block)
@@ -111,15 +192,16 @@
         large = 1.0 / (1.0 + small)
         small = small * large
         zeta = jnp.where(g >= 0, large, small)
-        keep = jnp.where(g >= 0, small, large)
         sig = 1.0 / (1.0 + jnp.exp(-c))
         cand = jnp.where(c >= 0, c + 0.5, sig)
-        keep_out[:, cols] = keep
+        keep_out[:, cols] = jnp.where(g >= 0, small, large)
+        keep_out[0:SUB, cols] = keep_out[0:SUB, cols] * mask[:, cols]
         drive_out[:, cols] = zeta * cand
         cand_out[:, cols] = cand
-        gate_out[:, cols] = small * large
-        pass_out[:, cols] = zeta * jnp.where(c >= 0, 1.0, sig * (1.0 - sig))
-    keep_out[0:SUB, :] = keep_out[0:SUB, :] * opened(first_len, seq_start, (SUB, hidden))
+        gate_out[:, cols] = (small * large).astype(BF16)
+        pass_out[:, cols] = (zeta * jnp.where(c >= 0, 1.0, sig * (1.0 - sig))).astype(BF16)
+        for i in (2, 3, 4, 5, 6):
+            stage.send(outs[i].at[:, pl.ds(b * block, block)], stage.targets[i].at[:, pl.ds(b * block, block)])
 
     def step(i, carry):
         total, state = carry
@@ -142,80 +224,100 @@
             k = k * subk[at, :]
         totals[0, r : r + 1, :] = k
         totals[1, r : r + 1, :] = s
-
-
-def by_core(first, mine, other, at, for_even, for_odd):
-    @pl.when(first)
+    stage.done(7, 8, 9)
+    stage.need(7)
+    up_out[...] = dot(order, cotangent[...].reshape(count, width)).astype(BF16)
+    stage.done(10)
+
+
+def give_pair(stage, even, pairs):
+    found = []
+    for one, two, mine, other in pairs:
+        found.append((stage.copy(one, mine), stage.copy(two, other), one, two, mine, other, stage.next))
+
+    @pl.when(even)
     def _():
-        mine[at, :] = for_even
-        other[at, :] = for_odd
-
-    @pl.when(jnp.logical_not(first))
+        for first, second, *_ in found:
+            first.start()
+            second.start()
+
+    @pl.when(jnp.logical_not(even))
     def _():
-        mine[at, :] = for_odd
-        other[at, :] = for_even
-
-
-def mlp_kernel(
-    first_len, carried, subk, subs, keep, drive, x, up, w_out, gain_two, w_up, w_down,
-    state_out, before_out, output, mine_a, other_a, mine_b, other_b,
-    grad_middle_out, grad_gain_two, grad_state, subb, totals,
-    low, second_low, tail, second_grad, middle_ref,
-):
+        for _, _, one, two, mine, other, at in found:
+            pltpu.make_async_copy(two, mine, stage.sems.at[at - 2]).start()
+            pltpu.make_async_copy(one, other, stage.sems.at[at - 1]).start()
+
+    for first, second, *_ in found:
+        stage.pending += [first, second]
+
+
+def mlp_kernel(stage, scalars, ins, outs, extra, scratch):
+    (first_len,) = scalars
+    carried, subk, subs, keep, drive, cand, gate, x, w_out, gain_two, w_up, w_down, up = ins
+    blend, output, grad_middle_out, grad_gain_two, grad_state, subb, totals = outs
+    mine_a, other_a, mine_b, other_b = extra
+    before, low, second_low, tail, second_grad, middle_ref, for_even, for_odd, out_even, out_odd = scratch
     count, width = x.shape
     hidden, ff = keep.shape[1], w_up.shape[1]
     rows = carried.shape[0]
     group_len = count // rows
     parts = SUB // rows
-    steps = count // SUB
+    pairs = count // SUB // 2
     seq_start = lax.axis_index("seq") * group_len
     even = lax.axis_index("row") % 2 == 0
-    mask = opened(first_len, seq_start, (SUB, hidden))
+    stage.need(0, 1, 2)
     for r in range(rows):
         s = carried[r : r + 1, :]
-        before_out[r * parts : r * parts + 1, :] = s
+        before[r * parts : r * parts + 1, :] = s
         for h in range(1, parts):
             at = slice(r * parts + h - 1, r * parts + h)
             s = subs[at, :] + subk[at, :] * s
-            before_out[r * parts + h : r * parts + h + 1, :] = s
-    before_out[...] = before_out[...] * mask
-
-    def step(i, state):
-        at = pl.ds(pl.multiple_of(i * SUB, SUB), SUB)
-        state = keep[at, :] * state + drive[at, :]
-        state_out[at, :] = state
-        return state
-
-    lax.fori_loop(0, steps, step, before_out[...], unroll=8)
-    low[...] = state_out[...].astype(BF16)
+            before[r * parts + h : r * parts + h + 1, :] = s
+
+    def two(i, state):
+        at = pl.ds(pl.multiple_of(i * 2 * SUB, 2 * SUB), 2 * SUB)
+        k, d, c, g = keep[at, :], drive[at, :], cand[at, :], gate[at, :].astype(F32)
+        first = k[:SUB] * state + d[:SUB]
+        second = k[SUB:] * first + d[SUB:]
+        low[at, :] = jnp.concatenate([first, second], axis=0).astype(BF16)
+        earlier = jnp.concatenate([state, first], axis=0)
+        blend[at, :] = ((c - earlier) * g).astype(BF16)
+        return second
+
+    state = before[...] * opened(first_len, seq_start, (SUB, hidden))
+    for c in range(CHUNKS):
+        stage.need_chunk(c, 3, 4, 5, 6)
+        state = lax.fori_loop(c * pairs // CHUNKS, (c + 1) * pairs // CHUNKS, two, state, unroll=2)
+    stage.done(0)
+    stage.need(7, 8, 9)
     middle = x[...].astype(F32) + dot(low[...], w_out[...])
     middle_ref[...] = middle
     second_low[...] = (middle * rms(middle) * gain_two[...]).astype(BF16)
     tail[...] = jnp.zeros_like(tail)
     second_grad[...] = jnp.zeros_like(second_grad)
+    stage.need(10, 11, 12)
     block = width
     half = ff // block // 2
-    for mine, other, begin in ((mine_a, other_a, 0), (mine_b, other_b, half)):
-
-        def part(b, carry):
-            cols = pl.ds(pl.multiple_of((b + begin) * block, block), block)
-            at = pl.ds(pl.multiple_of(b * block, block), block)
-            pre = dot(second_low[...], w_up[:, cols])
-            back = dot_rt(up[...], w_down[cols, :])
-            scaled = pre * 0.7071067811865476
-            phi = 0.5 + 0.5 * lax.erf(scaled)
-            active = (pre * phi).astype(BF16)
-            slope = phi + pre * (0.3989422804014327 * jnp.exp(-scaled * scaled))
-            up_low = (slope * back).astype(BF16)
-            by_core(even, mine, other, at, dot_lt(active, up[...]), dot_lt(second_low[...], up_low))
-            tail[...] += dot(active, w_down[cols, :])
-            second_grad[...] += dot_rt(up_low, w_up[:, cols])
-            return carry
-
-        lax.fori_loop(0, half, part, 0)
-    order = segment_order(count)
-    result = (middle_ref[...] + tail[...]).astype(BF16)
-    output[...] = dot_lt(order, result).astype(BF16).reshape(output.shape)
+
+    def part(b, carry):
+        at = pl.ds(pl.multiple_of(b * block, block), block)
+        pre = dot(second_low[...], w_up[:, at])
+        back = dot_rt(up[...], w_down[at, :])
+        scaled = pre * 0.7071067811865476
+        phi = 0.5 + 0.5 * lax.erf(scaled)
+        active = (pre * phi).astype(BF16)
+        slope = phi + pre * (0.3989422804014327 * jnp.exp(-scaled * scaled))
+        up_low = (slope * back).astype(BF16)
+        for_even[at, :] = dot_lt(active, up[...])
+        for_odd[at, :] = dot_lt(second_low[...], up_low)
+        tail[...] += dot(active, w_down[at, :])
+        second_grad[...] += dot_rt(up_low, w_up[:, at])
+        return carry
+
+    for k, (mine, other) in enumerate(((mine_a, other_a), (mine_b, other_b))):
+        lax.fori_loop(k * half, (k + 1) * half, part, 0)
+        at, to = pl.ds(k * half * block, half * block), pl.ds(0, half * block)
+        give_pair(stage, even, [(for_even.at[at], for_odd.at[at], mine.at[to], other.at[to])])
 
     middle = middle_ref[...]
     scale = rms(middle)
@@ -225,19 +327,16 @@
     grad = grad * gain_two[...]
     grad_middle = up[...].astype(F32) + scale * (grad - unit * jnp.mean(grad * unit, axis=-1, keepdims=True))
     grad_middle_out[...] = grad_middle
+    stage.done(2, 3)
     middle_low = grad_middle.astype(BF16)
     grad_state[...] = dot_rt(middle_low, w_out[...])
-    half_h = hidden // 2
-    by_core(
-        even, mine_b, other_b, slice(half * block, half * block + half_h),
-        dot_lt(low[:, :half_h], middle_low), dot_lt(low[:, half_h:], middle_low),
-    )
+    stage.done(4)
 
     def back_step(i, passed):
-        at = pl.ds(pl.multiple_of((steps - 1 - i) * SUB, SUB), SUB)
+        at = pl.ds(pl.multiple_of((2 * pairs - 1 - i) * SUB, SUB), SUB)
         return keep[at, :] * (grad_state[at, :] + passed)
 
-    subb[...] = lax.fori_loop(0, steps, back_step, jnp.zeros((SUB, hidden), F32), unroll=8)
+    subb[...] = lax.fori_loop(0, 2 * pairs, back_step, jnp.zeros((SUB, hidden), F32), unroll=8)
     for r in range(rows):
         end = r * parts + parts - 1
         b = subb[end : end + 1, :]
@@ -245,20 +344,32 @@
             at = slice(r * parts + h, r * parts + h + 1)
             b = subb[at, :] + subk[at, :] * b
         totals[r : r + 1, :] = b
-
-
-def first_kernel(
-    first_len, returned, subk, subb, keep, grad_state, state, before, cand, gate, passing, conv_low,
-    x_ref, rim, gain_one, conv_weight, w_z, w_h, grad_middle, grad_gain_two, token,
-    mine_a, other_a, mine_b, other_b, grad_tokens, sent, tail_normed, tail_middle,
-    incoming, gate_low, cand_low, ext, spread, grad_ext, bias_sum, small,
-):
+    stage.done(5, 6)
+    half_h = hidden // 2
+    out_even[...] = dot_lt(low[:, :half_h], middle_low)
+    out_odd[...] = dot_lt(low[:, half_h:], middle_low)
+    to = pl.ds(half * block, half_h)
+    give_pair(stage, even, [(out_even, out_odd, mine_b.at[to], other_b.at[to])])
+    result = (middle_ref[...] + tail[...]).astype(BF16)
+    output[...] = dot_lt(segment_order(count), result).astype(BF16).reshape(output.shape)
+    stage.done(1)
+
+
+def first_kernel(stage, scalars, ins, outs, extra, scratch):
+    (first_len,) = scalars
+    (returned, subk, subb, keep, grad_state, blend, passing, conv_low, w_z, w_h, x_ref, rim, gain_one, conv_weight,
+     grad_middle, grad_gain_two) = ins
+    grad_tokens, sent, tail_normed, tail_middle = outs
+    mine_a, other_a, mine_b, other_b = extra
+    incoming, gate_low, cand_low, ext, spread, grad_ext, bias_sum, small, for_even, for_odd, rest = scratch
     count, width = x_ref.shape
     hidden = keep.shape[1]
     rows, lag = rim.shape[0], rim.shape[1]
     parts = SUB // rows
-    steps = count // SUB
+    pairs = count // SUB // 2
     seq_start = lax.axis_index("seq") * (count // rows)
+    even = lax.axis_index("row") % 2 == 0
+    stage.need(0, 1, 2)
     for r in range(rows):
         b = returned[r : r + 1, :]
         incoming[r * parts + parts - 1 : (r + 1) * parts, :] = b
@@ -266,35 +377,36 @@
             at = slice(r * parts + h + 1, r * parts + h + 2)
             b = subb[at, :] + subk[at, :] * b
             incoming[r * parts + h : r * parts + h + 1, :] = b
-    def one(step_at, passed, bias):
-        at = pl.ds(pl.multiple_of(step_at * SUB, SUB), SUB)
-        prior = pl.ds(pl.multiple_of(jnp.maximum(step_at - 1, 0) * SUB, SUB), SUB)
-        adjoint = grad_state[at, :] + passed
-        earlier = jnp.where(step_at > 0, state[prior, :], before[...])
-        grad_g = adjoint * (cand[at, :] - earlier) * gate[at, :]
-        return keep[at, :] * adjoint, bias + grad_g, grad_g, adjoint * passing[at, :]
 
     def two(i, carry):
-        pair = steps // 2 - 1 - i
-        passed, bias, late_g, late_c = one(2 * pair + 1, *carry)
-        passed, bias, early_g, early_c = one(2 * pair, passed, bias)
-        at = pl.ds(pl.multiple_of(pair * 2 * SUB, 2 * SUB), 2 * SUB)
-        gate_low[at, :] = jnp.concatenate([early_g, late_g], axis=0).astype(BF16)
-        cand_low[at, :] = jnp.concatenate([early_c, late_c], axis=0).astype(BF16)
-        return passed, bias
-
-    _, bias = lax.fori_loop(
-        0, steps // 2, two, (incoming[...], jnp.zeros((SUB, hidden), F32)), unroll=2
-    )
+        passed, bias = carry
+        at = pl.ds(pl.multiple_of((pairs - 1 - i) * 2 * SUB, 2 * SUB), 2 * SUB)
+        k, g = keep[at, :], grad_state[at, :]
+        late = g[SUB:] + passed
+        early = g[:SUB] + k[SUB:] * late
+        adjoint = jnp.concatenate([early, late], axis=0)
+        grad_g = adjoint * blend[at, :].astype(F32)
+        gate_low[at, :] = grad_g.astype(BF16)
+        cand_low[at, :] = (adjoint * passing[at, :].astype(F32)).astype(BF16)
+        return k[:SUB] * early, bias + grad_g[:SUB] + grad_g[SUB:]
+
+    carry = (incoming[...], jnp.zeros((SUB, hidden), F32))
+    for c in range(CHUNKS):
+        stage.need_chunk(CHUNKS - 1 - c, 3, 4, 5, 6)
+        carry = lax.fori_loop(c * pairs // CHUNKS, (c + 1) * pairs // CHUNKS, two, carry, unroll=2)
+    bias = carry[1]
     bias_sum[...] = jnp.sum(bias, axis=0, keepdims=True)
-    even = lax.axis_index("row") % 2 == 0
+    stage.need(7)
     half = width // 2
-    for k, (mine, other) in enumerate(((mine_a, other_a), (mine_b, other_b))):
-        cols = slice(k * half, (k + 1) * half)
-        by_core(
-            even, mine.at[:, :hidden], other.at[:, :hidden], slice(0, half),
-            dot_lt(conv_low[:, cols], gate_low[...]), dot_lt(conv_low[:, cols], cand_low[...]),
-        )
+    for_even[...] = dot_lt(conv_low[...], gate_low[...])
+    for_odd[...] = dot_lt(conv_low[...], cand_low[...])
+    cols = pl.ds(0, hidden)
+    low_rows, high_rows = pl.ds(0, half), pl.ds(half, half)
+    give_pair(stage, even, [
+        (for_even.at[low_rows], for_odd.at[low_rows], mine_a, other_a),
+        (for_even.at[high_rows], for_odd.at[high_rows], mine_b.at[:, cols], other_b.at[:, cols]),
+    ])
+    stage.need(8, 9, 10, 11, 12, 13, 14, 15)
     grad_mixed = dot_rt(gate_low[...], w_z[...]) + dot_rt(cand_low[...], w_h[...])
 
     x = x_ref[...].astype(F32)
@@ -336,14 +448,11 @@
     small[0:1, :] = jnp.sum(grad_normed * unit, axis=0, keepdims=True) + jnp.sum(
         grad_gain, axis=0, keepdims=True
     )
-    for mine, keeps in ((mine_b, even), (other_b, jnp.logical_not(even))):
-
-        @pl.when(keeps)
-        def _():
-            mine[:, hidden:] = jnp.zeros((half, 128), F32)
-            for j in range(width // 128):
-                mine[j * SUB : (j + 1) * SUB, hidden:] = small[:, j * 128 : (j + 1) * 128]
-
+    rest[...] = jnp.zeros_like(rest)
+    for j in range(width // 128):
+        rest[j * SUB : (j + 1) * SUB, :] = small[:, j * 128 : (j + 1) * 128]
+    past = pl.ds(hidden, 128)
+    give_pair(stage, even, [(rest.at[low_rows], rest.at[high_rows], mine_b.at[:, past], other_b.at[:, past])])
     for k in range(lag):
         at = count - lag * SUB + k * SUB
         for r in range(rows):
@@ -353,8 +462,10 @@
             tail_middle[r, to : to + 1, :] = grad_middle[row : row + 1, :]
     grad = grad_normed * gain
     grad_x = grad_middle[...] + scale * (grad - unit * jnp.mean(grad * unit, axis=-1, keepdims=True))
+    stage.done(1, 2, 3)
     order = segment_order(count)
     grad_tokens[...] = dot_lt(order, grad_x.astype(BF16)).astype(BF16).reshape(grad_tokens.shape)
+    stage.done(0)
 
 
 def tail_kernel(tokens, tail_normed, tail_middle, received, gain_one, _, grad_tokens, spread):
@@ -373,19 +484,6 @@
 
 def shaped(*shapes):
     return tuple(jax.ShapeDtypeStruct(shape, kind) for shape, kind in shapes)
-
-
-def call(kernel, in_specs, outs, scratch, flops, **more):
-    return pl.pallas_call(
-        kernel,
-        in_specs=in_specs,
-        out_specs=(VMEM,) * len(outs),
-        out_shape=shaped(*outs),
-        scratch_shapes=[pltpu.VMEM(shape, kind) for shape, kind in scratch],
-        compiler_params=pltpu.CompilerParams(vmem_limit_bytes=20 << 20),
-        cost_estimate=pl.CostEstimate(flops=flops, bytes_accessed=1 << 20, transcendentals=0),
-        **more,
-    )
 
 
 def swapped(array, axis, bit):
@@ -567,47 +665,84 @@
         return 2 * len(self.steps) + 2
 
 
-def finish_kernel(
-    mine_a, got_a, mine_b, got_b, mine_c, got_c, mine_d, got_d,
-    grad_down, grad_up, grad_out, grad_z, grad_h, small, sems,
-):
-    block = mine_a.shape[1]
-    width, hidden = grad_z.shape
-    half = width // 2
+def moved(stage_refs, routes, sems):
+    into = []
+    for i, (source, buffer, target) in enumerate(routes):
+        copy = pltpu.make_async_copy(source, buffer, sems.at[i])
+        copy.start()
+        into.append(copy)
+    out = []
+    for i, (source, buffer, target) in enumerate(routes):
+        into[i].wait()
+        copy = pltpu.make_async_copy(buffer, target, sems.at[len(routes) + i])
+        copy.start()
+        out.append(copy)
+    for copy in out:
+        copy.wait()
+
+
+def finish_mlp(_, mine_a, got_a, mine_b, got_b, grad_down, grad_up, grad_out, buffer_a, buffer_b, sems):
+    rows, width = mine_a.shape
+    half_h = grad_out.shape[0] // 2
     even = lax.axis_index("row") % 2 == 0
 
-    def run(a_even, a_odd, b_even, b_odd, c_even, c_odd, d_even, d_odd):
-        rows = mine_a.shape[0]
-        copies = [
-            (a_even, grad_down.at[pl.ds(0, rows), :]),
-            (b_even.at[pl.ds(0, rows), :], grad_down.at[pl.ds(rows, rows), :]),
-            (b_even.at[pl.ds(rows, hidden // 2), :], grad_out.at[pl.ds(0, hidden // 2), :]),
-            (b_odd.at[pl.ds(rows, hidden // 2), :], grad_out.at[pl.ds(hidden // 2, hidden // 2), :]),
-        ]
-        for k in range(rows // block):
-            at = pl.ds(k * block, block)
-            copies.append((a_odd.at[at, :], grad_up.at[:, at]))
-            copies.append((b_odd.at[at, :], grad_up.at[:, pl.ds(rows + k * block, block)]))
-        for k, (one, two) in enumerate(((c_even, c_odd), (d_even, d_odd))):
-            to = pl.ds(k * half, half)
-            copies.append((one.at[:, pl.ds(0, hidden)], grad_z.at[to, :]))
-            copies.append((two.at[:, pl.ds(0, hidden)], grad_h.at[to, :]))
-        copies.append((d_even.at[pl.ds(0, small.shape[0]), pl.ds(hidden, 128)], small))
-        started = [pltpu.make_async_copy(*pair, sems.at[i]) for i, pair in enumerate(copies)]
-        for copy in started:
-            copy.start()
-        for copy in started:
-            copy.wait()
-
-    pairs = ((mine_a, got_a), (mine_b, got_b), (mine_c, got_c), (mine_d, got_d))
+    def run(a, b):
+        routes, room = [], {0: 0, 1: 0}
+        for k, (pair, begin) in enumerate(((a, 0), (b, rows))):
+            for j in range(rows // width):
+                at, to = pl.ds(j * width, width), pl.ds(begin + j * width, width)
+                buffers = buffer_a if k == 0 else buffer_b
+                routes.append((pair[0].at[at], buffers.at[0].at[at], grad_down.at[to]))
+                routes.append((pair[1].at[at], buffers.at[1].at[at], grad_up.at[:, to]))
+        for k in range(2):
+            at = pl.ds(rows, half_h)
+            routes.append((b[k].at[at], buffer_b.at[k].at[at], grad_out.at[pl.ds(k * half_h, half_h)]))
+        moved(None, routes, sems)
 
     @pl.when(even)
     def _():
-        run(*[ref for pair in pairs for ref in pair])
+        run((mine_a, got_a), (mine_b, got_b))
 
     @pl.when(jnp.logical_not(even))
     def _():
-        run(*[ref for pair in pairs for ref in pair[::-1]])
+        run((got_a, mine_a), (got_b, mine_b))
+
+
+def finish_gates(_, mine_c, got_c, mine_d, got_d, grad_z, grad_h, small, buffer_c, buffer_d, sems):
+    half, hidden = grad_z.shape[0] // 2, grad_z.shape[1]
+    even = lax.axis_index("row") % 2 == 0
+
+    def run(c, d):
+        cols, low, high = pl.ds(0, hidden), pl.ds(0, half), pl.ds(half, half)
+        routes = []
+        for k, target in enumerate((grad_z, grad_h)):
+            routes.append((c[k], buffer_c.at[k], target.at[low]))
+            routes.append((d[k].at[:, cols], buffer_d.at[k].at[:, cols], target.at[high]))
+        few, past = pl.ds(0, small.shape[0]), pl.ds(hidden, 128)
+        routes.append((d[0].at[few, past], buffer_d.at[0].at[few, past], small))
+        moved(None, routes, sems)
+
+    @pl.when(even)
+    def _():
+        run((mine_c, got_c), (mine_d, got_d))
+
+    @pl.when(jnp.logical_not(even))
+    def _():
+        run((got_c, mine_c), (got_d, mine_d))
+
+
+def finish_call(kernel, token, sums, outs, copies):
+    arrays = [array for one in sums for array in (one.mine, one.received)]
+    return pl.pallas_call(
+        kernel,
+        in_specs=[pl.BlockSpec(memory_space=pl.ANY)] + [HBM] * len(arrays),
+        out_specs=(HBM,) * len(outs),
+        out_shape=shaped(*outs),
+        scratch_shapes=[pltpu.VMEM((2,) + one.mine.shape, F32) for one in sums]
+        + [pltpu.SemaphoreType.DMA((2 * copies,))],
+        compiler_params=pltpu.CompilerParams(vmem_limit_bytes=32 << 20),
+        cost_estimate=pl.CostEstimate(flops=1, bytes_accessed=1, transcendentals=0),
+    )(token, *arrays)
 
 
 def per_device(
@@ -623,43 +758,57 @@
         tokens[:, group_len - lag :].astype(F32), "seq", [(i, i + 1) for i in range(devices - 1)]
     )
     th, tw = (count, hidden), (count, width)
-    x, up, conv_low, keep, drive, cand, gate, passing, subk, subs, totals = call(
+    chunks = {3: CHUNKS, 4: CHUNKS, 5: CHUNKS, 6: CHUNKS}
+    x, conv_low, keep, drive, cand, gate, passing, subk, subs, totals, up = staged_call(
         gates_kernel,
-        [SMEM] + [VMEM] * 8,
-        [(tw, BF16), (tw, BF16), (tw, BF16)] + [(th, F32)] * 5
-        + [((SUB, hidden), F32)] * 2 + [((2, rows, hidden), F32)],
-        [((count + lag * SUB, width), F32), ((lag, SUB, width), F32), ((8, 128), F32)],
+        [first_len],
+        [tokens, rim, gain_one, conv_weight, w_z, bias_z, w_h, cotangent],
+        [(tw, BF16), (tw, BF16), (th, F32), (th, F32), (th, F32), (th, BF16), (th, BF16),
+         ((SUB, hidden), F32), ((SUB, hidden), F32), ((2, rows, hidden), F32), (tw, BF16)],
+        [],
+        [((count + lag * SUB, width), F32), ((lag, SUB, width), F32)],
         4 * count * width * hidden,
-    )(first_len, tokens, cotangent, rim, gain_one, conv_weight, w_z, bias_z, w_h)
+        64,
+    )
     carried, levels = carry_forward(totals)
     pairs_a = ((ff // 2, width), F32)
     pairs_b = ((ff // 2 + hidden // 2, width), F32)
-    state, before, output, mine_a, other_a, mine_b, other_b, grad_middle, grad_gain_two, grad_state, subb, passed = call(
+    (blend, output, grad_middle, grad_gain_two, grad_state, subb, passed,
+     mine_a, other_a, mine_b, other_b) = staged_call(
         mlp_kernel,
-        [SMEM] + [VMEM] * 11,
-        [(th, F32), ((SUB, hidden), F32), (tokens.shape, BF16), pairs_a, pairs_a, pairs_b, pairs_b,
-         (tw, F32), ((1, width), F32), (th, F32), ((SUB, hidden), F32), ((rows, hidden), F32)],
-        [(th, BF16), (tw, BF16), (tw, F32), (tw, F32), (tw, F32)],
+        [first_len],
+        [carried, subk, subs, keep, drive, cand, gate, x, w_out, gain_two, w_up, w_down, up],
+        [(th, BF16), (tokens.shape, BF16), (tw, F32), ((1, width), F32), (th, F32), ((SUB, hidden), F32),
+         ((rows, hidden), F32)],
+        [pairs_a, pairs_a, pairs_b, pairs_b],
+        [((SUB, hidden), F32), (th, BF16), (tw, BF16), (tw, F32), (tw, F32), (tw, F32),
+         ((ff, width), F32), ((ff, width), F32), ((hidden // 2, width), F32), ((hidden // 2, width), F32)],
         12 * count * width * ff,
-    )(first_len, carried, subk, subs, keep, drive, x, up, w_out, gain_two, w_up, w_down)
+        64,
+        chunks,
+    )
     returned = carry_backward(passed, levels)
     sums = [Summed(mine_a, other_a, KINDS[0]), Summed(mine_b, other_b, KINDS[1])]
-    token = grad_gain_two
+    token = returned
     for turn in EARLY:
         token = sums[turn].advance(token)
     tile = 16
     pair = ((width // 2, hidden), F32)
     pair_small = ((width // 2, hidden + 128), F32)
-    mine_c, other_c, mine_d, other_d, grad_tokens, sent, tail_normed, tail_middle = call(
+    grad_tokens, sent, tail_normed, tail_middle, mine_c, other_c, mine_d, other_d = staged_call(
         first_kernel,
-        [SMEM] + [VMEM] * 19 + [pl.BlockSpec(memory_space=pl.ANY)],
-        [pair, pair, pair_small, pair_small, (tokens.shape, BF16),
-         ((rows, lag, width), F32)] + [((rows, tile, width), F32)] * 2,
+        [first_len],
+        [returned, subk, subb, keep, grad_state, blend, passing, conv_low, w_z, w_h, x, rim, gain_one,
+         conv_weight, grad_middle, grad_gain_two],
+        [(tokens.shape, BF16), ((rows, lag, width), F32)] + [((rows, tile, width), F32)] * 2,
+        [pair, pair, pair_small, pair_small],
         [((SUB, hidden), F32), (th, BF16), (th, BF16), ((count + lag * SUB, width), F32),
-         ((lag, SUB, width), F32), ((count + lag * SUB, width), F32), ((1, hidden), F32), ((SUB, width), F32)],
+         ((lag, SUB, width), F32), ((count + lag * SUB, width), F32), ((1, hidden), F32), ((SUB, width), F32),
+         ((width, hidden), F32), ((width, hidden), F32), ((width, 128), F32)],
         8 * count * width * hidden,
-    )(first_len, returned, subk, subb, keep, grad_state, state, before, cand, gate, passing, conv_low,
-      x, rim, gain_one, conv_weight, w_z, w_h, grad_middle, grad_gain_two, token)
+        64,
+        chunks,
+    )
     received = lax.ppermute(sent, "seq", [(i + 1, i) for i in range(devices - 1)])
     at_tail = pl.BlockSpec((rows, tile, width), lambda i: (0, group_len // tile - 1, 0))
     whole = lambda *shape: pl.BlockSpec(shape, lambda i: (0,) * len(shape))
@@ -679,17 +828,14 @@
         for one in sums:
             if one.at < one.turns():
                 token = one.advance(token)
-    anywhere = pl.BlockSpec(memory_space=pl.ANY)
-    grad_down, grad_up, grad_out, grad_z, grad_h, small = pl.pallas_call(
-        finish_kernel,
-        in_specs=[anywhere] * 8,
-        out_specs=(anywhere,) * 6,
-        out_shape=shaped(
-            ((ff, width), F32), ((width, ff), F32), ((hidden, width), F32), ((width, hidden), F32),
-            ((width, hidden), F32), ((SUB * width // 128, 128), F32),
-        ),
-        scratch_shapes=[pltpu.SemaphoreType.DMA((24,))],
-    )(*[array for one in sums for array in (one.mine, one.received)])
+    grad_down, grad_up, grad_out = finish_call(
+        finish_mlp, token, sums[:2], [((ff, width), F32), ((width, ff), F32), ((hidden, width), F32)],
+        2 * (ff // width) + 2,
+    )
+    grad_z, grad_h, small = finish_call(
+        finish_gates, token, sums[2:],
+        [((width, hidden), F32), ((width, hidden), F32), ((SUB * width // 128, 128), F32)], 5,
+    )
     small = small.reshape(width // 128, SUB, 128).swapaxes(0, 1).reshape(SUB, width)
     bias_at = 2 + lag
     gain_at = bias_at + hidden // width

time: 806 us -> 317 us (0.39)
  Pallas kernels: 496 us -> 70.9 us
  local copies, waits for them, and re-layouts: 47.1 us -> 6.47 us
  waiting for transfers between devices: 173 us -> 136 us
  starting transfers between devices: 86.8 us -> 97 us
    pallas_call x4 -> x5, Pallas kernels: 474 us -> 47.5 us  [the longest x3 37.6 us: staged_call(): pl.pallas_call(body, in_specs=[SMEM] * n_s + [HBM] * n_i, out_specs=(HBM,...]
    unnamed x104 -> x22, local copies, waits for them, and re-layouts: 45.2 us -> 5.28 us
    ppermute x6, waiting for transfers between devices: 34.3 us -> 12.5 us  [swapped(): lax.ppermute(array, axis, [(i, i ^ bit) for i in range(lax.axis_size(axis...]
    ppermute x40, waiting for transfers between devices: 133 us -> 118 us  [exchanged(): return lax.ppermute(array, BOTH, pairs)]
    ppermute x40, starting transfers between devices: 66.1 us -> 76.5 us  [exchanged(): return lax.ppermute(array, BOTH, pairs)]
  transfers between devices with their start and end apart: 48 -> 48, of which waited for: 24 -> 26; matrix products, arithmetic and copies ran while one was open for 0% -> 1% of each run, Pallas kernels for 3% -> 10%
where the time goes in v2:
time: 317 us; the launch traced here: 315 us
  waiting for transfers between devices  136 us (43%)
  starting transfers between devices  97 us (31%)
  Pallas kernels  70.9 us (22%)
  local copies, waits for them, and re-layouts  6.47 us (2%)
    ppermute x40, waiting for transfers between devices, exchanged(): return lax.ppermute(array, BOTH, pairs)  118 us
    ppermute x40, starting transfers between devices, exchanged(): return lax.ppermute(array, BOTH, pairs)  76.5 us
    pallas_call x3, Pallas kernels, staged_call(): pl.pallas_call(body, in_specs=[SMEM] * n_s + [HBM] * n_i, out_specs=(HBM,...  37.6 us
    pallas_call x36, Pallas kernels, piece_call(): pl.pallas_call(kernel, in_specs=[pl.BlockSpec(memory_space=pl.ANY)] + spe...  21.6 us
    ppermute x6, starting transfers between devices, swapped(): lax.ppermute(array, axis, [(i, i ^ bit) for i in range(lax.axis_size(axis...  14.4 us
    ppermute x6, waiting for transfers between devices, swapped(): lax.ppermute(array, axis, [(i, i ^ bit) for i in range(lax.axis_size(axis...  12.5 us
    pallas_call x2, Pallas kernels, finish_call(): pl.pallas_call(kernel, in_specs=[pl.BlockSpec(memory_space=pl.ANY)] + [HB...  9.92 us
  transfers between devices with their start and end apart: 48, of which 26 were waited for; matrix products, arithmetic and copies ran while one was open for 1% of the time, Pallas kernels for 10%

profile of v2, /device:TPU:0, one launch (start us, length us, event | category | flops | bytes accessed | tf_op | source)
XLA Modules:
  0.0 314.7 jit_solution(13157537469092375731)
XLA Ops:
  1.4 4.8 %collective-permute-start = (f32[4,3,512]{2,1,0:T(4,128)S(1)}, f32[4,3,512]{2,1,0:T(4,128)S(1)}, u32[]{:S(2)}, u32[]{:S(2)}) collective-permute-start(f32[4,3,512]{2,1,0:T(4,128)S(1)} %slice_convert_fusion), channel_id=1, source_target_pairs={{0,1},{1,2},{2,3},{3,4},{4,5},{5,6},{6,7},{8,9},{9,10},{10,11},{11... | collective-permute-start | bytes 73736 | tf_op jit(solution)/shard_map/ppermute | solution.py:757
  8.4 7.5 %shard_map.203 = (bf16[512,512]{1,0:T(8,128)(2,1)}, bf16[512,512]{1,0:T(8,128)(2,1)}, f32[512,1024]{1,0:T(8,128)}, f32[512,1024]{1,0:T(8,128)}, f32[512,1024]{1,...) custom-call(s32[4]{0:T(128)} %refs_0_.5, ...), custom_call_target="tpu_custom_call" | custom-call | flops 1073741824 | bytes 8388608 | tf_op jit(solution)/shard_map/pallas_call | solution.py:81
  15.9 2.3 collective-permute-start.1
  18.3 2.1 collective-permute-done.1
  21.1 3.1 collective-permute-start.2
  24.2 1.9 collective-permute-done.2
  26.1 3.1 collective-permute-start.3
  29.2 1.9 collective-permute-done.3
  31.7 19.2 %shard_map.204 = (bf16[512,1024]{1,0:T(8,128)(2,1)}, bf16[4,128,512]{2,1,0:T(8,128)(2,1)}, f32[512,512]{1,0:T(8,128)}, f32[1,512]{1,0:T(1,128)}, f32[512,1024]{1...) custom-call(s32[4]{0:T(128)} %refs_0_.5, ...), custom_call_target="tpu_custom_call" | custom-call | flops 6442450944 | bytes 8388608 | tf_op jit(solution)/shard_map/pallas_call | solution.py:81
  52.5 3.0 collective-permute-done.4
  56.2 2.0 collective-permute-start.5
  60.0 3.0 collective-permute-start.6
  68.7 3.4 %shard_map.209 = (f32[768,512]{1,0:T(8,128)}, f32[768,512]{1,0:T(8,128)S(1)}) custom-call(f32[512,512]{1,0:T(8,128)S(1)} %get-tuple-element.103.mine._, s32[1]{0:T(128)} %bitcast.12.bit, f32[1536,512]{1,0:T(8,128)S(1)} %copy-done, f32[1536,512]{1,0:T(8,128)} %collective-permute-done.10.received), custom_call_target="tpu_custom_call" | custom-call | flops 1 | bytes 1 | tf_op jit(solution)/shard_map/pallas_call | solution.py:620
  74.6 10.8 %shard_map.205 = (bf16[4,128,512]{2,1,0:T(8,128)(2,1)}, f32[4,3,512]{2,1,0:T(4,128)}, f32[4,16,512]{2,1,0:T(8,128)}, f32[4,16,512]{2,1,0:T(8,128)}, f32[256,1024...) custom-call(s32[4]{0:T(128)} %refs_0_.5, f32[4,1024]{1,0:T(4,128)} %copy-done.5, ...), custom_call_target="tpu_custom_call" | custom-call | flops 2147483648 | bytes 8388608 | tf_op jit(solution)/shard_map/pallas_call | solution.py:81
  86.1 2.1 collective-permute-done.9.received
  89.0 2.1 shard_map.208
  92.8 2.5 shard_map.210
  95.3 1.9 collective-permute-start.13
  97.2 2.8 collective-permute-start.12
  100.0 12.6 %collective-permute-done.12.received = f32[256,512]{1,0:T(8,128)S(1)} collective-permute-done((f32[256,512]{1,0:T(8,128)}, f32[256,512]{1,0:T(8,128)S(1)}, u32[]{:S(2)}, u32[]{:S(2)}) %collective-permute-start.12) | collective-permute-done | bytes 524320 | tf_op jit(solution)/shard_map/ppermute | solution.py:551
  113.4 2.1 shard_map.212
  115.5 2.1 shard_map.213
  117.7 2.2 shard_map.214
  119.9 3.4 %collective-permute-start.19 = (f32[128,1152]{1,0:T(8,128)}, f32[128,1152]{1,0:T(8,128)S(1)}, u32[]{:S(2)}, u32[]{:S(2)}) collective-permute-start(f32[128,1152]{1,0:T(8,128)} %get-tuple-element.127), channel_id=1, source_target_pairs={{0,2},{1,3},{2,0},{3,1},{4,6},{5,7},{6,4},{7,5},{8,24},{9,25},{10,... | collective-permute-start | bytes 1769480 | tf_op jit(solution)/shard_map/ppermute | solution.py:551
  126.4 9.0 %collective-permute-done.16.received = f32[128,512]{1,0:T(8,128)S(1)} collective-permute-done((f32[128,512]{1,0:T(8,128)}, f32[128,512]{1,0:T(8,128)S(1)}, u32[]{:S(2)}, u32[]{:S(2)}) %collective-permute-start.16) | collective-permute-done | bytes 262176 | tf_op jit(solution)/shard_map/ppermute | solution.py:551
  139.4 3.3 %collective-permute-start.23 = (f32[64,1152]{1,0:T(8,128)S(1)}, f32[64,1152]{1,0:T(8,128)S(1)}, u32[]{:S(2)}, u32[]{:S(2)}) collective-permute-start(f32[64,1152]{1,0:T(8,128)S(1)} %get-tuple-element.133), channel_id=1, source_target_pairs={{0,4},{1,5},{2,6},{3,7},{4,0},{5,1},{6,2},{7,3},{8,9},{9,8},{10,11... | collective-permute-start | bytes 884744 | tf_op jit(solution)/shard_map/ppermute | solution.py:551
  142.8 5.1 %collective-permute-done.20.received = f32[64,512]{1,0:T(8,128)S(1)} collective-permute-done((f32[64,512]{1,0:T(8,128)S(1)}, f32[64,512]{1,0:T(8,128)S(1)}, u32[]{:S(2)}, u32[]{:S(2)}) %collective-permute-start.20) | collective-permute-done | bytes 131104 | tf_op jit(solution)/shard_map/ppermute | solution.py:551
  150.0 2.5 collective-permute-done.22.received
  152.5 4.3 %collective-permute-done.23.received = f32[64,1152]{1,0:T(8,128)S(1)} collective-permute-done((f32[64,1152]{1,0:T(8,128)S(1)}, f32[64,1152]{1,0:T(8,128)S(1)}, u32[]{:S(2)}, u32[]{:S(2)}) %collective-permute-start.23) | collective-permute-done | bytes 294944 | tf_op jit(solution)/shard_map/ppermute | solution.py:551
  159.9 2.1 collective-permute-start.26
  161.9 16.1 %collective-permute-done.26.received = f32[32,1024]{1,0:T(8,128)S(1)} collective-permute-done((f32[32,1024]{1,0:T(8,128)S(1)}, f32[32,1024]{1,0:T(8,128)S(1)}, u32[]{:S(2)}, u32[]{:S(2)}) %collective-permute-start.26) | collective-permute-done | bytes 131104 | tf_op jit(solution)/shard_map/ppermute | solution.py:551
  181.6 3.8 %collective-permute-done.30.received = f32[16,1024]{1,0:T(8,128)S(1)} collective-permute-done((f32[16,1024]{1,0:T(8,128)S(1)}, f32[16,1024]{1,0:T(8,128)S(1)}, u32[]{:S(2)}, u32[]{:S(2)}) %collective-permute-start.30) | collective-permute-done | bytes 65568 | tf_op jit(solution)/shard_map/ppermute | solution.py:551
  185.5 15.1 %collective-permute-done.32.received = f32[256,512]{1,0:T(8,128)S(1)} collective-permute-done((f32[256,512]{1,0:T(8,128)S(1)}, f32[256,512]{1,0:T(8,128)S(1)}, u32[]{:S(2)}, u32[]{:S(2)}) %collective-permute-start.32) | collective-permute-done | bytes 524320 | tf_op jit(solution)/shard_map/ppermute | solution.py:551
  200.7 2.1 collective-permute-done.33.received
  207.2 3.8 %collective-permute-done.34.received = f32[16,1024]{1,0:T(8,128)S(1)} collective-permute-done((f32[16,1024]{1,0:T(8,128)S(1)}, f32[16,1024]{1,0:T(8,128)S(1)}, u32[]{:S(2)}, u32[]{:S(2)}) %collective-permute-start.34) | collective-permute-done | bytes 65568 | tf_op jit(solution)/shard_map/ppermute | solution.py:551
  211.1 8.2 %collective-permute-done.36.received = f32[512,512]{1,0:T(8,128)S(1)} collective-permute-done((f32[512,512]{1,0:T(8,128)S(1)}, f32[512,512]{1,0:T(8,128)S(1)}, u32[]{:S(2)}, u32[]{:S(2)}) %collective-permute-start.36) | collective-permute-done | bytes 1048608 | tf_op jit(solution)/shard_map/ppermute | solution.py:551
  220.8 14.3 %collective-permute-done.37.received = f32[768,512]{1,0:T(8,128)S(1)} collective-permute-done((f32[768,512]{1,0:T(8,128)S(1)}, f32[768,512]{1,0:T(8,128)S(1)}, u32[]{:S(2)}, u32[]{:S(2)}) %collective-permute-start.37) | collective-permute-done | bytes 1572896 | tf_op jit(solution)/shard_map/ppermute | solution.py:551
  235.4 27.3 %collective-permute-start.47 = (f32[1536,512]{1,0:T(8,128)S(1)}, f32[1536,512]{1,0:T(8,128)}, u32[]{:S(2)}, u32[]{:S(2)}) collective-permute-start(f32[1536,512]{1,0:T(8,128)S(1)} %shard_map.236._.mine_b), channel_id=1, source_target_pairs={{0,8},{1,9},{2,10},{3,11},{4,12},{5,13},{6,14},{7,15},{8,0},{9,1},... | collective-permute-start | bytes 9437192 | tf_op jit(solution)/shard_map/ppermute | solution.py:551
  263.1 3.7 %collective-permute-start.38 = (f32[32,1024]{1,0:T(8,128)S(1)}, f32[32,1024]{1,0:T(8,128)S(1)}, u32[]{:S(2)}, u32[]{:S(2)}) collective-permute-start(f32[32,1024]{1,0:T(8,128)S(1)} %shard_map.233._.mine), channel_id=1, source_target_pairs={{0,4},{1,5},{2,6},{3,7},{4,0},{5,1},{6,2},{7,3},{8,10},{9,11},{10,... | collective-permute-start | bytes 393224 | tf_op jit(solution)/shard_map/ppermute | solution.py:551
  266.8 2.9 collective-permute-done.38.received
  269.8 3.0 collective-permute-start.41
  272.8 3.0 collective-permute-start.40
  275.8 4.5 %collective-permute-done.40.received = f32[64,1024]{1,0:T(8,128)S(1)} collective-permute-done((f32[64,1024]{1,0:T(8,128)S(1)}, f32[64,1024]{1,0:T(8,128)S(1)}, u32[]{:S(2)}, u32[]{:S(2)}) %collective-permute-start.40) | collective-permute-done | bytes 262176 | tf_op jit(solution)/shard_map/ppermute | solution.py:551
  280.4 2.1 collective-permute-start.43
  283.9 7.8 %collective-permute-done.42.received = f32[128,1024]{1,0:T(8,128)S(1)} collective-permute-done((f32[128,1024]{1,0:T(8,128)S(1)}, f32[128,1024]{1,0:T(8,128)S(1)}, u32[]{:S(2)}, u32[]{:S(2)}) %collective-permute-start.42) | collective-permute-done | bytes 524320 | tf_op jit(solution)/shard_map/ppermute | solution.py:551
  295.8 4.5 %collective-permute-done.7.received = f32[4,3,512]{2,1,0:T(4,128)S(1)} collective-permute-done((f32[4,3,512]{2,1,0:T(4,128)S(1)}, f32[4,3,512]{2,1,0:T(4,128)S(1)}, u32[]{:S(2)}, u32[]{:S(2)}) %collective-permute-start.7) | collective-permute-done | bytes 24608 | tf_op jit(solution)/shard_map/ppermute | solution.py:812
  302.8 3.3 %shard_map.243 = (f32[512,1024]{1,0:T(8,128)}, f32[512,1024]{1,0:T(8,128)}, f32[32,128]{1,0:T(8,128)S(1)}) custom-call(f32[256,1152]{1,0:T(8,128)} %shard_map.242._.mine_d, f32[256,1024]{1,0:T(8,128)} %shard_map.241._.mine_c, f32[256,1024]{1,0:T(8,128)} %collective-permute-done.44.got_c, f32[256,1152]{1,0:T(8,128)} %shard_map.242._.mine_d, ...), custom_call_target="tpu_custom_call" | custom-call | flops 1 | bytes 1 | tf_op jit(solution)/shard_map/pallas_call | solution.py:736
  307.9 6.6 %shard_map.244 = (f32[2048,512]{1,0:T(8,128)}, f32[512,2048]{1,0:T(8,128)}, f32[1024,512]{1,0:T(8,128)}) custom-call(f32[256,1152]{1,0:T(8,128)} %shard_map.242._.mine_d, f32[1024,512]{1,0:T(8,128)} %shard_map.235._.mine_a, f32[1024,512]{1,0:T(8,128)} %collective-permute-done.46.got_a, f32[1536,512]{1,0:T(8,128)S(1)} %shard_map.236._.mine_b, ...), custom_call_target="tpu_custom_call" | custom-call | flops 1 | bytes 1 | tf_op jit(solution)/shard_map/pallas_call | solution.py:736
  (124 shorter events, 53.0 us)
Async XLA Ops:
  1.4 6.4 %collective-permute-start = (f32[4,3,512]{2,1,0:T(4,128)S(1)}, f32[4,3,512]{2,1,0:T(4,128)S(1)}, u32[]{:S(2)}, u32[]{:S(2)}) collective-permute-start(f32[4,3,512]{2,1,0:T(4,128)S(1)} %slice_convert_fusion), channel_id=1, source_target_pairs={{0,1},{1,2},{2,3},{3,4},{4,5},{5,6},{6,7},{8,9},{9,10},{10,11},{11... | collective-permute-start | bytes 73736 | tf_op jit(solution)/shard_map/ppermute | solution.py:757
  15.9 4.4 %collective-permute-start.1 = (f32[2,4,1024]{2,1,0:T(4,128)}, f32[2,4,1024]{2,1,0:T(4,128)S(1)}, u32[]{:S(2)}, u32[]{:S(2)}) collective-permute-start(f32[2,4,1024]{2,1,0:T(4,128)} %get-tuple-element.79), channel_id=1, source_target_pairs={{0,1},{1,0},{2,3},{3,2},{4,5},{5,4},{6,7},{7,6},{8,9},{9,8},{10,11... | collective-permute-start | bytes 98312 | tf_op jit(solution)/shard_map/ppermute | solution.py:490
  21.1 5.0 %collective-permute-start.2 = (f32[2,4,1024]{2,1,0:T(4,128)S(1)}, f32[2,4,1024]{2,1,0:T(4,128)S(1)}, u32[]{:S(2)}, u32[]{:S(2)}) collective-permute-start(f32[2,4,1024]{2,1,0:T(4,128)S(1)} %pad_maximum_fusion), channel_id=1, source_target_pairs={{0,2},{1,3},{2,0},{3,1},{4,6},{5,7},{6,4},{7,5},{8,10},{9,11},{10,... | collective-permute-start | bytes 98312 | tf_op jit(solution)/shard_map/ppermute | solution.py:490
  26.1 5.0 %collective-permute-start.3 = (f32[2,4,1024]{2,1,0:T(4,128)S(1)}, f32[2,4,1024]{2,1,0:T(4,128)S(1)}, u32[]{:S(2)}, u32[]{:S(2)}) collective-permute-start(f32[2,4,1024]{2,1,0:T(4,128)S(1)} %pad_maximum_fusion.1), channel_id=1, source_target_pairs={{0,4},{1,5},{2,6},{3,7},{4,0},{5,1},{6,2},{7,3},{8,12},{9,13},{10,... | collective-permute-start | bytes 98312 | tf_op jit(solution)/shard_map/ppermute | solution.py:490
  51.0 16.7 %collective-permute-start.10 = (f32[1536,512]{1,0:T(8,128)}, f32[1536,512]{1,0:T(8,128)}, u32[]{:S(2)}, u32[]{:S(2)}) collective-permute-start(f32[1536,512]{1,0:T(8,128)} %get-tuple-element.107), channel_id=1, source_target_pairs={{0,8},{1,9},{2,10},{3,11},{4,12},{5,13},{6,14},{7,15},{8,0},{9,1},... | collective-permute-start | bytes 9437192 | tf_op jit(solution)/shard_map/ppermute | solution.py:551
  51.0 13.8 %collective-permute-start.8 = (f32[1024,512]{1,0:T(8,128)}, f32[1024,512]{1,0:T(8,128)S(1)}, u32[]{:S(2)}, u32[]{:S(2)}) collective-permute-start(f32[1024,512]{1,0:T(8,128)} %get-tuple-element.102), channel_id=1, source_target_pairs={{0,8},{1,9},{2,10},{3,11},{4,12},{5,13},{6,14},{7,15},{8,0},{9,1},... | collective-permute-start | bytes 6291464 | tf_op jit(solution)/shard_map/ppermute | solution.py:551
  51.5 3.9 %collective-permute-start.4 = (f32[4,1024]{1,0:T(4,128)}, f32[4,1024]{1,0:T(4,128)S(1)}, u32[]{:S(2)}, u32[]{:S(2)}) collective-permute-start(f32[4,1024]{1,0:T(4,128)} %get-tuple-element.89), channel_id=1, source_target_pairs={{0,1},{1,0},{2,3},{3,2},{4,5},{5,4},{6,7},{7,6},{8,9},{9,8},{10,11... | collective-permute-start | bytes 49160 | tf_op jit(solution)/shard_map/ppermute | solution.py:490
  56.2 3.8 %collective-permute-start.5 = (f32[4,1024]{1,0:T(4,128)S(1)}, f32[4,1024]{1,0:T(4,128)S(1)}, u32[]{:S(2)}, u32[]{:S(2)}) collective-permute-start(f32[4,1024]{1,0:T(4,128)S(1)} %fusion.3), channel_id=1, source_target_pairs={{0,2},{1,3},{2,0},{3,1},{4,6},{5,7},{6,4},{7,5},{8,10},{9,11},{10,... | collective-permute-start | bytes 49160 | tf_op jit(solution)/shard_map/ppermute | solution.py:490
  60.0 4.7 %collective-permute-start.6 = (f32[4,1024]{1,0:T(4,128)S(1)}, f32[4,1024]{1,0:T(4,128)S(1)}, u32[]{:S(2)}, u32[]{:S(2)}) collective-permute-start(f32[4,1024]{1,0:T(4,128)S(1)} %fusion.6), channel_id=1, source_target_pairs={{0,4},{1,5},{2,6},{3,7},{4,0},{5,1},{6,2},{7,3},{8,12},{9,13},{10,... | collective-permute-start | bytes 49160 | tf_op jit(solution)/shard_map/ppermute | solution.py:490
  72.1 20.7 %collective-permute-start.11 = (f32[768,512]{1,0:T(8,128)}, f32[768,512]{1,0:T(8,128)}, u32[]{:S(2)}, u32[]{:S(2)}) collective-permute-start(f32[768,512]{1,0:T(8,128)} %get-tuple-element.109), channel_id=1, source_target_pairs={{0,1},{1,0},{2,3},{3,2},{4,5},{5,4},{6,7},{7,6},{8,24},{9,25},{10,... | collective-permute-start | bytes 4718600 | tf_op jit(solution)/shard_map/ppermute | solution.py:551
  73.0 15.1 %collective-permute-start.9 = (f32[512,512]{1,0:T(8,128)}, f32[512,512]{1,0:T(8,128)}, u32[]{:S(2)}, u32[]{:S(2)}) collective-permute-start(f32[512,512]{1,0:T(8,128)} %get-tuple-element.104), channel_id=1, source_target_pairs={{0,2},{1,3},{2,0},{3,1},{4,6},{5,7},{6,4},{7,5},{8,24},{9,25},{10,... | collective-permute-start | bytes 3145736 | tf_op jit(solution)/shard_map/ppermute | solution.py:551
  85.5 32.2 %collective-permute-start.15 = (f32[256,1152]{1,0:T(8,128)}, f32[256,1152]{1,0:T(8,128)}, u32[]{:S(2)}, u32[]{:S(2)}) collective-permute-start(f32[256,1152]{1,0:T(8,128)} %get-tuple-element.119), channel_id=1, source_target_pairs={{0,8},{1,9},{2,10},{3,11},{4,12},{5,13},{6,14},{7,15},{8,0},{9,1},... | collective-permute-start | bytes 3538952 | tf_op jit(solution)/shard_map/ppermute | solution.py:551
  85.6 30.0 %collective-permute-start.14 = (f32[256,1024]{1,0:T(8,128)}, f32[256,1024]{1,0:T(8,128)}, u32[]{:S(2)}, u32[]{:S(2)}) collective-permute-start(f32[256,1024]{1,0:T(8,128)} %get-tuple-element.116), channel_id=1, source_target_pairs={{0,8},{1,9},{2,10},{3,11},{4,12},{5,13},{6,14},{7,15},{8,0},{9,1},... | collective-permute-start | bytes 3145736 | tf_op jit(solution)/shard_map/ppermute | solution.py:551
  95.3 18.1 %collective-permute-start.13 = (f32[384,512]{1,0:T(8,128)}, f32[384,512]{1,0:T(8,128)}, u32[]{:S(2)}, u32[]{:S(2)}) collective-permute-start(f32[384,512]{1,0:T(8,128)} %get-tuple-element.113), channel_id=1, source_target_pairs={{0,2},{1,3},{2,0},{3,1},{4,6},{5,7},{6,4},{7,5},{8,9},{9,8},{10,11... | collective-permute-start | bytes 2359304 | tf_op jit(solution)/shard_map/ppermute | solution.py:551
  97.2 15.4 %collective-permute-start.12 = (f32[256,512]{1,0:T(8,128)}, f32[256,512]{1,0:T(8,128)S(1)}, u32[]{:S(2)}, u32[]{:S(2)}) collective-permute-start(f32[256,512]{1,0:T(8,128)} %get-tuple-element.111), channel_id=1, source_target_pairs={{0,4},{1,5},{2,6},{3,7},{4,0},{5,1},{6,2},{7,3},{8,9},{9,8},{10,11... | collective-permute-start | bytes 1572872 | tf_op jit(solution)/shard_map/ppermute | solution.py:551
  119.9 19.5 %collective-permute-start.19 = (f32[128,1152]{1,0:T(8,128)}, f32[128,1152]{1,0:T(8,128)S(1)}, u32[]{:S(2)}, u32[]{:S(2)}) collective-permute-start(f32[128,1152]{1,0:T(8,128)} %get-tuple-element.127), channel_id=1, source_target_pairs={{0,2},{1,3},{2,0},{3,1},{4,6},{5,7},{6,4},{7,5},{8,24},{9,25},{10,... | collective-permute-start | bytes 1769480 | tf_op jit(solution)/shard_map/ppermute | solution.py:551
  123.3 16.0 %collective-permute-start.18 = (f32[128,1024]{1,0:T(8,128)}, f32[128,1024]{1,0:T(8,128)S(1)}, u32[]{:S(2)}, u32[]{:S(2)}) collective-permute-start(f32[128,1024]{1,0:T(8,128)} %get-tuple-element.125), channel_id=1, source_target_pairs={{0,1},{1,0},{2,3},{3,2},{4,5},{5,4},{6,7},{7,6},{8,24},{9,25},{10,... | collective-permute-start | bytes 1572872 | tf_op jit(solution)/shard_map/ppermute | solution.py:551
  123.9 13.2 %collective-permute-start.17 = (f32[192,512]{1,0:T(8,128)}, f32[192,512]{1,0:T(8,128)S(1)}, u32[]{:S(2)}, u32[]{:S(2)}) collective-permute-start(f32[192,512]{1,0:T(8,128)} %get-tuple-element.123), channel_id=1, source_target_pairs={{0,4},{1,5},{2,6},{3,7},{4,0},{5,1},{6,2},{7,3},{8,10},{9,11},{10,... | collective-permute-start | bytes 1179656 | tf_op jit(solution)/shard_map/ppermute | solution.py:551
  125.0 10.5 %collective-permute-start.16 = (f32[128,512]{1,0:T(8,128)}, f32[128,512]{1,0:T(8,128)S(1)}, u32[]{:S(2)}, u32[]{:S(2)}) collective-permute-start(f32[128,512]{1,0:T(8,128)} %get-tuple-element.121), channel_id=1, source_target_pairs={{0,1},{1,0},{2,3},{3,2},{4,5},{5,4},{6,7},{7,6},{8,10},{9,11},{10,... | collective-permute-start | bytes 786440 | tf_op jit(solution)/shard_map/ppermute | solution.py:551
  137.2 10.7 %collective-permute-start.21 = (f32[96,512]{1,0:T(8,128)S(1)}, f32[96,512]{1,0:T(8,128)S(1)}, u32[]{:S(2)}, u32[]{:S(2)}) collective-permute-start(f32[96,512]{1,0:T(8,128)S(1)} %get-tuple-element.130), channel_id=1, source_target_pairs={{0,16},{1,17},{2,18},{3,19},{4,20},{5,21},{6,22},{7,23},{8,12},{9,... | collective-permute-start | bytes 589832 | tf_op jit(solution)/shard_map/ppermute | solution.py:551
  138.8 9.1 %collective-permute-start.20 = (f32[64,512]{1,0:T(8,128)S(1)}, f32[64,512]{1,0:T(8,128)S(1)}, u32[]{:S(2)}, u32[]{:S(2)}) collective-permute-start(f32[64,512]{1,0:T(8,128)S(1)} %get-tuple-element.129), channel_id=1, source_target_pairs={{0,16},{1,17},{2,18},{3,19},{4,20},{5,21},{6,22},{7,23},{8,12},{9,... | collective-permute-start | bytes 393224 | tf_op jit(solution)/shard_map/ppermute | solution.py:551
  139.4 17.4 %collective-permute-start.23 = (f32[64,1152]{1,0:T(8,128)S(1)}, f32[64,1152]{1,0:T(8,128)S(1)}, u32[]{:S(2)}, u32[]{:S(2)}) collective-permute-start(f32[64,1152]{1,0:T(8,128)S(1)} %get-tuple-element.133), channel_id=1, source_target_pairs={{0,4},{1,5},{2,6},{3,7},{4,0},{5,1},{6,2},{7,3},{8,9},{9,8},{10,11... | collective-permute-start | bytes 884744 | tf_op jit(solution)/shard_map/ppermute | solution.py:551
  142.8 9.7 %collective-permute-start.22 = (f32[64,1024]{1,0:T(8,128)S(1)}, f32[64,1024]{1,0:T(8,128)S(1)}, u32[]{:S(2)}, u32[]{:S(2)}) collective-permute-start(f32[64,1024]{1,0:T(8,128)S(1)} %get-tuple-element.131), channel_id=1, source_target_pairs={{0,2},{1,3},{2,0},{3,1},{4,6},{5,7},{6,4},{7,5},{8,9},{9,8},{10,11... | collective-permute-start | bytes 786440 | tf_op jit(solution)/shard_map/ppermute | solution.py:551
  147.9 8.9 %collective-permute-start.25 = (f32[96,512]{1,0:T(8,128)S(1)}, f32[96,512]{1,0:T(8,128)S(1)}, u32[]{:S(2)}, u32[]{:S(2)}) collective-permute-start(f32[96,512]{1,0:T(8,128)S(1)} %shard_map.220._.mine), channel_id=1, source_target_pairs={{0,16},{1,17},{2,18},{3,19},{4,20},{5,21},{6,22},{7,23},{8,12},{9,... | collective-permute-start | bytes 589832 | tf_op jit(solution)/shard_map/ppermute | solution.py:551
  149.5 7.3 %collective-permute-start.24 = (f32[64,512]{1,0:T(8,128)S(1)}, f32[64,512]{1,0:T(8,128)S(1)}, u32[]{:S(2)}, u32[]{:S(2)}) collective-permute-start(f32[64,512]{1,0:T(8,128)S(1)} %shard_map.219._.mine), channel_id=1, source_target_pairs={{0,16},{1,17},{2,18},{3,19},{4,20},{5,21},{6,22},{7,23},{8,12},{9,... | collective-permute-start | bytes 393224 | tf_op jit(solution)/shard_map/ppermute | solution.py:551
  156.9 21.2 %collective-permute-start.29 = (f32[192,512]{1,0:T(8,128)S(1)}, f32[192,512]{1,0:T(8,128)S(1)}, u32[]{:S(2)}, u32[]{:S(2)}) collective-permute-start(f32[192,512]{1,0:T(8,128)S(1)} %shard_map.224._.mine), channel_id=1, source_target_pairs={{0,4},{1,5},{2,6},{3,7},{4,0},{5,1},{6,2},{7,3},{8,10},{9,11},{10,... | collective-permute-start | bytes 1179656 | tf_op jit(solution)/shard_map/ppermute | solution.py:551
  157.9 20.2 %collective-permute-start.28 = (f32[128,512]{1,0:T(8,128)S(1)}, f32[128,512]{1,0:T(8,128)S(1)}, u32[]{:S(2)}, u32[]{:S(2)}) collective-permute-start(f32[128,512]{1,0:T(8,128)S(1)} %shard_map.223._.mine), channel_id=1, source_target_pairs={{0,1},{1,0},{2,3},{3,2},{4,5},{5,4},{6,7},{7,6},{8,10},{9,11},{10,... | collective-permute-start | bytes 786440 | tf_op jit(solution)/shard_map/ppermute | solution.py:551
  158.5 19.6 %collective-permute-start.27 = (f32[32,1152]{1,0:T(8,128)S(1)}, f32[32,1152]{1,0:T(8,128)S(1)}, u32[]{:S(2)}, u32[]{:S(2)}) collective-permute-start(f32[32,1152]{1,0:T(8,128)S(1)} %get-tuple-element.137), channel_id=1, source_target_pairs={{0,1},{1,0},{2,3},{3,2},{4,5},{5,4},{6,7},{7,6},{8,10},{9,11},{10,... | collective-permute-start | bytes 442376 | tf_op jit(solution)/shard_map/ppermute | solution.py:551
  159.9 18.1 %collective-permute-start.26 = (f32[32,1024]{1,0:T(8,128)S(1)}, f32[32,1024]{1,0:T(8,128)S(1)}, u32[]{:S(2)}, u32[]{:S(2)}) collective-permute-start(f32[32,1024]{1,0:T(8,128)S(1)} %get-tuple-element.135), channel_id=1, source_target_pairs={{0,4},{1,5},{2,6},{3,7},{4,0},{5,1},{6,2},{7,3},{8,10},{9,11},{10,... | collective-permute-start | bytes 393224 | tf_op jit(solution)/shard_map/ppermute | solution.py:551
  178.2 24.6 %collective-permute-start.33 = (f32[384,512]{1,0:T(8,128)S(1)}, f32[384,512]{1,0:T(8,128)S(1)}, u32[]{:S(2)}, u32[]{:S(2)}) collective-permute-start(f32[384,512]{1,0:T(8,128)S(1)} %shard_map.228._.mine), channel_id=1, source_target_pairs={{0,2},{1,3},{2,0},{3,1},{4,6},{5,7},{6,4},{7,5},{8,9},{9,8},{10,11... | collective-permute-start | bytes 2359304 | tf_op jit(solution)/shard_map/ppermute | solution.py:551
  178.3 22.3 %collective-permute-start.32 = (f32[256,512]{1,0:T(8,128)S(1)}, f32[256,512]{1,0:T(8,128)S(1)}, u32[]{:S(2)}, u32[]{:S(2)}) collective-permute-start(f32[256,512]{1,0:T(8,128)S(1)} %shard_map.227._.mine), channel_id=1, source_target_pairs={{0,4},{1,5},{2,6},{3,7},{4,0},{5,1},{6,2},{7,3},{8,9},{9,8},{10,11... | collective-permute-start | bytes 1572872 | tf_op jit(solution)/shard_map/ppermute | solution.py:551
  179.6 5.9 %collective-permute-start.31 = (f32[16,1152]{1,0:T(8,128)S(1)}, f32[16,1152]{1,0:T(8,128)S(1)}, u32[]{:S(2)}, u32[]{:S(2)}) collective-permute-start(f32[16,1152]{1,0:T(8,128)S(1)} %get-tuple-element.140), channel_id=1, source_target_pairs={{0,16},{1,17},{2,18},{3,19},{4,20},{5,21},{6,22},{7,23},{8,12},{9,... | collective-permute-start | bytes 221192 | tf_op jit(solution)/shard_map/ppermute | solution.py:551
  181.2 4.3 %collective-permute-start.30 = (f32[16,1024]{1,0:T(8,128)S(1)}, f32[16,1024]{1,0:T(8,128)S(1)}, u32[]{:S(2)}, u32[]{:S(2)}) collective-permute-start(f32[16,1024]{1,0:T(8,128)S(1)} %get-tuple-element.139), channel_id=1, source_target_pairs={{0,16},{1,17},{2,18},{3,19},{4,20},{5,21},{6,22},{7,23},{8,12},{9,... | collective-permute-start | bytes 196616 | tf_op jit(solution)/shard_map/ppermute | solution.py:551
  202.9 32.1 %collective-permute-start.37 = (f32[768,512]{1,0:T(8,128)S(1)}, f32[768,512]{1,0:T(8,128)S(1)}, u32[]{:S(2)}, u32[]{:S(2)}) collective-permute-start(f32[768,512]{1,0:T(8,128)S(1)} %shard_map.232._.mine), channel_id=1, source_target_pairs={{0,1},{1,0},{2,3},{3,2},{4,5},{5,4},{6,7},{7,6},{8,24},{9,25},{10,... | collective-permute-start | bytes 4718600 | tf_op jit(solution)/shard_map/ppermute | solution.py:551
  203.5 15.8 %collective-permute-start.36 = (f32[512,512]{1,0:T(8,128)S(1)}, f32[512,512]{1,0:T(8,128)S(1)}, u32[]{:S(2)}, u32[]{:S(2)}) collective-permute-start(f32[512,512]{1,0:T(8,128)S(1)} %shard_map.231._.mine), channel_id=1, source_target_pairs={{0,2},{1,3},{2,0},{3,1},{4,6},{5,7},{6,4},{7,5},{8,24},{9,25},{10,... | collective-permute-start | bytes 3145736 | tf_op jit(solution)/shard_map/ppermute | solution.py:551
  205.2 5.8 %collective-permute-start.35 = (f32[16,1152]{1,0:T(8,128)S(1)}, f32[16,1152]{1,0:T(8,128)S(1)}, u32[]{:S(2)}, u32[]{:S(2)}) collective-permute-start(f32[16,1152]{1,0:T(8,128)S(1)} %shard_map.230._.mine), channel_id=1, source_target_pairs={{0,16},{1,17},{2,18},{3,19},{4,20},{5,21},{6,22},{7,23},{8,12},{9,... | collective-permute-start | bytes 221192 | tf_op jit(solution)/shard_map/ppermute | solution.py:551
  206.8 4.3 %collective-permute-start.34 = (f32[16,1024]{1,0:T(8,128)S(1)}, f32[16,1024]{1,0:T(8,128)S(1)}, u32[]{:S(2)}, u32[]{:S(2)}) collective-permute-start(f32[16,1024]{1,0:T(8,128)S(1)} %shard_map.229._.mine), channel_id=1, source_target_pairs={{0,16},{1,17},{2,18},{3,19},{4,20},{5,21},{6,22},{7,23},{8,12},{9,... | collective-permute-start | bytes 196616 | tf_op jit(solution)/shard_map/ppermute | solution.py:551
  235.4 72.5 %collective-permute-start.47 = (f32[1536,512]{1,0:T(8,128)S(1)}, f32[1536,512]{1,0:T(8,128)}, u32[]{:S(2)}, u32[]{:S(2)}) collective-permute-start(f32[1536,512]{1,0:T(8,128)S(1)} %shard_map.236._.mine_b), channel_id=1, source_target_pairs={{0,8},{1,9},{2,10},{3,11},{4,12},{5,13},{6,14},{7,15},{8,0},{9,1},... | collective-permute-start | bytes 9437192 | tf_op jit(solution)/shard_map/ppermute | solution.py:551
  262.6 7.1 %collective-permute-start.39 = (f32[32,1152]{1,0:T(8,128)S(1)}, f32[32,1152]{1,0:T(8,128)S(1)}, u32[]{:S(2)}, u32[]{:S(2)}) collective-permute-start(f32[32,1152]{1,0:T(8,128)S(1)} %shard_map.234._.mine), channel_id=1, source_target_pairs={{0,1},{1,0},{2,3},{3,2},{4,5},{5,4},{6,7},{7,6},{8,10},{9,11},{10,... | collective-permute-start | bytes 442376 | tf_op jit(solution)/shard_map/ppermute | solution.py:551
  263.1 6.7 %collective-permute-start.38 = (f32[32,1024]{1,0:T(8,128)S(1)}, f32[32,1024]{1,0:T(8,128)S(1)}, u32[]{:S(2)}, u32[]{:S(2)}) collective-permute-start(f32[32,1024]{1,0:T(8,128)S(1)} %shard_map.233._.mine), channel_id=1, source_target_pairs={{0,4},{1,5},{2,6},{3,7},{4,0},{5,1},{6,2},{7,3},{8,10},{9,11},{10,... | collective-permute-start | bytes 393224 | tf_op jit(solution)/shard_map/ppermute | solution.py:551
  269.8 10.6 %collective-permute-start.41 = (f32[64,1152]{1,0:T(8,128)S(1)}, f32[64,1152]{1,0:T(8,128)S(1)}, u32[]{:S(2)}, u32[]{:S(2)}) collective-permute-start(f32[64,1152]{1,0:T(8,128)S(1)} %shard_map.238._.mine), channel_id=1, source_target_pairs={{0,4},{1,5},{2,6},{3,7},{4,0},{5,1},{6,2},{7,3},{8,9},{9,8},{10,11... | collective-permute-start | bytes 884744 | tf_op jit(solution)/shard_map/ppermute | solution.py:551
  272.8 7.5 %collective-permute-start.40 = (f32[64,1024]{1,0:T(8,128)S(1)}, f32[64,1024]{1,0:T(8,128)S(1)}, u32[]{:S(2)}, u32[]{:S(2)}) collective-permute-start(f32[64,1024]{1,0:T(8,128)S(1)} %shard_map.237._.mine), channel_id=1, source_target_pairs={{0,2},{1,3},{2,0},{3,1},{4,6},{5,7},{6,4},{7,5},{8,9},{9,8},{10,11... | collective-permute-start | bytes 786440 | tf_op jit(solution)/shard_map/ppermute | solution.py:551
  280.4 12.3 %collective-permute-start.43 = (f32[128,1152]{1,0:T(8,128)S(1)}, f32[128,1152]{1,0:T(8,128)S(1)}, u32[]{:S(2)}, u32[]{:S(2)}) collective-permute-start(f32[128,1152]{1,0:T(8,128)S(1)} %shard_map.240._.mine), channel_id=1, source_target_pairs={{0,2},{1,3},{2,0},{3,1},{4,6},{5,7},{6,4},{7,5},{8,24},{9,25},{10,... | collective-permute-start | bytes 1769480 | tf_op jit(solution)/shard_map/ppermute | solution.py:551
  282.5 9.2 %collective-permute-start.42 = (f32[128,1024]{1,0:T(8,128)S(1)}, f32[128,1024]{1,0:T(8,128)S(1)}, u32[]{:S(2)}, u32[]{:S(2)}) collective-permute-start(f32[128,1024]{1,0:T(8,128)S(1)} %shard_map.239._.mine), channel_id=1, source_target_pairs={{0,1},{1,0},{2,3},{3,2},{4,5},{5,4},{6,7},{7,6},{8,24},{9,25},{10,... | collective-permute-start | bytes 1572872 | tf_op jit(solution)/shard_map/ppermute | solution.py:551
  283.9 24.0 %collective-permute-start.46 = (f32[1024,512]{1,0:T(8,128)}, f32[1024,512]{1,0:T(8,128)}, u32[]{:S(2)}, u32[]{:S(2)}) collective-permute-start(f32[1024,512]{1,0:T(8,128)} %shard_map.235._.mine_a), channel_id=1, source_target_pairs={{0,8},{1,9},{2,10},{3,11},{4,12},{5,13},{6,14},{7,15},{8,0},{9,1},... | collective-permute-start | bytes 6291464 | tf_op jit(solution)/shard_map/ppermute | solution.py:551
  294.0 8.8 %collective-permute-start.45 = (f32[256,1152]{1,0:T(8,128)}, f32[256,1152]{1,0:T(8,128)}, u32[]{:S(2)}, u32[]{:S(2)}) collective-permute-start(f32[256,1152]{1,0:T(8,128)} %shard_map.242._.mine_d), channel_id=1, source_target_pairs={{0,8},{1,9},{2,10},{3,11},{4,12},{5,13},{6,14},{7,15},{8,0},{9,1},... | collective-permute-start | bytes 3538952 | tf_op jit(solution)/shard_map/ppermute | solution.py:551
  294.0 8.8 %collective-permute-start.44 = (f32[256,1024]{1,0:T(8,128)}, f32[256,1024]{1,0:T(8,128)}, u32[]{:S(2)}, u32[]{:S(2)}) collective-permute-start(f32[256,1024]{1,0:T(8,128)} %shard_map.241._.mine_c), channel_id=1, source_target_pairs={{0,8},{1,9},{2,10},{3,11},{4,12},{5,13},{6,14},{7,15},{8,0},{9,1},... | collective-permute-start | bytes 3145736 | tf_op jit(solution)/shard_map/ppermute | solution.py:551
  294.5 5.8 %collective-permute-start.7 = (f32[4,3,512]{2,1,0:T(4,128)S(1)}, f32[4,3,512]{2,1,0:T(4,128)S(1)}, u32[]{:S(2)}, u32[]{:S(2)}) collective-permute-start(f32[4,3,512]{2,1,0:T(4,128)S(1)} %copy-done.9), channel_id=1, source_target_pairs={{1,0},{2,1},{3,2},{4,3},{5,4},{6,5},{7,6},{9,8},{10,9},{11,10},{12... | collective-permute-start | bytes 73736 | tf_op jit(solution)/shard_map/ppermute | solution.py:812
  (10 other events, 58.8 us)

commit v3 on v2

--- a/solution.py
+++ b/solution.py
@@ -11,13 +11,14 @@
 EPS = 1e-06
 VMEM = pl.BlockSpec(memory_space=pltpu.VMEM)
 SMEM = pl.BlockSpec(memory_space=pltpu.SMEM)
-KINDS = "TSST"
+ORDERS = ("xyab", "abyx", "ayxb", "xbay")
 CHUNKS = 4
-EARLY = (0, 1, 0, 1)
+HOLD = 3
 SUB = 8
 
 
 HBM = pl.BlockSpec(memory_space=pltpu.HBM)
+ANY = pl.BlockSpec(memory_space=pl.ANY)
 
 
 class Staged:
@@ -66,7 +67,7 @@
             copy.wait()
 
 
-def staged_call(kernel, scalars, ins, outs, extra_outs, scratch, flops, copies, chunks=None, reverse=False):
+def staged_call(kernel, scalars, ins, outs, extra_outs, scratch, flops, copies, room, chunks=None):
     n_s, n_i, n_o, n_e = len(scalars), len(ins), len(outs), len(extra_outs)
 
     def body(*refs):
@@ -87,7 +88,7 @@
         + [pltpu.VMEM(shape, kind) for shape, kind in outs]
         + [pltpu.VMEM(shape, kind) for shape, kind in scratch]
         + [pltpu.SemaphoreType.DMA((copies,))],
-        compiler_params=pltpu.CompilerParams(vmem_limit_bytes=56 << 20),
+        compiler_params=pltpu.CompilerParams(vmem_limit_bytes=room << 20),
         cost_estimate=pl.CostEstimate(flops=flops, bytes_accessed=8 << 20, transcendentals=0),
     )(*scalars, *ins)
     return results
@@ -255,7 +256,7 @@
     (first_len,) = scalars
     carried, subk, subs, keep, drive, cand, gate, x, w_out, gain_two, w_up, w_down, up = ins
     blend, output, grad_middle_out, grad_gain_two, grad_state, subb, totals = outs
-    mine_a, other_a, mine_b, other_b = extra
+    mine, other, mine_out, other_out = extra
     before, low, second_low, tail, second_grad, middle_ref, for_even, for_odd, out_even, out_odd = scratch
     count, width = x.shape
     hidden, ff = keep.shape[1], w_up.shape[1]
@@ -314,10 +315,10 @@
         second_grad[...] += dot_rt(up_low, w_up[:, at])
         return carry
 
-    for k, (mine, other) in enumerate(((mine_a, other_a), (mine_b, other_b))):
+    for k in range(2):
         lax.fori_loop(k * half, (k + 1) * half, part, 0)
-        at, to = pl.ds(k * half * block, half * block), pl.ds(0, half * block)
-        give_pair(stage, even, [(for_even.at[at], for_odd.at[at], mine.at[to], other.at[to])])
+        at = pl.ds(k * half * block, half * block)
+        give_pair(stage, even, [(for_even.at[at], for_odd.at[at], mine.at[at], other.at[at])])
 
     middle = middle_ref[...]
     scale = rms(middle)
@@ -348,8 +349,7 @@
     half_h = hidden // 2
     out_even[...] = dot_lt(low[:, :half_h], middle_low)
     out_odd[...] = dot_lt(low[:, half_h:], middle_low)
-    to = pl.ds(half * block, half_h)
-    give_pair(stage, even, [(out_even, out_odd, mine_b.at[to], other_b.at[to])])
+    give_pair(stage, even, [(out_even, out_odd, mine_out, other_out)])
     result = (middle_ref[...] + tail[...]).astype(BF16)
     output[...] = dot_lt(segment_order(count), result).astype(BF16).reshape(output.shape)
     stage.done(1)
@@ -520,24 +520,27 @@
 
 def carry_backward(passed, levels):
     after_b, after_k = jnp.zeros_like(passed), jnp.ones_like(passed)
+    seen = []
     for bit, (keep, other_k) in zip(bits_of("seq"), levels):
         other_b = swapped(passed, "seq", bit)
         late = upper("seq", bit)
         after_b = jnp.where(late, after_b, after_b + after_k * other_b)
         after_k = jnp.where(late, after_k, after_k * other_k)
         passed = jnp.where(late, other_b + other_k * passed, passed + keep * other_b)
-    return after_b
+        seen.append(passed)
+    return after_b, seen
 
 
 BOTH = ("row", "seq")
 
 
-def axis_steps(kind):
-    row = [("row", bit) for bit in bits_of("row")[1:]]
+def axis_steps(order):
     seq = [("seq", bit) for bit in bits_of("seq")]
-    near, far = seq[:1], seq[1:]
-    even = {"P": near + row + far, "S": near + far + row, "T": far + near + row}[kind]
-    return list(zip(even, row + near + far))
+    parts = {"x": seq[:1], "y": [("row", bit) for bit in bits_of("row")[1:]], "a": seq[1:2], "b": seq[2:]}
+    swap = {"x": "y", "y": "x", "a": "a", "b": "b"}
+    even = sum((parts[letter] for letter in order), [])
+    odd = sum((parts[swap[letter]] for letter in order), [])
+    return list(zip(even, odd))
 
 
 def exchanged(array, even, odd):
@@ -551,9 +554,9 @@
     return lax.ppermute(array, BOTH, pairs)
 
 
-def place_bit(even, odd):
-    one, two = [lax.axis_index(axis) // bit % 2 for axis, bit in (even, odd)]
-    return jnp.where(lax.axis_index("row") % 2 == 0, one, two).astype(jnp.int32).reshape(1)
+def place_bit(step):
+    even, odd = [lax.axis_index(axis) // bit % 2 for axis, bit in step]
+    return jnp.where(lax.axis_index("row") % 2 == 0, even, odd)
 
 
 def by_rows(total, body):
@@ -569,30 +572,30 @@
     lax.fori_loop(0, total // chunk, turn, 0)
 
 
-def aligned(at, half):
-    return pl.multiple_of(at, SUB) if half % SUB == 0 else at
-
-
-def split_kernel(_, bit, mine, received, send, keep):
-    half = send.shape[0]
+def tiled(first, rows):
+    return pl.multiple_of(first, SUB) if rows % SUB == 0 else first
+
+
+def split_rows(step, mine, received, send, keep):
+    half, bit = send.shape[0], place_bit(step)
     if half % SUB:
         first = mine[:half, :] + received[:half, :]
         second = mine[half:, :] + received[half:, :]
-        lower = jnp.broadcast_to(bit[0] == 0, first.shape)
+        lower = jnp.broadcast_to(bit == 0, first.shape)
         send[...] = jnp.where(lower, second, first)
         keep[...] = jnp.where(lower, first, second)
         return
 
     def body(i, chunk):
         to = pl.ds(i, chunk)
-        for out, begin in ((send, (1 - bit[0]) * half), (keep, bit[0] * half)):
+        for out, begin in ((send, (1 - bit) * half), (keep, bit * half)):
             at = pl.ds(pl.multiple_of(i + begin, SUB), chunk)
             out[to, :] = mine[at, :] + received[at, :]
 
     by_rows(half, body)
 
 
-def add_kernel(_, mine, received, out):
+def add_rows(_, mine, received, out):
     def body(i, chunk):
         at = pl.ds(i, chunk)
         out[at, :] = mine[at, :] + received[at, :]
@@ -600,149 +603,147 @@
     by_rows(mine.shape[0], body)
 
 
-def join_kernel(_, bit, mine, received, out):
-    half = mine.shape[0]
+def join_rows(step, mine, received, out):
+    half, bit = mine.shape[0], place_bit(step)
     if half % SUB:
-        lower = jnp.broadcast_to(bit[0] == 0, mine.shape)
+        lower = jnp.broadcast_to(bit == 0, mine.shape)
         out[:half, :] = jnp.where(lower, mine[...], received[...])
         out[half:, :] = jnp.where(lower, received[...], mine[...])
         return
 
     def body(i, chunk):
         at = pl.ds(i, chunk)
-        for source, begin in ((mine, bit[0] * half), (received, (1 - bit[0]) * half)):
+        for source, begin in ((mine, bit * half), (received, (1 - bit) * half)):
             out[pl.ds(pl.multiple_of(i + begin, SUB), chunk), :] = source[at, :]
 
     by_rows(half, body)
 
 
-def piece_call(kernel, specs, outs, *operands):
+CORE = (("row", 1),) * 2
+
+
+class Summed:
+    def __init__(self, mine, other, order):
+        self.steps = axis_steps(order)
+        self.mine, self.stage = mine, 1
+        self.received = exchanged(other, *CORE)
+
+    def work(self):
+        count = len(self.steps)
+        rows, width = self.mine.shape
+        if self.stage <= count:
+            return split_rows, self.steps[self.stage - 1], [(rows // 2, width)] * 2
+        if self.stage == count + 1:
+            return add_rows, None, [(rows, width)]
+        return join_rows, self.steps[2 * count + 1 - self.stage], [(2 * rows, width)]
+
+    def give(self, outs):
+        count = len(self.steps)
+        self.mine = outs[-1]
+        step = self.steps[self.stage - 1 if self.stage <= count else 2 * count - self.stage]
+        self.received = exchanged(outs[0], *step)
+        self.stage += 1
+
+    def busy(self):
+        return self.stage <= 2 * len(self.steps)
+
+    def across(self):
+        self.others = exchanged(self.mine, *CORE), exchanged(self.received, *CORE)
+
+
+def wave(tokens, sums, through=()):
+    works = [one.work() for one in sums]
+
+    def kernel(*refs):
+        refs = refs[len(tokens) + len(through) :]
+        ins, outs = refs[: 2 * len(sums)], list(refs[2 * len(sums) + len(through) :])
+        for i, (rows, step, shapes) in enumerate(works):
+            mine_outs = [outs.pop(0) for _ in shapes]
+            rows(step, ins[2 * i], ins[2 * i + 1], *mine_outs)
+
+    shapes = [shape for _, _, shapes in works for shape in shapes]
+    outs = list(pl.pallas_call(
+        kernel,
+        in_specs=[ANY] * (len(tokens) + len(through)) + [VMEM] * (2 * len(sums)),
+        out_specs=(ANY,) * len(through) + (VMEM,) * len(shapes),
+        out_shape=shaped(*[(array.shape, F32) for array in through], *[(shape, F32) for shape in shapes]),
+        input_output_aliases={len(tokens) + i: i for i in range(len(through))},
+        compiler_params=pltpu.CompilerParams(vmem_limit_bytes=24 << 20),
+        cost_estimate=pl.CostEstimate(flops=1, bytes_accessed=1, transcendentals=0),
+    )(*tokens, *through, *[array for one in sums for array in (one.mine, one.received)]))
+    passed = [outs.pop(0) for _ in through]
+    first = outs[0]
+    for one, (_, _, shapes) in zip(sums, works):
+        one.give([outs.pop(0) for _ in shapes])
+    return first, passed
+
+
+def finish_kernel(steps, routes, total, _, *refs):
+    count = len(steps)
+    arrays, outs = refs[: 4 * count], refs[4 * count : 4 * count + total]
+    buffers, sems = refs[4 * count + total : -1], refs[-1]
+    even = lax.axis_index("row") % 2 == 0
+    base, plans = 0, []
+    for k, step in enumerate(steps):
+        own = arrays[4 * k : 4 * k + 4]
+        rows = own[0].shape[0]
+        for parity in range(2):
+            axis, bit = step[parity]
+            place = lax.axis_index(axis) // bit % 2
+            longest = 0
+            for is_own in (True, False):
+                for upper_half in range(2):
+                    pair = own[:2] if is_own else own[2:]
+                    plan = []
+                    for half in range(2):
+                        source = pair[half ^ upper_half]
+                        buffer = buffers[k].at[parity, half]
+                        for at, columns, output, to in routes(k, parity, half * rows, rows):
+                            plan.append((source.at[at, columns], buffer.at[at, columns], outs[output].at[to]))
+                    mine = even if is_own == (parity == 0) else jnp.logical_not(even)
+                    plans.append((jnp.logical_and(mine, place == upper_half), plan, base))
+                    longest = max(longest, len(plan))
+            base += longest
+    for condition, plan, first in plans:
+
+        @pl.when(condition)
+        def _():
+            for i, (source, buffer, _) in enumerate(plan):
+                pltpu.make_async_copy(source, buffer, sems.at[0, first + i]).start()
+
+    for condition, plan, first in plans:
+
+        @pl.when(condition)
+        def _():
+            for i, (source, buffer, target) in enumerate(plan):
+                pltpu.make_async_copy(source, buffer, sems.at[0, first + i]).wait()
+                pltpu.make_async_copy(buffer, target, sems.at[1, first + i]).start()
+
+    for condition, plan, first in plans:
+
+        @pl.when(condition)
+        def _():
+            for i, (source, buffer, target) in enumerate(plan):
+                pltpu.make_async_copy(buffer, target, sems.at[1, first + i]).wait()
+
+
+def finish_call(routes, token, sums, outs):
+    arrays = [array for one in sums for array in (one.mine, one.received, *one.others)]
     return pl.pallas_call(
-        kernel,
-        in_specs=[pl.BlockSpec(memory_space=pl.ANY)] + specs,
-        out_specs=(VMEM,) * len(outs),
-        out_shape=shaped(*[(shape, F32) for shape in outs]),
-        compiler_params=pltpu.CompilerParams(vmem_limit_bytes=16 << 20),
-        cost_estimate=pl.CostEstimate(flops=1, bytes_accessed=1, transcendentals=0),
-    )(*operands)
-
-
-class Summed:
-    def __init__(self, mine, other, kind):
-        self.steps = axis_steps(kind)
-        self.core = (("row", 1),) * 2
-        self.mine, self.other, self.at = mine, other, 0
-        self.width = mine.shape[1]
-
-    def advance(self, token):
-        count, at = len(self.steps), self.at
-        self.at += 1
-        if at == 0:
-            self.received = exchanged(self.other, *self.core)
-            return token
-        rows = self.mine.shape[0]
-        if at <= count:
-            step = self.steps[at - 1]
-            half = (rows // 2, self.width)
-            send, self.mine = piece_call(
-                split_kernel, [SMEM, VMEM, VMEM], [half, half], token, place_bit(*step), self.mine, self.received
-            )
-            self.received = exchanged(send, *step)
-            return self.mine
-        if at == count + 1:
-            (self.mine,) = piece_call(add_kernel, [VMEM] * 2, [self.mine.shape], token, self.mine, self.received)
-        else:
-            step = self.steps[2 * count + 1 - at]
-            (self.mine,) = piece_call(
-                join_kernel, [SMEM, VMEM, VMEM], [(2 * rows, self.width)], token, place_bit(*step), self.mine,
-                self.received,
-            )
-        step = self.steps[2 * count - at] if at <= 2 * count else self.core
-        self.received = exchanged(self.mine, *step)
-        return self.mine
-
-    def turns(self):
-        return 2 * len(self.steps) + 2
-
-
-def moved(stage_refs, routes, sems):
-    into = []
-    for i, (source, buffer, target) in enumerate(routes):
-        copy = pltpu.make_async_copy(source, buffer, sems.at[i])
-        copy.start()
-        into.append(copy)
-    out = []
-    for i, (source, buffer, target) in enumerate(routes):
-        into[i].wait()
-        copy = pltpu.make_async_copy(buffer, target, sems.at[len(routes) + i])
-        copy.start()
-        out.append(copy)
-    for copy in out:
-        copy.wait()
-
-
-def finish_mlp(_, mine_a, got_a, mine_b, got_b, grad_down, grad_up, grad_out, buffer_a, buffer_b, sems):
-    rows, width = mine_a.shape
-    half_h = grad_out.shape[0] // 2
-    even = lax.axis_index("row") % 2 == 0
-
-    def run(a, b):
-        routes, room = [], {0: 0, 1: 0}
-        for k, (pair, begin) in enumerate(((a, 0), (b, rows))):
-            for j in range(rows // width):
-                at, to = pl.ds(j * width, width), pl.ds(begin + j * width, width)
-                buffers = buffer_a if k == 0 else buffer_b
-                routes.append((pair[0].at[at], buffers.at[0].at[at], grad_down.at[to]))
-                routes.append((pair[1].at[at], buffers.at[1].at[at], grad_up.at[:, to]))
-        for k in range(2):
-            at = pl.ds(rows, half_h)
-            routes.append((b[k].at[at], buffer_b.at[k].at[at], grad_out.at[pl.ds(k * half_h, half_h)]))
-        moved(None, routes, sems)
-
-    @pl.when(even)
-    def _():
-        run((mine_a, got_a), (mine_b, got_b))
-
-    @pl.when(jnp.logical_not(even))
-    def _():
-        run((got_a, mine_a), (got_b, mine_b))
-
-
-def finish_gates(_, mine_c, got_c, mine_d, got_d, grad_z, grad_h, small, buffer_c, buffer_d, sems):
-    half, hidden = grad_z.shape[0] // 2, grad_z.shape[1]
-    even = lax.axis_index("row") % 2 == 0
-
-    def run(c, d):
-        cols, low, high = pl.ds(0, hidden), pl.ds(0, half), pl.ds(half, half)
-        routes = []
-        for k, target in enumerate((grad_z, grad_h)):
-            routes.append((c[k], buffer_c.at[k], target.at[low]))
-            routes.append((d[k].at[:, cols], buffer_d.at[k].at[:, cols], target.at[high]))
-        few, past = pl.ds(0, small.shape[0]), pl.ds(hidden, 128)
-        routes.append((d[0].at[few, past], buffer_d.at[0].at[few, past], small))
-        moved(None, routes, sems)
-
-    @pl.when(even)
-    def _():
-        run((mine_c, got_c), (mine_d, got_d))
-
-    @pl.when(jnp.logical_not(even))
-    def _():
-        run((got_c, mine_c), (got_d, mine_d))
-
-
-def finish_call(kernel, token, sums, outs, copies):
-    arrays = [array for one in sums for array in (one.mine, one.received)]
-    return pl.pallas_call(
-        kernel,
-        in_specs=[pl.BlockSpec(memory_space=pl.ANY)] + [HBM] * len(arrays),
+        functools.partial(finish_kernel, [one.steps[0] for one in sums], routes, len(outs)),
+        in_specs=[pl.BlockSpec(memory_space=pl.ANY)] * (1 + len(arrays)),
         out_specs=(HBM,) * len(outs),
         out_shape=shaped(*outs),
-        scratch_shapes=[pltpu.VMEM((2,) + one.mine.shape, F32) for one in sums]
-        + [pltpu.SemaphoreType.DMA((2 * copies,))],
+        scratch_shapes=[pltpu.VMEM((2, 2) + one.mine.shape, F32) for one in sums]
+        + [pltpu.SemaphoreType.DMA((2, 48))],
         compiler_params=pltpu.CompilerParams(vmem_limit_bytes=32 << 20),
         cost_estimate=pl.CostEstimate(flops=1, bytes_accessed=1, transcendentals=0),
     )(token, *arrays)
+
+
+def cut(first, rows, marks):
+    inside = [first] + [m for m in marks if first < m < first + rows] + [first + rows]
+    return [(a - first, a, b - a) for a, b in zip(inside, inside[1:])]
 
 
 def per_device(
@@ -769,29 +770,27 @@
         [((count + lag * SUB, width), F32), ((lag, SUB, width), F32)],
         4 * count * width * hidden,
         64,
+        56,
     )
     carried, levels = carry_forward(totals)
-    pairs_a = ((ff // 2, width), F32)
-    pairs_b = ((ff // 2 + hidden // 2, width), F32)
-    (blend, output, grad_middle, grad_gain_two, grad_state, subb, passed,
-     mine_a, other_a, mine_b, other_b) = staged_call(
+    mlp_pair, out_pair = ((ff, width), F32), ((hidden // 2, width), F32)
+    blend, output, grad_middle, grad_gain_two, grad_state, subb, passed, mine_a, other_a, mine_b, other_b = staged_call(
         mlp_kernel,
         [first_len],
         [carried, subk, subs, keep, drive, cand, gate, x, w_out, gain_two, w_up, w_down, up],
         [(th, BF16), (tokens.shape, BF16), (tw, F32), ((1, width), F32), (th, F32), ((SUB, hidden), F32),
          ((rows, hidden), F32)],
-        [pairs_a, pairs_a, pairs_b, pairs_b],
+        [mlp_pair, mlp_pair, out_pair, out_pair],
         [((SUB, hidden), F32), (th, BF16), (tw, BF16), (tw, F32), (tw, F32), (tw, F32),
          ((ff, width), F32), ((ff, width), F32), ((hidden // 2, width), F32), ((hidden // 2, width), F32)],
         12 * count * width * ff,
         64,
+        56,
         chunks,
     )
-    returned = carry_backward(passed, levels)
-    sums = [Summed(mine_a, other_a, KINDS[0]), Summed(mine_b, other_b, KINDS[1])]
-    token = returned
-    for turn in EARLY:
-        token = sums[turn].advance(token)
+    returned, seen = carry_backward(passed, levels)
+    early = [Summed(mine_a, other_a, ORDERS[0]), Summed(mine_b, other_b, ORDERS[1])]
+    token, _ = wave([(passed, *seen)[HOLD]], early)
     tile = 16
     pair = ((width // 2, hidden), F32)
     pair_small = ((width // 2, hidden + 128), F32)
@@ -807,6 +806,7 @@
          ((width, hidden), F32), ((width, hidden), F32), ((width, 128), F32)],
         8 * count * width * hidden,
         64,
+        30,
         chunks,
     )
     received = lax.ppermute(sent, "seq", [(i + 1, i) for i in range(devices - 1)])
@@ -822,19 +822,50 @@
         scratch_shapes=[pltpu.VMEM((tile, width), F32)],
         input_output_aliases={5: 0},
     )(tokens, tail_normed, tail_middle, received, gain_one, grad_tokens)
-    sums += [Summed(mine_c, other_c, KINDS[2]), Summed(mine_d, other_d, KINDS[3])]
-    token = tail_normed
-    while any(one.at < one.turns() for one in sums):
-        for one in sums:
-            if one.at < one.turns():
-                token = one.advance(token)
+    late = [Summed(mine_c, other_c, ORDERS[2]), Summed(mine_d, other_d, ORDERS[3])]
+    tokens = [[tail_normed], [grad_tokens]]
+    while late[0].busy():
+        more = tokens.pop(0) if tokens else []
+        if early[0].busy():
+            token, _ = wave([token, *more], early + late)
+        else:
+            token, ready = wave([token, *more], late, [one.received for one in early])
+            for one, received in zip(early, ready):
+                one.received = received
+    for one in early:
+        one.across()
+    for one in late:
+        one.across()
+
+    def mlp_routes(k, parity, first, rows):
+        everything, plan = pl.ds(0, width), []
+        if k == 1:
+            return [(pl.ds(0, rows), everything, 2, (pl.ds(first + parity * hidden // 2, rows), everything))]
+        for offset, at, size in cut(first, rows, range(0, ff, width)):
+            inner = pl.ds(offset, size)
+            if parity == 0:
+                plan.append((inner, everything, 0, (pl.ds(at, size), everything)))
+            else:
+                block = at // width * width
+                plan.append((inner, everything, 1, (pl.ds(at - block, size), pl.ds(block, width))))
+        return plan
+
+    def gate_routes(k, parity, first, rows):
+        inner, cols = pl.ds(0, rows), pl.ds(0, hidden)
+        plan = [(inner, cols, parity, (pl.ds(first + k * width // 2, rows), cols))]
+        few = SUB * width // 128
+        if k == 1 and parity == 0 and first < few:
+            least = min(rows, few - first)
+            at, all_cols = pl.ds(0, least), pl.ds(0, 128)
+            plan.append((at, pl.ds(hidden, 128), 2, (pl.ds(first, least), all_cols)))
+        return plan
+
     grad_down, grad_up, grad_out = finish_call(
-        finish_mlp, token, sums[:2], [((ff, width), F32), ((width, ff), F32), ((hidden, width), F32)],
-        2 * (ff // width) + 2,
+        mlp_routes, token, early, [((ff, width), F32), ((width, ff), F32), ((hidden, width), F32)]
     )
     grad_z, grad_h, small = finish_call(
-        finish_gates, token, sums[2:],
-        [((width, hidden), F32), ((width, hidden), F32), ((SUB * width // 128, 128), F32)], 5,
+        gate_routes, grad_out, late,
+        [((width, hidden), F32), ((width, hidden), F32), ((SUB * width // 128, 128), F32)],
     )
     small = small.reshape(width // 128, SUB, 128).swapaxes(0, 1).reshape(SUB, width)
     bias_at = 2 + lag

time: 317 us -> 270 us (0.85)
  starting transfers between devices: 97 us -> 66.6 us
  Pallas kernels: 70.9 us -> 50.4 us
  local copies, waits for them, and re-layouts: 6.47 us -> 15 us
    ppermute x40 -> x44, starting transfers between devices: 76.5 us -> 46 us  [exchanged(): return lax.ppermute(array, BOTH, pairs)]
    pallas_call x38 -> x11, Pallas kernels: 31.5 us -> 13.4 us  [the longest x2 8.73 us: finish_call(): pl.pallas_call(functools.partial(finish_kernel, [one.steps[0] for one in...]
    ppermute x40 -> x44, waiting for transfers between devices: 118 us -> 108 us  [exchanged(): return lax.ppermute(array, BOTH, pairs)]
    unnamed x22 -> x60, local copies, waits for them, and re-layouts: 5.28 us -> 13.8 us
    ppermute x1, waiting for transfers between devices: 4.51 us -> 10.7 us  [per_device(): lax.ppermute(sent, 'seq', [(i + 1, i) for i in range(devices - 1)])]
  transfers between devices with their start and end apart: 48 -> 52, of which waited for: 26 -> 30; matrix products, arithmetic and copies ran while one was open for 1% -> 0% of each run, Pallas kernels for 10% -> 6%
where the time goes in v3:
time: 270 us; the launch traced here: 269 us
  waiting for transfers between devices  133 us (49%)
  starting transfers between devices  66.6 us (25%)
  Pallas kernels  50.4 us (19%)
  local copies, waits for them, and re-layouts  15 us (6%)
  other arithmetic  2.93 us (1%)
    ppermute x44, waiting for transfers between devices, exchanged(): return lax.ppermute(array, BOTH, pairs)  108 us
    ppermute x44, starting transfers between devices, exchanged(): return lax.ppermute(array, BOTH, pairs)  46 us
    pallas_call x3, Pallas kernels, staged_call(): pl.pallas_call(body, in_specs=[SMEM] * n_s + [HBM] * n_i, out_specs=(HBM,...  35.2 us
    ppermute x6, starting transfers between devices, swapped(): lax.ppermute(array, axis, [(i, i ^ bit) for i in range(lax.axis_size(axis...  14.4 us
    unnamed x60, local copies, waits for them, and re-layouts  13.8 us
    ppermute x6, waiting for transfers between devices, swapped(): lax.ppermute(array, axis, [(i, i ^ bit) for i in range(lax.axis_size(axis...  12.5 us
    ppermute x1, waiting for transfers between devices, per_device(): lax.ppermute(sent, 'seq', [(i + 1, i) for i in range(devices - 1)])  10.7 us
    pallas_call x2, Pallas kernels, finish_call(): pl.pallas_call(functools.partial(finish_kernel, [one.steps[0] for one in...  8.73 us
  transfers between devices with their start and end apart: 52, of which 30 were waited for; matrix products, arithmetic and copies ran while one was open for 0% of the time, Pallas kernels for 6%

profile of v3, /device:TPU:0, one launch (start us, length us, event | category | flops | bytes accessed | tf_op | source)
XLA Modules:
  0.0 268.9 jit_solution(10646272778689658991)
XLA Ops:
  1.4 4.8 %collective-permute-start = (f32[4,3,512]{2,1,0:T(4,128)S(1)}, f32[4,3,512]{2,1,0:T(4,128)S(1)}, u32[]{:S(2)}, u32[]{:S(2)}) collective-permute-start(f32[4,3,512]{2,1,0:T(4,128)S(1)} %slice_convert_fusion), channel_id=1, source_target_pairs={{0,1},{1,2},{2,3},{3,4},{4,5},{5,6},{6,7},{8,9},{9,10},{10,11},{11... | collective-permute-start | bytes 73736 | tf_op jit(solution)/shard_map/ppermute | solution.py:758
  8.5 7.5 %shard_map.203 = (bf16[512,512]{1,0:T(8,128)(2,1)}, bf16[512,512]{1,0:T(8,128)(2,1)}, f32[512,1024]{1,0:T(8,128)}, f32[512,1024]{1,0:T(8,128)}, f32[512,1024]{1,...) custom-call(s32[4]{0:T(128)} %refs_0_.5, ...), custom_call_target="tpu_custom_call" | custom-call | flops 1073741824 | bytes 8388608 | tf_op jit(solution)/shard_map/pallas_call | solution.py:82
  15.9 2.4 collective-permute-start.1
  18.3 2.1 collective-permute-done.1
  21.2 3.1 %collective-permute-start.2 = (f32[2,4,1024]{2,1,0:T(4,128)S(1)}, f32[2,4,1024]{2,1,0:T(4,128)S(1)}, u32[]{:S(2)}, u32[]{:S(2)}) collective-permute-start(f32[2,4,1024]{2,1,0:T(4,128)S(1)} %pad_maximum_fusion), channel_id=1, source_target_pairs={{0,2},{1,3},{2,0},{3,1},{4,6},{5,7},{6,4},{7,5},{8,10},{9,11},{10,... | collective-permute-start | bytes 98312 | tf_op jit(solution)/shard_map/ppermute | solution.py:490
  24.3 1.9 collective-permute-done.2
  26.2 3.1 %collective-permute-start.3 = (f32[2,4,1024]{2,1,0:T(4,128)S(1)}, f32[2,4,1024]{2,1,0:T(4,128)S(1)}, u32[]{:S(2)}, u32[]{:S(2)}) collective-permute-start(f32[2,4,1024]{2,1,0:T(4,128)S(1)} %pad_maximum_fusion.1), channel_id=1, source_target_pairs={{0,4},{1,5},{2,6},{3,7},{4,0},{5,1},{6,2},{7,3},{8,12},{9,13},{10,... | collective-permute-start | bytes 98312 | tf_op jit(solution)/shard_map/ppermute | solution.py:490
  29.3 1.9 collective-permute-done.3
  31.8 19.2 %shard_map.204 = (bf16[512,1024]{1,0:T(8,128)(2,1)}, bf16[4,128,512]{2,1,0:T(8,128)(2,1)}, f32[512,512]{1,0:T(8,128)}, f32[1,512]{1,0:T(1,128)}, f32[512,1024]{1...) custom-call(s32[4]{0:T(128)} %refs_0_.5, ...), custom_call_target="tpu_custom_call" | custom-call | flops 6442450944 | bytes 8388608 | tf_op jit(solution)/shard_map/pallas_call | solution.py:82
  52.5 3.0 %collective-permute-done.4 = f32[4,1024]{1,0:T(4,128)S(1)} collective-permute-done((f32[4,1024]{1,0:T(4,128)}, f32[4,1024]{1,0:T(4,128)S(1)}, u32[]{:S(2)}, u32[]{:S(2)}) %collective-permute-start.4) | collective-permute-done | bytes 16416 | tf_op jit(solution)/shard_map/ppermute | solution.py:490
  56.2 2.0 collective-permute-start.5
  58.2 1.8 collective-permute-done.5
  60.1 3.0 %collective-permute-start.6 = (f32[4,1024]{1,0:T(4,128)S(1)}, f32[4,1024]{1,0:T(4,128)S(1)}, u32[]{:S(2)}, u32[]{:S(2)}) collective-permute-start(f32[4,1024]{1,0:T(4,128)S(1)} %fusion.8), channel_id=1, source_target_pairs={{0,4},{1,5},{2,6},{3,7},{4,0},{5,1},{6,2},{7,3},{8,12},{9,13},{10,... | collective-permute-start | bytes 49160 | tf_op jit(solution)/shard_map/ppermute | solution.py:490
  64.8 2.2 copy-done
  72.2 8.6 %shard_map.205 = (bf16[4,128,512]{2,1,0:T(8,128)(2,1)}, f32[4,3,512]{2,1,0:T(4,128)S(1)}, f32[4,16,512]{2,1,0:T(8,128)S(1)}, f32[4,16,512]{2,1,0:T(8,128)S(1)}, ...) custom-call(s32[4]{0:T(128)S(1)} %copy-done.26, ...), custom_call_target="tpu_custom_call" | custom-call | flops 2147483648 | bytes 8388608 | tf_op jit(solution)/shard_map/pallas_call | solution.py:82
  81.4 1.9 collective-permute-start.11
  83.3 1.9 collective-permute-done.12.refs_7_
  85.2 10.2 %collective-permute-done.11.refs_5_ = f32[256,512]{1,0:T(8,128)S(1)} collective-permute-done((f32[256,512]{1,0:T(8,128)S(1)}, f32[256,512]{1,0:T(8,128)S(1)}, u32[]{:S(2)}, u32[]{:S(2)}) %collective-permute-start.11) | collective-permute-done | bytes 524320 | tf_op jit(solution)/shard_map/ppermute | solution.py:554
  102.6 2.8 %collective-permute-start.15 = (f32[128,512]{1,0:T(8,128)}, f32[128,512]{1,0:T(8,128)}, u32[]{:S(2)}, u32[]{:S(2)}) collective-permute-start(f32[128,512]{1,0:T(8,128)} %get-tuple-element.134), channel_id=1, source_target_pairs={{0,4},{1,5},{2,6},{3,7},{4,0},{5,1},{6,2},{7,3},{8,12},{9,13},{10,... | collective-permute-start | bytes 786440 | tf_op jit(solution)/shard_map/ppermute | solution.py:554
  106.7 10.7 %collective-permute-done.7.received = f32[4,3,512]{2,1,0:T(4,128)S(1)} collective-permute-done((f32[4,3,512]{2,1,0:T(4,128)S(1)}, f32[4,3,512]{2,1,0:T(4,128)S(1)}, u32[]{:S(2)}, u32[]{:S(2)}) %collective-permute-start.7) | collective-permute-done | bytes 24608 | tf_op jit(solution)/shard_map/ppermute | solution.py:812
  118.0 1.9 shard_map.206.refs_1_
  124.6 2.7 %collective-permute-start.18 = (f32[256,512]{1,0:T(8,128)S(1)}, f32[256,512]{1,0:T(8,128)S(1)}, u32[]{:S(2)}, u32[]{:S(2)}) collective-permute-start(f32[256,512]{1,0:T(8,128)S(1)} %get-tuple-element.139.refs_0_), channel_id=1, source_target_pairs={{0,2},{1,3},{2,0},{3,1},{4,6},{5,7},{6,4},{7,5},{8,10},{9,11},{10,... | collective-permute-start | bytes 1572872 | tf_op jit(solution)/shard_map/ppermute | solution.py:554
  127.3 2.3 collective-permute-start.21
  131.6 5.8 %collective-permute-done.19.refs_4_ = f32[64,512]{1,0:T(8,128)S(1)} collective-permute-done((f32[64,512]{1,0:T(8,128)S(1)}, f32[64,512]{1,0:T(8,128)S(1)}, u32[]{:S(2)}, u32[]{:S(2)}) %collective-permute-start.19) | collective-permute-done | bytes 131104 | tf_op jit(solution)/shard_map/ppermute | solution.py:554
  137.4 8.3 %collective-permute-done.21.refs_8_ = f32[64,1152]{1,0:T(8,128)S(1)} collective-permute-done((f32[64,1152]{1,0:T(8,128)S(1)}, f32[64,1152]{1,0:T(8,128)S(1)}, u32[]{:S(2)}, u32[]{:S(2)}) %collective-permute-start.21) | collective-permute-done | bytes 294944 | tf_op jit(solution)/shard_map/ppermute | solution.py:554
  146.4 2.9 %collective-permute-start.22 = (f32[128,512]{1,0:T(8,128)S(1)}, f32[128,512]{1,0:T(8,128)S(1)}, u32[]{:S(2)}, u32[]{:S(2)}) collective-permute-start(f32[128,512]{1,0:T(8,128)S(1)} %get-tuple-element.147.refs_0_), channel_id=1, source_target_pairs={{0,4},{1,5},{2,6},{3,7},{4,0},{5,1},{6,2},{7,3},{8,12},{9,13},{10,... | collective-permute-start | bytes 786440 | tf_op jit(solution)/shard_map/ppermute | solution.py:554
  150.7 2.0 collective-permute-start.23
  152.7 3.6 %collective-permute-done.23.refs_4_ = f32[32,512]{1,0:T(8,128)S(1)} collective-permute-done((f32[32,512]{1,0:T(8,128)S(1)}, f32[32,512]{1,0:T(8,128)S(1)}, u32[]{:S(2)}, u32[]{:S(2)}) %collective-permute-start.23) | collective-permute-done | bytes 65568 | tf_op jit(solution)/shard_map/ppermute | solution.py:554
  156.3 1.8 collective-permute-done.25.refs_8_
  158.1 3.2 %collective-permute-done.22.refs_2_ = f32[128,512]{1,0:T(8,128)S(1)} collective-permute-done((f32[128,512]{1,0:T(8,128)S(1)}, f32[128,512]{1,0:T(8,128)S(1)}, u32[]{:S(2)}, u32[]{:S(2)}) %collective-permute-start.22) | collective-permute-done | bytes 262176 | tf_op jit(solution)/shard_map/ppermute | solution.py:554
  162.2 2.8 %collective-permute-start.28 = (f32[16,1024]{1,0:T(8,128)S(1)}, f32[16,1024]{1,0:T(8,128)S(1)}, u32[]{:S(2)}, u32[]{:S(2)}) collective-permute-start(f32[16,1024]{1,0:T(8,128)S(1)} %get-tuple-element.158), channel_id=1, source_target_pairs={{0,4},{1,5},{2,6},{3,7},{4,0},{5,1},{6,2},{7,3},{8,12},{9,13},{10,... | collective-permute-start | bytes 196616 | tf_op jit(solution)/shard_map/ppermute | solution.py:554
  166.5 11.8 %collective-permute-done.28.refs_6_ = f32[16,1024]{1,0:T(8,128)S(1)} collective-permute-done((f32[16,1024]{1,0:T(8,128)S(1)}, f32[16,1024]{1,0:T(8,128)S(1)}, u32[]{:S(2)}, u32[]{:S(2)}) %collective-permute-start.28) | collective-permute-done | bytes 65568 | tf_op jit(solution)/shard_map/ppermute | solution.py:554
  182.2 7.6 %collective-permute-done.32.refs_6_ = f32[16,1024]{1,0:T(8,128)S(1)} collective-permute-done((f32[16,1024]{1,0:T(8,128)S(1)}, f32[16,1024]{1,0:T(8,128)S(1)}, u32[]{:S(2)}, u32[]{:S(2)}) %collective-permute-start.32) | collective-permute-done | bytes 65568 | tf_op jit(solution)/shard_map/ppermute | solution.py:554
  189.8 2.2 collective-permute-done.30.refs_2_
  192.2 2.2 collective-permute-start.34
  197.4 6.0 %collective-permute-done.36.refs_6_ = f32[32,1024]{1,0:T(8,128)S(1)} collective-permute-done((f32[32,1024]{1,0:T(8,128)S(1)}, f32[32,1024]{1,0:T(8,128)S(1)}, u32[]{:S(2)}, u32[]{:S(2)}) %collective-permute-start.36) | collective-permute-done | bytes 131104 | tf_op jit(solution)/shard_map/ppermute | solution.py:554
  203.4 2.5 collective-permute-done.35.refs_4_
  205.9 2.6 collective-permute-done.34.refs_2_
  211.9 2.0 collective-permute-start.40
  213.9 7.2 %collective-permute-done.40.refs_4_ = f32[64,1024]{1,0:T(8,128)S(1)} collective-permute-done((f32[64,1024]{1,0:T(8,128)S(1)}, f32[64,1024]{1,0:T(8,128)S(1)}, u32[]{:S(2)}, u32[]{:S(2)}) %collective-permute-start.40) | collective-permute-done | bytes 262176 | tf_op jit(solution)/shard_map/ppermute | solution.py:554
  221.1 7.3 %collective-permute-done.41.refs_6_ = f32[64,1152]{1,0:T(8,128)S(1)} collective-permute-done((f32[64,1152]{1,0:T(8,128)S(1)}, f32[64,1152]{1,0:T(8,128)S(1)}, u32[]{:S(2)}, u32[]{:S(2)}) %collective-permute-start.41) | collective-permute-done | bytes 294944 | tf_op jit(solution)/shard_map/ppermute | solution.py:554
  229.6 8.1 %collective-permute-done.38.refs_1_ = f32[1024,512]{1,0:T(8,128)S(1)} collective-permute-done((f32[1024,512]{1,0:T(8,128)S(1)}, f32[1024,512]{1,0:T(8,128)S(1)}, u32[]{:S(2)}, u32[]{:S(2)}) %collective-permute-start.38) | collective-permute-done | bytes 2097184 | tf_op jit(solution)/shard_map/ppermute | solution.py:554
  238.4 1.8 collective-permute-start.45
  240.2 2.6 collective-permute-done.44.refs_6_
  244.1 4.2 %collective-permute-done.49.refs_5_ = f32[128,1152]{1,0:T(8,128)S(1)} collective-permute-done((f32[128,1152]{1,0:T(8,128)S(1)}, f32[128,1152]{1,0:T(8,128)S(1)}, u32[]{:S(2)}, u32[]{:S(2)}) %collective-permute-start.49) | collective-permute-done | bytes 589856 | tf_op jit(solution)/shard_map/ppermute | solution.py:554
  248.8 8.0 %collective-permute-done.46.refs_1_ = f32[128,1024]{1,0:T(8,128)S(1)} collective-permute-done((f32[128,1024]{1,0:T(8,128)S(1)}, f32[128,1024]{1,0:T(8,128)S(1)}, u32[]{:S(2)}, u32[]{:S(2)}) %collective-permute-start.46) | collective-permute-done | bytes 524320 | tf_op jit(solution)/shard_map/ppermute | solution.py:554
  256.7 5.5 %shard_map.216 = (f32[2048,512]{1,0:T(8,128)}, f32[512,2048]{1,0:T(8,128)}, f32[1024,512]{1,0:T(8,128)}) custom-call(f32[128,1024]{1,0:T(8,128)S(1)} %get-tuple-element.173._.refs_0_, f32[1024,512]{1,0:T(8,128)S(1)} %get-tuple-element.169.refs_0_, f32[1024,512]{1,0:T(8,128)S(1)} %get-tuple-element.174.refs_1_, ...), custom_call_target="tpu_custom_call" | custom-call | flops 1 | bytes 1 | tf_op jit(solution)/shard_map/pallas_call | solution.py:732
  263.9 3.2 %shard_map.217 = (f32[512,1024]{1,0:T(8,128)}, f32[512,1024]{1,0:T(8,128)}, f32[32,128]{1,0:T(8,128)S(1)}) custom-call(f32[1024,512]{1,0:T(8,128)S(1)} %copy-done.1, f32[128,1024]{1,0:T(8,128)S(1)} %get-tuple-element.173._.refs_0_, f32[128,1024]{1,0:T(8,128)S(1)} %collective-permute-done.46.refs_1_, f32[128,1024]{1,0:T(8,128)S(1)} %collective-permute-done.47.refs_2_, ...), custom_call_target="tpu_custom_call" | custom-call | flops 1 | bytes 1 | tf_op jit(solution)/shard_map/pallas_call | solution.py:732
  (143 shorter events, 51.6 us)
Async XLA Ops:
  1.4 6.4 %collective-permute-start = (f32[4,3,512]{2,1,0:T(4,128)S(1)}, f32[4,3,512]{2,1,0:T(4,128)S(1)}, u32[]{:S(2)}, u32[]{:S(2)}) collective-permute-start(f32[4,3,512]{2,1,0:T(4,128)S(1)} %slice_convert_fusion), channel_id=1, source_target_pairs={{0,1},{1,2},{2,3},{3,4},{4,5},{5,6},{6,7},{8,9},{9,10},{10,11},{11... | collective-permute-start | bytes 73736 | tf_op jit(solution)/shard_map/ppermute | solution.py:758
  15.9 4.5 %collective-permute-start.1 = (f32[2,4,1024]{2,1,0:T(4,128)}, f32[2,4,1024]{2,1,0:T(4,128)S(1)}, u32[]{:S(2)}, u32[]{:S(2)}) collective-permute-start(f32[2,4,1024]{2,1,0:T(4,128)} %get-tuple-element.97), channel_id=1, source_target_pairs={{0,1},{1,0},{2,3},{3,2},{4,5},{5,4},{6,7},{7,6},{8,9},{9,8},{10,11... | collective-permute-start | bytes 98312 | tf_op jit(solution)/shard_map/ppermute | solution.py:490
  21.2 5.0 %collective-permute-start.2 = (f32[2,4,1024]{2,1,0:T(4,128)S(1)}, f32[2,4,1024]{2,1,0:T(4,128)S(1)}, u32[]{:S(2)}, u32[]{:S(2)}) collective-permute-start(f32[2,4,1024]{2,1,0:T(4,128)S(1)} %pad_maximum_fusion), channel_id=1, source_target_pairs={{0,2},{1,3},{2,0},{3,1},{4,6},{5,7},{6,4},{7,5},{8,10},{9,11},{10,... | collective-permute-start | bytes 98312 | tf_op jit(solution)/shard_map/ppermute | solution.py:490
  26.2 5.0 %collective-permute-start.3 = (f32[2,4,1024]{2,1,0:T(4,128)S(1)}, f32[2,4,1024]{2,1,0:T(4,128)S(1)}, u32[]{:S(2)}, u32[]{:S(2)}) collective-permute-start(f32[2,4,1024]{2,1,0:T(4,128)S(1)} %pad_maximum_fusion.1), channel_id=1, source_target_pairs={{0,4},{1,5},{2,6},{3,7},{4,0},{5,1},{6,2},{7,3},{8,12},{9,13},{10,... | collective-permute-start | bytes 98312 | tf_op jit(solution)/shard_map/ppermute | solution.py:490
  51.0 13.8 %collective-permute-start.8 = (f32[2048,512]{1,0:T(8,128)}, f32[2048,512]{1,0:T(8,128)S(1)}, u32[]{:S(2)}, u32[]{:S(2)}) collective-permute-start(f32[2048,512]{1,0:T(8,128)} %get-tuple-element.120), channel_id=1, source_target_pairs={{0,8},{1,9},{2,10},{3,11},{4,12},{5,13},{6,14},{7,15},{8,0},{9,1},... | collective-permute-start | bytes 12582920 | tf_op jit(solution)/shard_map/ppermute | solution.py:554
  51.1 13.8 %collective-permute-start.9 = (f32[512,512]{1,0:T(8,128)}, f32[512,512]{1,0:T(8,128)S(1)}, u32[]{:S(2)}, u32[]{:S(2)}) collective-permute-start(f32[512,512]{1,0:T(8,128)} %get-tuple-element.122), channel_id=1, source_target_pairs={{0,8},{1,9},{2,10},{3,11},{4,12},{5,13},{6,14},{7,15},{8,0},{9,1},... | collective-permute-start | bytes 3145736 | tf_op jit(solution)/shard_map/ppermute | solution.py:554
  60.1 4.7 %collective-permute-start.6 = (f32[4,1024]{1,0:T(4,128)S(1)}, f32[4,1024]{1,0:T(4,128)S(1)}, u32[]{:S(2)}, u32[]{:S(2)}) collective-permute-start(f32[4,1024]{1,0:T(4,128)S(1)} %fusion.8), channel_id=1, source_target_pairs={{0,4},{1,5},{2,6},{3,7},{4,0},{5,1},{6,2},{7,3},{8,12},{9,13},{10,... | collective-permute-start | bytes 49160 | tf_op jit(solution)/shard_map/ppermute | solution.py:490
  69.0 26.5 %collective-permute-start.10 = (f32[1024,512]{1,0:T(8,128)S(1)}, f32[1024,512]{1,0:T(8,128)S(1)}, u32[]{:S(2)}, u32[]{:S(2)}) collective-permute-start(f32[1024,512]{1,0:T(8,128)S(1)} %get-tuple-element.123.refs_0_), channel_id=1, source_target_pairs={{0,1},{1,0},{2,3},{3,2},{4,5},{5,4},{6,7},{7,6},{8,24},{9,25},{10,... | collective-permute-start | bytes 6291464 | tf_op jit(solution)/shard_map/ppermute | solution.py:554
  80.8 4.4 %collective-permute-start.13 = (f32[256,1152]{1,0:T(8,128)S(1)}, f32[256,1152]{1,0:T(8,128)S(1)}, u32[]{:S(2)}, u32[]{:S(2)}) collective-permute-start(f32[256,1152]{1,0:T(8,128)S(1)} %get-tuple-element.130), channel_id=1, source_target_pairs={{0,8},{1,9},{2,10},{3,11},{4,12},{5,13},{6,14},{7,15},{8,0},{9,1},... | collective-permute-start | bytes 3538952 | tf_op jit(solution)/shard_map/ppermute | solution.py:554
  81.4 14.1 %collective-permute-start.11 = (f32[256,512]{1,0:T(8,128)S(1)}, f32[256,512]{1,0:T(8,128)S(1)}, u32[]{:S(2)}, u32[]{:S(2)}) collective-permute-start(f32[256,512]{1,0:T(8,128)S(1)} %get-tuple-element.126), channel_id=1, source_target_pairs={{0,2},{1,3},{2,0},{3,1},{4,6},{5,7},{6,4},{7,5},{8,10},{9,11},{10,... | collective-permute-start | bytes 1572872 | tf_op jit(solution)/shard_map/ppermute | solution.py:554
  98.7 21.1 %collective-permute-start.14 = (f32[512,512]{1,0:T(8,128)S(1)}, f32[512,512]{1,0:T(8,128)S(1)}, u32[]{:S(2)}, u32[]{:S(2)}) collective-permute-start(f32[512,512]{1,0:T(8,128)S(1)} %get-tuple-element.131.refs_0_), channel_id=1, source_target_pairs={{0,16},{1,17},{2,18},{3,19},{4,20},{5,21},{6,22},{7,23},{8,9},{9,8... | collective-permute-start | bytes 3145736 | tf_op jit(solution)/shard_map/ppermute | solution.py:554
  100.2 19.6 %collective-permute-start.17 = (f32[128,1152]{1,0:T(8,128)}, f32[128,1152]{1,0:T(8,128)}, u32[]{:S(2)}, u32[]{:S(2)}) collective-permute-start(f32[128,1152]{1,0:T(8,128)} %get-tuple-element.138), channel_id=1, source_target_pairs={{0,1},{1,0},{2,3},{3,2},{4,5},{5,4},{6,7},{7,6},{8,24},{9,25},{10,... | collective-permute-start | bytes 1769480 | tf_op jit(solution)/shard_map/ppermute | solution.py:554
  101.0 18.9 %collective-permute-start.16 = (f32[128,1024]{1,0:T(8,128)}, f32[128,1024]{1,0:T(8,128)}, u32[]{:S(2)}, u32[]{:S(2)}) collective-permute-start(f32[128,1024]{1,0:T(8,128)} %get-tuple-element.136), channel_id=1, source_target_pairs={{0,2},{1,3},{2,0},{3,1},{4,6},{5,7},{6,4},{7,5},{8,10},{9,11},{10,... | collective-permute-start | bytes 1572872 | tf_op jit(solution)/shard_map/ppermute | solution.py:554
  102.6 17.3 %collective-permute-start.15 = (f32[128,512]{1,0:T(8,128)}, f32[128,512]{1,0:T(8,128)}, u32[]{:S(2)}, u32[]{:S(2)}) collective-permute-start(f32[128,512]{1,0:T(8,128)} %get-tuple-element.134), channel_id=1, source_target_pairs={{0,4},{1,5},{2,6},{3,7},{4,0},{5,1},{6,2},{7,3},{8,12},{9,13},{10,... | collective-permute-start | bytes 786440 | tf_op jit(solution)/shard_map/ppermute | solution.py:554
  105.4 12.0 %collective-permute-start.7 = (f32[4,3,512]{2,1,0:T(4,128)S(1)}, f32[4,3,512]{2,1,0:T(4,128)S(1)}, u32[]{:S(2)}, u32[]{:S(2)}) collective-permute-start(f32[4,3,512]{2,1,0:T(4,128)S(1)} %get-tuple-element.117), channel_id=1, source_target_pairs={{1,0},{2,1},{3,2},{4,3},{5,4},{6,5},{7,6},{9,8},{10,9},{11,10},{12... | collective-permute-start | bytes 73736 | tf_op jit(solution)/shard_map/ppermute | solution.py:812
  124.6 21.6 %collective-permute-start.18 = (f32[256,512]{1,0:T(8,128)S(1)}, f32[256,512]{1,0:T(8,128)S(1)}, u32[]{:S(2)}, u32[]{:S(2)}) collective-permute-start(f32[256,512]{1,0:T(8,128)S(1)} %get-tuple-element.139.refs_0_), channel_id=1, source_target_pairs={{0,2},{1,3},{2,0},{3,1},{4,6},{5,7},{6,4},{7,5},{8,10},{9,11},{10,... | collective-permute-start | bytes 1572872 | tf_op jit(solution)/shard_map/ppermute | solution.py:554
  127.3 18.4 %collective-permute-start.21 = (f32[64,1152]{1,0:T(8,128)S(1)}, f32[64,1152]{1,0:T(8,128)S(1)}, u32[]{:S(2)}, u32[]{:S(2)}) collective-permute-start(f32[64,1152]{1,0:T(8,128)S(1)} %get-tuple-element.146), channel_id=1, source_target_pairs={{0,4},{1,5},{2,6},{3,7},{4,0},{5,1},{6,2},{7,3},{8,12},{9,13},{10,... | collective-permute-start | bytes 884744 | tf_op jit(solution)/shard_map/ppermute | solution.py:554
  129.6 7.8 %collective-permute-start.20 = (f32[64,1024]{1,0:T(8,128)S(1)}, f32[64,1024]{1,0:T(8,128)S(1)}, u32[]{:S(2)}, u32[]{:S(2)}) collective-permute-start(f32[64,1024]{1,0:T(8,128)S(1)} %get-tuple-element.144), channel_id=1, source_target_pairs={{0,16},{1,17},{2,18},{3,19},{4,20},{5,21},{6,22},{7,23},{8,9},{9,8... | collective-permute-start | bytes 786440 | tf_op jit(solution)/shard_map/ppermute | solution.py:554
  130.1 7.3 %collective-permute-start.19 = (f32[64,512]{1,0:T(8,128)S(1)}, f32[64,512]{1,0:T(8,128)S(1)}, u32[]{:S(2)}, u32[]{:S(2)}) collective-permute-start(f32[64,512]{1,0:T(8,128)S(1)} %get-tuple-element.142), channel_id=1, source_target_pairs={{0,16},{1,17},{2,18},{3,19},{4,20},{5,21},{6,22},{7,23},{8,9},{9,8... | collective-permute-start | bytes 393224 | tf_op jit(solution)/shard_map/ppermute | solution.py:554
  146.4 14.9 %collective-permute-start.22 = (f32[128,512]{1,0:T(8,128)S(1)}, f32[128,512]{1,0:T(8,128)S(1)}, u32[]{:S(2)}, u32[]{:S(2)}) collective-permute-start(f32[128,512]{1,0:T(8,128)S(1)} %get-tuple-element.147.refs_0_), channel_id=1, source_target_pairs={{0,4},{1,5},{2,6},{3,7},{4,0},{5,1},{6,2},{7,3},{8,12},{9,13},{10,... | collective-permute-start | bytes 786440 | tf_op jit(solution)/shard_map/ppermute | solution.py:554
  149.3 8.8 %collective-permute-start.25 = (f32[32,1152]{1,0:T(8,128)S(1)}, f32[32,1152]{1,0:T(8,128)S(1)}, u32[]{:S(2)}, u32[]{:S(2)}) collective-permute-start(f32[32,1152]{1,0:T(8,128)S(1)} %get-tuple-element.154), channel_id=1, source_target_pairs={{0,2},{1,3},{2,0},{3,1},{4,6},{5,7},{6,4},{7,5},{8,10},{9,11},{10,... | collective-permute-start | bytes 442376 | tf_op jit(solution)/shard_map/ppermute | solution.py:554
  150.6 5.7 %collective-permute-start.24 = (f32[32,1024]{1,0:T(8,128)S(1)}, f32[32,1024]{1,0:T(8,128)S(1)}, u32[]{:S(2)}, u32[]{:S(2)}) collective-permute-start(f32[32,1024]{1,0:T(8,128)S(1)} %get-tuple-element.152), channel_id=1, source_target_pairs={{0,1},{1,0},{2,3},{3,2},{4,5},{5,4},{6,7},{7,6},{8,24},{9,25},{10,... | collective-permute-start | bytes 393224 | tf_op jit(solution)/shard_map/ppermute | solution.py:554
  150.7 5.6 %collective-permute-start.23 = (f32[32,512]{1,0:T(8,128)S(1)}, f32[32,512]{1,0:T(8,128)S(1)}, u32[]{:S(2)}, u32[]{:S(2)}) collective-permute-start(f32[32,512]{1,0:T(8,128)S(1)} %get-tuple-element.150), channel_id=1, source_target_pairs={{0,1},{1,0},{2,3},{3,2},{4,5},{5,4},{6,7},{7,6},{8,24},{9,25},{10,... | collective-permute-start | bytes 196616 | tf_op jit(solution)/shard_map/ppermute | solution.py:554
  161.4 16.9 %collective-permute-start.26 = (f32[128,512]{1,0:T(8,128)S(1)}, f32[128,512]{1,0:T(8,128)S(1)}, u32[]{:S(2)}, u32[]{:S(2)}) collective-permute-start(f32[128,512]{1,0:T(8,128)S(1)} %get-tuple-element.155.refs_0_.refs_1_), channel_id=1, source_target_pairs={{0,4},{1,5},{2,6},{3,7},{4,0},{5,1},{6,2},{7,3},{8,12},{9,13},{10,... | collective-permute-start | bytes 786440 | tf_op jit(solution)/shard_map/ppermute | solution.py:554
  161.5 16.8 %collective-permute-start.29 = (f32[16,1152]{1,0:T(8,128)S(1)}, f32[16,1152]{1,0:T(8,128)S(1)}, u32[]{:S(2)}, u32[]{:S(2)}) collective-permute-start(f32[16,1152]{1,0:T(8,128)S(1)} %get-tuple-element.160), channel_id=1, source_target_pairs={{0,16},{1,17},{2,18},{3,19},{4,20},{5,21},{6,22},{7,23},{8,9},{9,8... | collective-permute-start | bytes 221192 | tf_op jit(solution)/shard_map/ppermute | solution.py:554
  162.2 16.0 %collective-permute-start.28 = (f32[16,1024]{1,0:T(8,128)S(1)}, f32[16,1024]{1,0:T(8,128)S(1)}, u32[]{:S(2)}, u32[]{:S(2)}) collective-permute-start(f32[16,1024]{1,0:T(8,128)S(1)} %get-tuple-element.158), channel_id=1, source_target_pairs={{0,4},{1,5},{2,6},{3,7},{4,0},{5,1},{6,2},{7,3},{8,12},{9,13},{10,... | collective-permute-start | bytes 196616 | tf_op jit(solution)/shard_map/ppermute | solution.py:554
  178.3 13.7 %collective-permute-start.30 = (f32[256,512]{1,0:T(8,128)S(1)}, f32[256,512]{1,0:T(8,128)S(1)}, u32[]{:S(2)}, u32[]{:S(2)}) collective-permute-start(f32[256,512]{1,0:T(8,128)S(1)} %get-tuple-element.161.refs_0_.refs_1_), channel_id=1, source_target_pairs={{0,2},{1,3},{2,0},{3,1},{4,6},{5,7},{6,4},{7,5},{8,10},{9,11},{10,... | collective-permute-start | bytes 1572872 | tf_op jit(solution)/shard_map/ppermute | solution.py:554
  178.4 11.4 %collective-permute-start.31 = (f32[64,512]{1,0:T(8,128)S(1)}, f32[64,512]{1,0:T(8,128)S(1)}, u32[]{:S(2)}, u32[]{:S(2)}) collective-permute-start(f32[64,512]{1,0:T(8,128)S(1)} %get-tuple-element.162.refs_3_), channel_id=1, source_target_pairs={{0,16},{1,17},{2,18},{3,19},{4,20},{5,21},{6,22},{7,23},{8,9},{9,8... | collective-permute-start | bytes 393224 | tf_op jit(solution)/shard_map/ppermute | solution.py:554
  179.8 10.0 %collective-permute-start.33 = (f32[16,1152]{1,0:T(8,128)S(1)}, f32[16,1152]{1,0:T(8,128)S(1)}, u32[]{:S(2)}, u32[]{:S(2)}) collective-permute-start(f32[16,1152]{1,0:T(8,128)S(1)} %get-tuple-element.164.refs_7_), channel_id=1, source_target_pairs={{0,16},{1,17},{2,18},{3,19},{4,20},{5,21},{6,22},{7,23},{8,9},{9,8... | collective-permute-start | bytes 221192 | tf_op jit(solution)/shard_map/ppermute | solution.py:554
  180.5 9.3 %collective-permute-start.32 = (f32[16,1024]{1,0:T(8,128)S(1)}, f32[16,1024]{1,0:T(8,128)S(1)}, u32[]{:S(2)}, u32[]{:S(2)}) collective-permute-start(f32[16,1024]{1,0:T(8,128)S(1)} %get-tuple-element.163.refs_5_), channel_id=1, source_target_pairs={{0,4},{1,5},{2,6},{3,7},{4,0},{5,1},{6,2},{7,3},{8,12},{9,13},{10,... | collective-permute-start | bytes 196616 | tf_op jit(solution)/shard_map/ppermute | solution.py:554
  192.2 16.4 %collective-permute-start.34 = (f32[512,512]{1,0:T(8,128)S(1)}, f32[512,512]{1,0:T(8,128)S(1)}, u32[]{:S(2)}, u32[]{:S(2)}) collective-permute-start(f32[512,512]{1,0:T(8,128)S(1)} %get-tuple-element.165.refs_0_.refs_1_), channel_id=1, source_target_pairs={{0,16},{1,17},{2,18},{3,19},{4,20},{5,21},{6,22},{7,23},{8,9},{9,8... | collective-permute-start | bytes 3145736 | tf_op jit(solution)/shard_map/ppermute | solution.py:554
  194.3 11.5 %collective-permute-start.35 = (f32[128,512]{1,0:T(8,128)S(1)}, f32[128,512]{1,0:T(8,128)S(1)}, u32[]{:S(2)}, u32[]{:S(2)}) collective-permute-start(f32[128,512]{1,0:T(8,128)S(1)} %get-tuple-element.166.refs_3_), channel_id=1, source_target_pairs={{0,4},{1,5},{2,6},{3,7},{4,0},{5,1},{6,2},{7,3},{8,12},{9,13},{10,... | collective-permute-start | bytes 786440 | tf_op jit(solution)/shard_map/ppermute | solution.py:554
  195.6 7.8 %collective-permute-start.37 = (f32[32,1152]{1,0:T(8,128)S(1)}, f32[32,1152]{1,0:T(8,128)S(1)}, u32[]{:S(2)}, u32[]{:S(2)}) collective-permute-start(f32[32,1152]{1,0:T(8,128)S(1)} %get-tuple-element.168.refs_7_), channel_id=1, source_target_pairs={{0,2},{1,3},{2,0},{3,1},{4,6},{5,7},{6,4},{7,5},{8,10},{9,11},{10,... | collective-permute-start | bytes 442376 | tf_op jit(solution)/shard_map/ppermute | solution.py:554
  197.0 6.4 %collective-permute-start.36 = (f32[32,1024]{1,0:T(8,128)S(1)}, f32[32,1024]{1,0:T(8,128)S(1)}, u32[]{:S(2)}, u32[]{:S(2)}) collective-permute-start(f32[32,1024]{1,0:T(8,128)S(1)} %get-tuple-element.167.refs_5_), channel_id=1, source_target_pairs={{0,1},{1,0},{2,3},{3,2},{4,5},{5,4},{6,7},{7,6},{8,24},{9,25},{10,... | collective-permute-start | bytes 393224 | tf_op jit(solution)/shard_map/ppermute | solution.py:554
  208.8 28.9 %collective-permute-start.38 = (f32[1024,512]{1,0:T(8,128)S(1)}, f32[1024,512]{1,0:T(8,128)S(1)}, u32[]{:S(2)}, u32[]{:S(2)}) collective-permute-start(f32[1024,512]{1,0:T(8,128)S(1)} %get-tuple-element.169.refs_0_), channel_id=1, source_target_pairs={{0,1},{1,0},{2,3},{3,2},{4,5},{5,4},{6,7},{7,6},{8,24},{9,25},{10,... | collective-permute-start | bytes 6291464 | tf_op jit(solution)/shard_map/ppermute | solution.py:554
  208.9 35.2 %collective-permute-start.42 = (f32[1024,512]{1,0:T(8,128)S(1)}, f32[1024,512]{1,0:T(8,128)S(1)}, u32[]{:S(2)}, u32[]{:S(2)}) collective-permute-start(f32[1024,512]{1,0:T(8,128)S(1)} %get-tuple-element.169.refs_0_), channel_id=1, source_target_pairs={{0,8},{1,9},{2,10},{3,11},{4,12},{5,13},{6,14},{7,15},{8,0},{9,1},... | collective-permute-start | bytes 6291464 | tf_op jit(solution)/shard_map/ppermute | solution.py:554
  208.9 20.7 %collective-permute-start.39 = (f32[256,512]{1,0:T(8,128)S(1)}, f32[256,512]{1,0:T(8,128)S(1)}, u32[]{:S(2)}, u32[]{:S(2)}) collective-permute-start(f32[256,512]{1,0:T(8,128)S(1)} %get-tuple-element.170.refs_4_), channel_id=1, source_target_pairs={{0,2},{1,3},{2,0},{3,1},{4,6},{5,7},{6,4},{7,5},{8,10},{9,11},{10,... | collective-permute-start | bytes 1572872 | tf_op jit(solution)/shard_map/ppermute | solution.py:554
  210.3 18.1 %collective-permute-start.41 = (f32[64,1152]{1,0:T(8,128)S(1)}, f32[64,1152]{1,0:T(8,128)S(1)}, u32[]{:S(2)}, u32[]{:S(2)}) collective-permute-start(f32[64,1152]{1,0:T(8,128)S(1)} %get-tuple-element.172.refs_5_), channel_id=1, source_target_pairs={{0,4},{1,5},{2,6},{3,7},{4,0},{5,1},{6,2},{7,3},{8,12},{9,13},{10,... | collective-permute-start | bytes 884744 | tf_op jit(solution)/shard_map/ppermute | solution.py:554
  211.9 9.2 %collective-permute-start.40 = (f32[64,1024]{1,0:T(8,128)S(1)}, f32[64,1024]{1,0:T(8,128)S(1)}, u32[]{:S(2)}, u32[]{:S(2)}) collective-permute-start(f32[64,1024]{1,0:T(8,128)S(1)} %get-tuple-element.171.refs_3_), channel_id=1, source_target_pairs={{0,16},{1,17},{2,18},{3,19},{4,20},{5,21},{6,22},{7,23},{8,9},{9,8... | collective-permute-start | bytes 786440 | tf_op jit(solution)/shard_map/ppermute | solution.py:554
  237.8 18.9 %collective-permute-start.43 = (f32[1024,512]{1,0:T(8,128)S(1)}, f32[1024,512]{1,0:T(8,128)S(1)}, u32[]{:S(2)}, u32[]{:S(2)}) collective-permute-start(f32[1024,512]{1,0:T(8,128)S(1)} %get-tuple-element.174.refs_1_), channel_id=1, source_target_pairs={{0,8},{1,9},{2,10},{3,11},{4,12},{5,13},{6,14},{7,15},{8,0},{9,1},... | collective-permute-start | bytes 6291464 | tf_op jit(solution)/shard_map/ppermute | solution.py:554
  237.9 4.9 %collective-permute-start.44 = (f32[256,512]{1,0:T(8,128)S(1)}, f32[256,512]{1,0:T(8,128)S(1)}, u32[]{:S(2)}, u32[]{:S(2)}) collective-permute-start(f32[256,512]{1,0:T(8,128)S(1)} %get-tuple-element.170.refs_4_), channel_id=1, source_target_pairs={{0,8},{1,9},{2,10},{3,11},{4,12},{5,13},{6,14},{7,15},{8,0},{9,1},... | collective-permute-start | bytes 1572872 | tf_op jit(solution)/shard_map/ppermute | solution.py:554
  238.4 9.9 %collective-permute-start.49 = (f32[128,1152]{1,0:T(8,128)S(1)}, f32[128,1152]{1,0:T(8,128)S(1)}, u32[]{:S(2)}, u32[]{:S(2)}) collective-permute-start(f32[128,1152]{1,0:T(8,128)S(1)} %get-tuple-element.177.refs_4_), channel_id=1, source_target_pairs={{0,1},{1,0},{2,3},{3,2},{4,5},{5,4},{6,7},{7,6},{8,24},{9,25},{10,... | collective-permute-start | bytes 1769480 | tf_op jit(solution)/shard_map/ppermute | solution.py:554
  238.4 9.9 %collective-permute-start.45 = (f32[256,512]{1,0:T(8,128)S(1)}, f32[256,512]{1,0:T(8,128)S(1)}, u32[]{:S(2)}, u32[]{:S(2)}) collective-permute-start(f32[256,512]{1,0:T(8,128)S(1)} %get-tuple-element.175.refs_5_), channel_id=1, source_target_pairs={{0,8},{1,9},{2,10},{3,11},{4,12},{5,13},{6,14},{7,15},{8,0},{9,1},... | collective-permute-start | bytes 1572872 | tf_op jit(solution)/shard_map/ppermute | solution.py:554
  242.8 14.0 %collective-permute-start.46 = (f32[128,1024]{1,0:T(8,128)S(1)}, f32[128,1024]{1,0:T(8,128)S(1)}, u32[]{:S(2)}, u32[]{:S(2)}) collective-permute-start(f32[128,1024]{1,0:T(8,128)S(1)} %get-tuple-element.173._.refs_0_), channel_id=1, source_target_pairs={{0,2},{1,3},{2,0},{3,1},{4,6},{5,7},{6,4},{7,5},{8,10},{9,11},{10,... | collective-permute-start | bytes 1572872 | tf_op jit(solution)/shard_map/ppermute | solution.py:554
  244.1 18.2 %collective-permute-start.50 = (f32[128,1152]{1,0:T(8,128)S(1)}, f32[128,1152]{1,0:T(8,128)S(1)}, u32[]{:S(2)}, u32[]{:S(2)}) collective-permute-start(f32[128,1152]{1,0:T(8,128)S(1)} %get-tuple-element.177.refs_4_), channel_id=1, source_target_pairs={{0,8},{1,9},{2,10},{3,11},{4,12},{5,13},{6,14},{7,15},{8,0},{9,1},... | collective-permute-start | bytes 1769480 | tf_op jit(solution)/shard_map/ppermute | solution.py:554
  248.3 14.1 %collective-permute-start.51 = (f32[128,1152]{1,0:T(8,128)S(1)}, f32[128,1152]{1,0:T(8,128)S(1)}, u32[]{:S(2)}, u32[]{:S(2)}) collective-permute-start(f32[128,1152]{1,0:T(8,128)S(1)} %collective-permute-done.49.refs_5_), channel_id=1, source_target_pairs={{0,8},{1,9},{2,10},{3,11},{4,12},{5,13},{6,14},{7,15},{8,0},{9,1},... | collective-permute-start | bytes 1769480 | tf_op jit(solution)/shard_map/ppermute | solution.py:554
  248.3 14.0 %collective-permute-start.47 = (f32[128,1024]{1,0:T(8,128)S(1)}, f32[128,1024]{1,0:T(8,128)S(1)}, u32[]{:S(2)}, u32[]{:S(2)}) collective-permute-start(f32[128,1024]{1,0:T(8,128)S(1)} %get-tuple-element.173._.refs_0_), channel_id=1, source_target_pairs={{0,8},{1,9},{2,10},{3,11},{4,12},{5,13},{6,14},{7,15},{8,0},{9,1},... | collective-permute-start | bytes 1572872 | tf_op jit(solution)/shard_map/ppermute | solution.py:554
  256.7 5.6 %collective-permute-start.48 = (f32[128,1024]{1,0:T(8,128)S(1)}, f32[128,1024]{1,0:T(8,128)S(1)}, u32[]{:S(2)}, u32[]{:S(2)}) collective-permute-start(f32[128,1024]{1,0:T(8,128)S(1)} %collective-permute-done.46.refs_1_), channel_id=1, source_target_pairs={{0,8},{1,9},{2,10},{3,11},{4,12},{5,13},{6,14},{7,15},{8,0},{9,1},... | collective-permute-start | bytes 1572872 | tf_op jit(solution)/shard_map/ppermute | solution.py:554
  (33 other events, 223.6 us)

commit v4 on v3

--- a/solution.py
+++ b/solution.py
@@ -11,9 +11,14 @@
 EPS = 1e-06
 VMEM = pl.BlockSpec(memory_space=pltpu.VMEM)
 SMEM = pl.BlockSpec(memory_space=pltpu.SMEM)
-ORDERS = ("xyab", "abyx", "ayxb", "xbay")
+ORDERS = ("xyab", "xyab", "abxy", "xyab")
+TAIL = 5
 CHUNKS = 4
-HOLD = 3
+FINISH = 56
+WAVE = 24
+LAST = 30
+UNROLL = 2
+HOLD = 1
 SUB = 8
 
 
@@ -68,6 +73,9 @@
 
 
 def staged_call(kernel, scalars, ins, outs, extra_outs, scratch, flops, copies, room, chunks=None):
+    views = [one[1] if isinstance(one, tuple) else None for one in ins]
+    ins = [one[0] if isinstance(one, tuple) else one for one in ins]
+    inside = [one.shape if view is None else tuple(at.size for at in view) for one, view in zip(ins, views)]
     n_s, n_i, n_o, n_e = len(scalars), len(ins), len(outs), len(extra_outs)
 
     def body(*refs):
@@ -75,6 +83,7 @@
         for size in (n_s, n_i, n_o, n_e, n_i, n_o, len(scratch)):
             cut.append(cut[-1] + size)
         scalar, source, target, extra, buffer, result, own = [refs[a:b] for a, b in zip(cut, cut[1:])]
+        source = [ref if view is None else ref.at[view] for ref, view in zip(source, views)]
         stage = Staged(source, buffer, target, result, refs[-1], chunks or {})
         kernel(stage, scalar, buffer, result, extra, own)
         stage.finish()
@@ -84,7 +93,7 @@
         in_specs=[SMEM] * n_s + [HBM] * n_i,
         out_specs=(HBM,) * (n_o + n_e),
         out_shape=shaped(*outs, *extra_outs),
-        scratch_shapes=[pltpu.VMEM(a.shape, a.dtype) for a in ins]
+        scratch_shapes=[pltpu.VMEM(shape, a.dtype) for shape, a in zip(inside, ins)]
         + [pltpu.VMEM(shape, kind) for shape, kind in outs]
         + [pltpu.VMEM(shape, kind) for shape, kind in scratch]
         + [pltpu.SemaphoreType.DMA((copies,))],
@@ -252,19 +261,39 @@
         stage.pending += [first, second]
 
 
-def mlp_kernel(stage, scalars, ins, outs, extra, scratch):
+def mlp_blocks(pre_in, up, w_up, w_down, tail, second_grad, for_even, for_odd):
+    block = pre_in.shape[1]
+
+    def part(b, carry):
+        at = pl.ds(pl.multiple_of(b * block, block), block)
+        pre = dot(pre_in[...], w_up[:, at])
+        back = dot_rt(up[...], w_down[at, :])
+        scaled = pre * 0.7071067811865476
+        phi = 0.5 + 0.5 * lax.erf(scaled)
+        active = (pre * phi).astype(BF16)
+        slope = phi + pre * (0.3989422804014327 * jnp.exp(-scaled * scaled))
+        up_low = (slope * back).astype(BF16)
+        for_even[at, :] = dot_lt(active, up[...])
+        for_odd[at, :] = dot_lt(pre_in[...], up_low)
+        tail[...] += dot(active, w_down[at, :])
+        second_grad[...] += dot_rt(up_low, w_up[:, at])
+        return carry
+
+    lax.fori_loop(0, w_down.shape[0] // block, part, 0, unroll=UNROLL)
+
+
+def state_kernel(stage, scalars, ins, outs, extra, scratch):
     (first_len,) = scalars
     carried, subk, subs, keep, drive, cand, gate, x, w_out, gain_two, w_up, w_down, up = ins
-    blend, output, grad_middle_out, grad_gain_two, grad_state, subb, totals = outs
-    mine, other, mine_out, other_out = extra
-    before, low, second_low, tail, second_grad, middle_ref, for_even, for_odd, out_even, out_odd = scratch
+    blend, low, middle_ref, second_low, tail, second_grad = outs
+    mine, other = extra
+    before, for_even, for_odd = scratch
     count, width = x.shape
-    hidden, ff = keep.shape[1], w_up.shape[1]
+    hidden = keep.shape[1]
     rows = carried.shape[0]
-    group_len = count // rows
     parts = SUB // rows
     pairs = count // SUB // 2
-    seq_start = lax.axis_index("seq") * group_len
+    seq_start = lax.axis_index("seq") * (count // rows)
     even = lax.axis_index("row") % 2 == 0
     stage.need(0, 1, 2)
     for r in range(rows):
@@ -289,37 +318,35 @@
     for c in range(CHUNKS):
         stage.need_chunk(c, 3, 4, 5, 6)
         state = lax.fori_loop(c * pairs // CHUNKS, (c + 1) * pairs // CHUNKS, two, state, unroll=2)
-    stage.done(0)
+    stage.done(0, 1)
     stage.need(7, 8, 9)
     middle = x[...].astype(F32) + dot(low[...], w_out[...])
     middle_ref[...] = middle
     second_low[...] = (middle * rms(middle) * gain_two[...]).astype(BF16)
+    stage.done(2, 3)
     tail[...] = jnp.zeros_like(tail)
     second_grad[...] = jnp.zeros_like(second_grad)
     stage.need(10, 11, 12)
-    block = width
-    half = ff // block // 2
-
-    def part(b, carry):
-        at = pl.ds(pl.multiple_of(b * block, block), block)
-        pre = dot(second_low[...], w_up[:, at])
-        back = dot_rt(up[...], w_down[at, :])
-        scaled = pre * 0.7071067811865476
-        phi = 0.5 + 0.5 * lax.erf(scaled)
-        active = (pre * phi).astype(BF16)
-        slope = phi + pre * (0.3989422804014327 * jnp.exp(-scaled * scaled))
-        up_low = (slope * back).astype(BF16)
-        for_even[at, :] = dot_lt(active, up[...])
-        for_odd[at, :] = dot_lt(second_low[...], up_low)
-        tail[...] += dot(active, w_down[at, :])
-        second_grad[...] += dot_rt(up_low, w_up[:, at])
-        return carry
-
-    for k in range(2):
-        lax.fori_loop(k * half, (k + 1) * half, part, 0)
-        at = pl.ds(k * half * block, half * block)
-        give_pair(stage, even, [(for_even.at[at], for_odd.at[at], mine.at[at], other.at[at])])
-
+    mlp_blocks(second_low, up, w_up, w_down, tail, second_grad, for_even, for_odd)
+    stage.done(4, 5)
+    give_pair(stage, even, [(for_even, for_odd, mine, other)])
+
+
+def mlp_kernel(stage, scalars, ins, outs, extra, scratch):
+    second_low, up, w_up, w_down, tail, second_grad, middle_ref, gain_two, w_out, low, keep, subk = ins
+    output, grad_middle_out, grad_gain_two, grad_state, subb, totals = outs
+    mine, other, mine_out, other_out = extra
+    for_even, for_odd, out_even, out_odd = scratch
+    count, width = middle_ref.shape
+    hidden = keep.shape[1]
+    rows = totals.shape[0]
+    parts = SUB // rows
+    pairs = count // SUB // 2
+    even = lax.axis_index("row") % 2 == 0
+    stage.need(0, 1, 2, 3, 4, 5)
+    mlp_blocks(second_low, up, w_up, w_down, tail, second_grad, for_even, for_odd)
+    give_pair(stage, even, [(for_even, for_odd, mine, other)])
+    stage.need(6, 7, 8)
     middle = middle_ref[...]
     scale = rms(middle)
     unit = middle * scale
@@ -328,10 +355,11 @@
     grad = grad * gain_two[...]
     grad_middle = up[...].astype(F32) + scale * (grad - unit * jnp.mean(grad * unit, axis=-1, keepdims=True))
     grad_middle_out[...] = grad_middle
-    stage.done(2, 3)
+    stage.done(1, 2)
     middle_low = grad_middle.astype(BF16)
     grad_state[...] = dot_rt(middle_low, w_out[...])
-    stage.done(4)
+    stage.done(3)
+    stage.need(9, 10, 11)
 
     def back_step(i, passed):
         at = pl.ds(pl.multiple_of((2 * pairs - 1 - i) * SUB, SUB), SUB)
@@ -345,14 +373,14 @@
             at = slice(r * parts + h, r * parts + h + 1)
             b = subb[at, :] + subk[at, :] * b
         totals[r : r + 1, :] = b
-    stage.done(5, 6)
+    stage.done(4, 5)
     half_h = hidden // 2
     out_even[...] = dot_lt(low[:, :half_h], middle_low)
     out_odd[...] = dot_lt(low[:, half_h:], middle_low)
     give_pair(stage, even, [(out_even, out_odd, mine_out, other_out)])
     result = (middle_ref[...] + tail[...]).astype(BF16)
     output[...] = dot_lt(segment_order(count), result).astype(BF16).reshape(output.shape)
-    stage.done(1)
+    stage.done(0)
 
 
 def first_kernel(stage, scalars, ins, outs, extra, scratch):
@@ -360,7 +388,7 @@
     (returned, subk, subb, keep, grad_state, blend, passing, conv_low, w_z, w_h, x_ref, rim, gain_one, conv_weight,
      grad_middle, grad_gain_two) = ins
     grad_tokens, sent, tail_normed, tail_middle = outs
-    mine_a, other_a, mine_b, other_b = extra
+    mine, other = extra
     incoming, gate_low, cand_low, ext, spread, grad_ext, bias_sum, small, for_even, for_odd, rest = scratch
     count, width = x_ref.shape
     hidden = keep.shape[1]
@@ -397,15 +425,10 @@
     bias = carry[1]
     bias_sum[...] = jnp.sum(bias, axis=0, keepdims=True)
     stage.need(7)
-    half = width // 2
     for_even[...] = dot_lt(conv_low[...], gate_low[...])
     for_odd[...] = dot_lt(conv_low[...], cand_low[...])
     cols = pl.ds(0, hidden)
-    low_rows, high_rows = pl.ds(0, half), pl.ds(half, half)
-    give_pair(stage, even, [
-        (for_even.at[low_rows], for_odd.at[low_rows], mine_a, other_a),
-        (for_even.at[high_rows], for_odd.at[high_rows], mine_b.at[:, cols], other_b.at[:, cols]),
-    ])
+    give_pair(stage, even, [(for_even, for_odd, mine.at[:, cols], other.at[:, cols])])
     stage.need(8, 9, 10, 11, 12, 13, 14, 15)
     grad_mixed = dot_rt(gate_low[...], w_z[...]) + dot_rt(cand_low[...], w_h[...])
 
@@ -452,7 +475,7 @@
     for j in range(width // 128):
         rest[j * SUB : (j + 1) * SUB, :] = small[:, j * 128 : (j + 1) * 128]
     past = pl.ds(hidden, 128)
-    give_pair(stage, even, [(rest.at[low_rows], rest.at[high_rows], mine_b.at[:, past], other_b.at[:, past])])
+    give_pair(stage, even, [(rest, rest, mine.at[:, past], other.at[:, past])])
     for k in range(lag):
         at = count - lag * SUB + k * SUB
         for r in range(rows):
@@ -518,17 +541,17 @@
     return before_s, levels
 
 
-def carry_backward(passed, levels):
+def carry_backward(passed, levels, between):
     after_b, after_k = jnp.zeros_like(passed), jnp.ones_like(passed)
-    seen = []
-    for bit, (keep, other_k) in zip(bits_of("seq"), levels):
+    for i, (bit, (keep, other_k)) in enumerate(zip(bits_of("seq"), levels)):
+        if i == HOLD:
+            passed = between(passed)
         other_b = swapped(passed, "seq", bit)
         late = upper("seq", bit)
         after_b = jnp.where(late, after_b, after_b + after_k * other_b)
         after_k = jnp.where(late, after_k, after_k * other_k)
         passed = jnp.where(late, other_b + other_k * passed, passed + keep * other_b)
-        seen.append(passed)
-    return after_b, seen
+    return after_b
 
 
 BOTH = ("row", "seq")
@@ -668,7 +691,7 @@
         out_specs=(ANY,) * len(through) + (VMEM,) * len(shapes),
         out_shape=shaped(*[(array.shape, F32) for array in through], *[(shape, F32) for shape in shapes]),
         input_output_aliases={len(tokens) + i: i for i in range(len(through))},
-        compiler_params=pltpu.CompilerParams(vmem_limit_bytes=24 << 20),
+        compiler_params=pltpu.CompilerParams(vmem_limit_bytes=WAVE << 20),
         cost_estimate=pl.CostEstimate(flops=1, bytes_accessed=1, transcendentals=0),
     )(*tokens, *through, *[array for one in sums for array in (one.mine, one.received)]))
     passed = [outs.pop(0) for _ in through]
@@ -678,10 +701,10 @@
     return first, passed
 
 
-def finish_kernel(steps, routes, total, _, *refs):
+def finish_kernel(steps, routes, total, few, _, *refs):
     count = len(steps)
     arrays, outs = refs[: 4 * count], refs[4 * count : 4 * count + total]
-    buffers, sems = refs[4 * count + total : -1], refs[-1]
+    buffers, sems = refs[4 * count + total : 5 * count + total], refs[-1]
     even = lax.axis_index("row") % 2 == 0
     base, plans = 0, []
     for k, step in enumerate(steps):
@@ -726,17 +749,43 @@
             for i, (source, buffer, target) in enumerate(plan):
                 pltpu.make_async_copy(buffer, target, sems.at[1, first + i]).wait()
 
-
-def finish_call(routes, token, sums, outs):
+    if few:
+        spread_small(outs[2:], refs[5 * count + total :])
+
+
+def spread_small(outs, scratch):
+    packed, *targets = outs
+    tiles, *rows, sems = scratch
+    copy = pltpu.make_async_copy(packed, tiles, sems.at[0, 0])
+    copy.start()
+    copy.wait()
+    width = targets[0].shape[1]
+    line = 0
+    for row in rows:
+        for r in range(row.shape[0]):
+            for j in range(row.shape[1] // 128):
+                at = (line + j * 128 // width, j * 128 % width // 128)
+                source = at[1] * SUB + at[0]
+                row[r : r + 1, j * 128 : (j + 1) * 128] = tiles[source : source + 1, :]
+            line += row.shape[1] // width
+    copies = [pltpu.make_async_copy(row, out, sems.at[1, i]) for i, (row, out) in enumerate(zip(rows, targets))]
+    for copy in copies:
+        copy.start()
+    for copy in copies:
+        copy.wait()
+
+
+def finish_call(routes, token, sums, outs, few=0):
     arrays = [array for one in sums for array in (one.mine, one.received, *one.others)]
     return pl.pallas_call(
-        functools.partial(finish_kernel, [one.steps[0] for one in sums], routes, len(outs)),
+        functools.partial(finish_kernel, [one.steps[0] for one in sums], routes, len(outs), few),
         in_specs=[pl.BlockSpec(memory_space=pl.ANY)] * (1 + len(arrays)),
         out_specs=(HBM,) * len(outs),
         out_shape=shaped(*outs),
         scratch_shapes=[pltpu.VMEM((2, 2) + one.mine.shape, F32) for one in sums]
+        + ([pltpu.VMEM(*out) for out in outs[2:]] if few else [])
         + [pltpu.SemaphoreType.DMA((2, 48))],
-        compiler_params=pltpu.CompilerParams(vmem_limit_bytes=32 << 20),
+        compiler_params=pltpu.CompilerParams(vmem_limit_bytes=FINISH << 20),
         cost_estimate=pl.CostEstimate(flops=1, bytes_accessed=1, transcendentals=0),
     )(token, *arrays)
 
@@ -773,40 +822,57 @@
         56,
     )
     carried, levels = carry_forward(totals)
-    mlp_pair, out_pair = ((ff, width), F32), ((hidden // 2, width), F32)
-    blend, output, grad_middle, grad_gain_two, grad_state, subb, passed, mine_a, other_a, mine_b, other_b = staged_call(
-        mlp_kernel,
+    half_ff = ff // 2
+    mlp_pair, out_pair = ((half_ff, width), F32), ((hidden // 2, width), F32)
+    low_half, high_half, every = pl.ds(0, half_ff), pl.ds(half_ff, half_ff), pl.ds(0, width)
+    blend, low, middle, second_low, tail, second_grad, mine_a, other_a = staged_call(
+        state_kernel,
         [first_len],
-        [carried, subk, subs, keep, drive, cand, gate, x, w_out, gain_two, w_up, w_down, up],
-        [(th, BF16), (tokens.shape, BF16), (tw, F32), ((1, width), F32), (th, F32), ((SUB, hidden), F32),
-         ((rows, hidden), F32)],
-        [mlp_pair, mlp_pair, out_pair, out_pair],
-        [((SUB, hidden), F32), (th, BF16), (tw, BF16), (tw, F32), (tw, F32), (tw, F32),
-         ((ff, width), F32), ((ff, width), F32), ((hidden // 2, width), F32), ((hidden // 2, width), F32)],
-        12 * count * width * ff,
+        [carried, subk, subs, keep, drive, cand, gate, x, w_out, gain_two, (w_up, (every, low_half)),
+         (w_down, (low_half, every)), up],
+        [(th, BF16), (th, BF16), (tw, F32), (tw, BF16), (tw, F32), (tw, F32)],
+        [mlp_pair, mlp_pair],
+        [((SUB, hidden), F32), ((half_ff, width), F32), ((half_ff, width), F32)],
+        6 * count * width * ff,
         64,
         56,
         chunks,
     )
-    returned, seen = carry_backward(passed, levels)
-    early = [Summed(mine_a, other_a, ORDERS[0]), Summed(mine_b, other_b, ORDERS[1])]
-    token, _ = wave([(passed, *seen)[HOLD]], early)
+    output, grad_middle, grad_gain_two, grad_state, subb, passed, mine_b, other_b, mine_c, other_c = staged_call(
+        mlp_kernel,
+        [],
+        [second_low, up, (w_up, (every, high_half)), (w_down, (high_half, every)), tail, second_grad, middle, gain_two,
+         w_out, low, keep, subk],
+        [(tokens.shape, BF16), (tw, F32), ((1, width), F32), (th, F32), ((SUB, hidden), F32), ((rows, hidden), F32)],
+        [mlp_pair, mlp_pair, out_pair, out_pair],
+        [((half_ff, width), F32)] * 2 + [((hidden // 2, width), F32)] * 2,
+        8 * count * width * ff,
+        64,
+        56,
+    )
+    first = Summed(mine_a, other_a, ORDERS[0])
+    early = [Summed(mine_b, other_b, ORDERS[1]), Summed(mine_c, other_c, ORDERS[2])]
+
+    def between(passed):
+        return wave([], [first], [passed])[1][0]
+
+    returned = carry_backward(passed, levels, between)
+    token, (returned,) = wave([], [first] + early, [returned])
     tile = 16
-    pair = ((width // 2, hidden), F32)
-    pair_small = ((width // 2, hidden + 128), F32)
-    grad_tokens, sent, tail_normed, tail_middle, mine_c, other_c, mine_d, other_d = staged_call(
+    pair = ((width, hidden + 128), F32)
+    grad_tokens, sent, tail_normed, tail_middle, mine_d, other_d = staged_call(
         first_kernel,
         [first_len],
         [returned, subk, subb, keep, grad_state, blend, passing, conv_low, w_z, w_h, x, rim, gain_one,
          conv_weight, grad_middle, grad_gain_two],
         [(tokens.shape, BF16), ((rows, lag, width), F32)] + [((rows, tile, width), F32)] * 2,
-        [pair, pair, pair_small, pair_small],
+        [pair, pair],
         [((SUB, hidden), F32), (th, BF16), (th, BF16), ((count + lag * SUB, width), F32),
          ((lag, SUB, width), F32), ((count + lag * SUB, width), F32), ((1, hidden), F32), ((SUB, width), F32),
          ((width, hidden), F32), ((width, hidden), F32), ((width, 128), F32)],
         8 * count * width * hidden,
         64,
-        30,
+        LAST,
         chunks,
     )
     received = lax.ppermute(sent, "seq", [(i + 1, i) for i in range(devices - 1)])
@@ -822,24 +888,22 @@
         scratch_shapes=[pltpu.VMEM((tile, width), F32)],
         input_output_aliases={5: 0},
     )(tokens, tail_normed, tail_middle, received, gain_one, grad_tokens)
-    late = [Summed(mine_c, other_c, ORDERS[2]), Summed(mine_d, other_d, ORDERS[3])]
-    tokens = [[tail_normed], [grad_tokens]]
-    while late[0].busy():
+    late = Summed(mine_d, other_d, ORDERS[3])
+    tokens = [[tail_normed]] + [[]] * (TAIL - 3) + [[grad_tokens]]
+    left = [[first], early]
+    while late.busy():
         more = tokens.pop(0) if tokens else []
-        if early[0].busy():
-            token, _ = wave([token, *more], early + late)
-        else:
-            token, ready = wave([token, *more], late, [one.received for one in early])
-            for one, received in zip(early, ready):
-                one.received = received
-    for one in early:
-        one.across()
-    for one in late:
-        one.across()
-
+        ended = [] if not left or left[0][0].busy() else left.pop(0)
+        running = sum(left, []) + [late]
+        token, ready = wave([token, *more], running, [one.received for one in ended])
+        for one, received in zip(ended, ready):
+            one.received = received
+            one.across()
     def mlp_routes(k, parity, first, rows):
         everything, plan = pl.ds(0, width), []
-        if k == 1:
+        first = first + k * half_ff
+        if k == 2:
+            first = first - ff
             return [(pl.ds(0, rows), everything, 2, (pl.ds(first + parity * hidden // 2, rows), everything))]
         for offset, at, size in cut(first, rows, range(0, ff, width)):
             inner = pl.ds(offset, size)
@@ -850,39 +914,51 @@
                 plan.append((inner, everything, 1, (pl.ds(at - block, size), pl.ds(block, width))))
         return plan
 
+    few = SUB * width // 128
+
     def gate_routes(k, parity, first, rows):
         inner, cols = pl.ds(0, rows), pl.ds(0, hidden)
-        plan = [(inner, cols, parity, (pl.ds(first + k * width // 2, rows), cols))]
-        few = SUB * width // 128
-        if k == 1 and parity == 0 and first < few:
+        plan = [(inner, cols, parity, (pl.ds(first, rows), cols))]
+        if parity == 0 and first < few:
             least = min(rows, few - first)
             at, all_cols = pl.ds(0, least), pl.ds(0, 128)
             plan.append((at, pl.ds(hidden, 128), 2, (pl.ds(first, least), all_cols)))
         return plan
 
     grad_down, grad_up, grad_out = finish_call(
-        mlp_routes, token, early, [((ff, width), F32), ((width, ff), F32), ((hidden, width), F32)]
-    )
-    grad_z, grad_h, small = finish_call(
-        gate_routes, grad_out, late,
-        [((width, hidden), F32), ((width, hidden), F32), ((SUB * width // 128, 128), F32)],
-    )
-    small = small.reshape(width // 128, SUB, 128).swapaxes(0, 1).reshape(SUB, width)
-    bias_at = 2 + lag
-    gain_at = bias_at + hidden // width
+        mlp_routes, token, [first, *early], [((ff, width), F32), ((width, ff), F32), ((hidden, width), F32)]
+    )
+    (late.received,) = held([grad_out], [late.received])
+    late.across()
+    grad_z, grad_h, small, grad_gain_one, grad_conv, grad_bias, grad_gain = finish_call(
+        gate_routes, grad_out, [late],
+        [((width, hidden), F32), ((width, hidden), F32), ((SUB * width // 128, 128), F32), ((1, width), F32),
+         ((lag + 1, width), F32), ((1, hidden), F32), ((1, width), F32)],
+        few,
+    )
     return (
         output,
         grad_tokens,
-        small[0],
-        small[1:bias_at],
+        grad_gain_one.reshape(width),
+        grad_conv,
         grad_z,
-        small[bias_at:gain_at].reshape(hidden),
+        grad_bias.reshape(hidden),
         grad_h,
         grad_out,
-        small[gain_at],
+        grad_gain.reshape(width),
         grad_up,
         grad_down,
     )
+
+
+def held(tokens, arrays):
+    return pl.pallas_call(
+        lambda *_: None,
+        in_specs=[ANY] * (len(tokens) + len(arrays)),
+        out_specs=(ANY,) * len(arrays),
+        out_shape=shaped(*[(array.shape, F32) for array in arrays]),
+        input_output_aliases={len(tokens) + i: i for i in range(len(arrays))},
+    )(*tokens, *arrays)
 
 
 def solution(mesh):

time: 270 us -> 257 us (0.952)
  waiting for transfers between devices: 133 us -> 113 us
  Pallas kernels: 50.4 us -> 58.4 us
  local copies, waits for them, and re-layouts: 15 us -> 9.38 us
  starting transfers between devices: 66.6 us -> 71.9 us
    ppermute x44, waiting for transfers between devices: 108 us -> 93.5 us  [exchanged(): return lax.ppermute(array, BOTH, pairs)]
    ppermute x1, waiting for transfers between devices: 10.7 us -> 4.51 us  [per_device(): lax.ppermute(sent, 'seq', [(i + 1, i) for i in range(devices - 1)])]
    ppermute x44, starting transfers between devices: 46 us -> 52 us  [exchanged(): return lax.ppermute(array, BOTH, pairs)]
    pallas_call x2, Pallas kernels: 8.73 us -> 14.1 us  [finish_call(): pl.pallas_call(functools.partial(finish_kernel, [one.steps[0] for one in...]
    pallas_call x3 -> x4, Pallas kernels: 35.2 us -> 40.1 us  [staged_call(): pl.pallas_call(body, in_specs=[SMEM] * n_s + [HBM] * n_i, out_specs=(HBM,...]
    unnamed x60 -> x80, local copies, waits for them, and re-layouts: 13.8 us -> 9.38 us
  transfers between devices with their start and end apart: 52 -> 52, of which waited for: 30 -> 33; matrix products, arithmetic and copies ran while one was open for 0% -> 0% of each run, Pallas kernels for 6% -> 8%
where the time goes in v4:
time: 257 us
  waiting for transfers between devices  113 us (44%)
  starting transfers between devices  71.9 us (28%)
  Pallas kernels  58.4 us (23%)
  local copies, waits for them, and re-layouts  9.38 us (4%)
  other arithmetic  2.93 us (1%)
    ppermute x44, waiting for transfers between devices, exchanged(): return lax.ppermute(array, BOTH, pairs)  93.5 us
    ppermute x44, starting transfers between devices, exchanged(): return lax.ppermute(array, BOTH, pairs)  52 us
    pallas_call x4, Pallas kernels, staged_call(): pl.pallas_call(body, in_specs=[SMEM] * n_s + [HBM] * n_i, out_specs=(HBM,...  40.1 us
    pallas_call x2, Pallas kernels, finish_call(): pl.pallas_call(functools.partial(finish_kernel, [one.steps[0] for one in...  14.1 us
    ppermute x6, starting transfers between devices, swapped(): lax.ppermute(array, axis, [(i, i ^ bit) for i in range(lax.axis_size(axis...  13.7 us
    ppermute x6, waiting for transfers between devices, swapped(): lax.ppermute(array, axis, [(i, i ^ bit) for i in range(lax.axis_size(axis...  13.1 us
    unnamed x80, local copies, waits for them, and re-layouts  9.38 us
  transfers between devices with their start and end apart: 52, of which 33 were waited for; matrix products, arithmetic and copies ran while one was open for 0% of the time, Pallas kernels for 8%

profile of v4, /device:TPU:0, one launch (start us, length us, event | category | flops | bytes accessed | tf_op | source)
XLA Modules:
  0.0 256.7 jit_solution(5912238904149664486)
XLA Ops:
  1.4 4.8 %collective-permute-start = (f32[4,3,512]{2,1,0:T(4,128)S(1)}, f32[4,3,512]{2,1,0:T(4,128)S(1)}, u32[]{:S(2)}, u32[]{:S(2)}) collective-permute-start(f32[4,3,512]{2,1,0:T(4,128)S(1)} %slice_convert_fusion), channel_id=1, source_target_pairs={{0,1},{1,2},{2,3},{3,4},{4,5},{5,6},{6,7},{8,9},{9,10},{10,11},{11... | collective-permute-start | bytes 73736 | tf_op jit(solution)/shard_map/ppermute | solution.py:807
  6.3 1.6 collective-permute-done.refs_2_.refs_12_
  8.4 7.5 %shard_map.203 = (bf16[512,512]{1,0:T(8,128)(2,1)}, bf16[512,512]{1,0:T(8,128)(2,1)}, f32[512,1024]{1,0:T(8,128)}, f32[512,1024]{1,0:T(8,128)}, f32[512,1024]{1,...) custom-call(s32[4]{0:T(128)} %refs_0_.5, ...), custom_call_target="tpu_custom_call" | custom-call | flops 1073741824 | bytes 8388608 | tf_op jit(solution)/shard_map/pallas_call | solution.py:91
  15.9 2.4 collective-permute-start.1
  18.3 2.1 collective-permute-done.1
  21.2 3.1 %collective-permute-start.2 = (f32[2,4,1024]{2,1,0:T(4,128)S(1)}, f32[2,4,1024]{2,1,0:T(4,128)S(1)}, u32[]{:S(2)}, u32[]{:S(2)}) collective-permute-start(f32[2,4,1024]{2,1,0:T(4,128)S(1)} %pad_maximum_fusion), channel_id=1, source_target_pairs={{0,2},{1,3},{2,0},{3,1},{4,6},{5,7},{6,4},{7,5},{8,10},{9,11},{10,... | collective-permute-start | bytes 98312 | tf_op jit(solution)/shard_map/ppermute | solution.py:513
  24.3 1.9 collective-permute-done.2
  26.2 3.0 %collective-permute-start.3 = (f32[2,4,1024]{2,1,0:T(4,128)S(1)}, f32[2,4,1024]{2,1,0:T(4,128)S(1)}, u32[]{:S(2)}, u32[]{:S(2)}) collective-permute-start(f32[2,4,1024]{2,1,0:T(4,128)S(1)} %pad_maximum_fusion.1), channel_id=1, source_target_pairs={{0,4},{1,5},{2,6},{3,7},{4,0},{5,1},{6,2},{7,3},{8,12},{9,13},{10,... | collective-permute-start | bytes 98312 | tf_op jit(solution)/shard_map/ppermute | solution.py:513
  29.3 1.9 collective-permute-done.3
  31.8 12.9 %shard_map.204 = (bf16[512,1024]{1,0:T(8,128)(2,1)}, bf16[512,1024]{1,0:T(8,128)(2,1)}, f32[512,512]{1,0:T(8,128)}, bf16[512,512]{1,0:T(8,128)(2,1)}, f32[512,51...) custom-call(s32[4]{0:T(128)} %refs_0_.5, f32[4,1024]{1,0:T(4,128)} %add_select_fusion.2.refs_1_, ...), custom_call_target="tpu_custom_call" | custom-call | flops 3221225472 | bytes 8388608 | tf_op jit(solution)/shard_map/pallas_call | solution.py:91
  44.8 10.8 %shard_map.205 = (bf16[4,128,512]{2,1,0:T(8,128)(2,1)}, f32[512,512]{1,0:T(8,128)}, f32[1,512]{1,0:T(1,128)}, f32[512,1024]{1,0:T(8,128)}, f32[8,1024]{1,0:T(8,1...) custom-call(bf16[512,512]{1,0:T(8,128)(2,1)} %get-tuple-element.117., ...), custom_call_target="tpu_custom_call" | custom-call | flops 4294967296 | bytes 8388608 | tf_op jit(solution)/shard_map/pallas_call | solution.py:91
  57.2 3.0 %collective-permute-done.4 = f32[4,1024]{1,0:T(4,128)S(1)} collective-permute-done((f32[4,1024]{1,0:T(4,128)}, f32[4,1024]{1,0:T(4,128)S(1)}, u32[]{:S(2)}, u32[]{:S(2)}) %collective-permute-start.4) | collective-permute-done | bytes 16416 | tf_op jit(solution)/shard_map/ppermute | solution.py:513
  63.8 2.2 collective-permute-done.6
  66.0 2.6 %collective-permute-start.7 = (f32[4,1024]{1,0:T(4,128)S(1)}, f32[4,1024]{1,0:T(4,128)S(1)}, u32[]{:S(2)}, u32[]{:S(2)}) collective-permute-start(f32[4,1024]{1,0:T(4,128)S(1)} %fusion.6), channel_id=1, source_target_pairs={{0,4},{1,5},{2,6},{3,7},{4,0},{5,1},{6,2},{7,3},{8,12},{9,13},{10,... | collective-permute-start | bytes 49160 | tf_op jit(solution)/shard_map/ppermute | solution.py:513
  68.7 2.1 collective-permute-done.7
  70.8 5.4 %collective-permute-done.8.refs_2_ = f32[512,512]{1,0:T(8,128)S(1)} collective-permute-done((f32[512,512]{1,0:T(8,128)S(1)}, f32[512,512]{1,0:T(8,128)S(1)}, u32[]{:S(2)}, u32[]{:S(2)}) %collective-permute-start.8) | collective-permute-done | bytes 1048608 | tf_op jit(solution)/shard_map/ppermute | solution.py:577
  80.7 8.9 %shard_map.208 = (bf16[4,128,512]{2,1,0:T(8,128)(2,1)}, f32[4,3,512]{2,1,0:T(4,128)S(1)}, f32[4,16,512]{2,1,0:T(8,128)S(1)}, f32[4,16,512]{2,1,0:T(8,128)S(1)}, ...) custom-call(s32[4]{0:T(128)S(1)} %copy-done.28, f32[4,1024]{1,0:T(4,128)S(1)} %get-tuple-element.133.refs_1_, ...), custom_call_target="tpu_custom_call" | custom-call | flops 2147483648 | bytes 8388608 | tf_op jit(solution)/shard_map/pallas_call | solution.py:91
  93.8 11.6 %collective-permute-done.14.refs_7_ = f32[256,512]{1,0:T(8,128)S(1)} collective-permute-done((f32[256,512]{1,0:T(8,128)S(1)}, f32[256,512]{1,0:T(8,128)S(1)}, u32[]{:S(2)}, u32[]{:S(2)}) %collective-permute-start.14) | collective-permute-done | bytes 524320 | tf_op jit(solution)/shard_map/ppermute | solution.py:577
  105.5 1.7 collective-permute-done.12.refs_3_
  107.2 3.1 %collective-permute-done.13.refs_5_ = f32[512,512]{1,0:T(8,128)S(1)} collective-permute-done((f32[512,512]{1,0:T(8,128)S(1)}, f32[512,512]{1,0:T(8,128)S(1)}, u32[]{:S(2)}, u32[]{:S(2)}) %collective-permute-start.13) | collective-permute-done | bytes 1048608 | tf_op jit(solution)/shard_map/ppermute | solution.py:577
  113.3 2.6 %collective-permute-start.18 = (f32[128,512]{1,0:T(8,128)S(1)}, f32[128,512]{1,0:T(8,128)S(1)}, u32[]{:S(2)}, u32[]{:S(2)}) collective-permute-start(f32[128,512]{1,0:T(8,128)S(1)} %get-tuple-element.158), channel_id=1, source_target_pairs={{0,4},{1,5},{2,6},{3,7},{4,0},{5,1},{6,2},{7,3},{8,12},{9,13},{10,... | collective-permute-start | bytes 786440 | tf_op jit(solution)/shard_map/ppermute | solution.py:577
  117.4 9.8 %collective-permute-done.18.refs_6_ = f32[128,512]{1,0:T(8,128)S(1)} collective-permute-done((f32[128,512]{1,0:T(8,128)S(1)}, f32[128,512]{1,0:T(8,128)S(1)}, u32[]{:S(2)}, u32[]{:S(2)}) %collective-permute-start.18) | collective-permute-done | bytes 262176 | tf_op jit(solution)/shard_map/ppermute | solution.py:577
  127.2 5.4 %collective-permute-done.19.refs_8_ = f32[256,1152]{1,0:T(8,128)S(1)} collective-permute-done((f32[256,1152]{1,0:T(8,128)S(1)}, f32[256,1152]{1,0:T(8,128)S(1)}, u32[]{:S(2)}, u32[]{:S(2)}) %collective-permute-start.19) | collective-permute-done | bytes 1179680 | tf_op jit(solution)/shard_map/ppermute | solution.py:577
  133.3 2.0 collective-permute-start.21
  135.8 2.8 %collective-permute-start.20 = (f32[64,512]{1,0:T(8,128)S(1)}, f32[64,512]{1,0:T(8,128)S(1)}, u32[]{:S(2)}, u32[]{:S(2)}) collective-permute-start(f32[64,512]{1,0:T(8,128)S(1)} %get-tuple-element.161.refs_0_), channel_id=1, source_target_pairs={{0,4},{1,5},{2,6},{3,7},{4,0},{5,1},{6,2},{7,3},{8,12},{9,13},{10,... | collective-permute-start | bytes 393224 | tf_op jit(solution)/shard_map/ppermute | solution.py:577
  138.7 3.1 %collective-permute-done.22.refs_6_ = f32[64,512]{1,0:T(8,128)S(1)} collective-permute-done((f32[64,512]{1,0:T(8,128)S(1)}, f32[64,512]{1,0:T(8,128)S(1)}, u32[]{:S(2)}, u32[]{:S(2)}) %collective-permute-start.22) | collective-permute-done | bytes 131104 | tf_op jit(solution)/shard_map/ppermute | solution.py:577
  144.1 2.1 collective-permute-start.27
  146.2 1.7 collective-permute-start.25
  152.0 4.5 %collective-permute-done.11.received = f32[4,3,512]{2,1,0:T(4,128)S(1)} collective-permute-done((f32[4,3,512]{2,1,0:T(4,128)S(1)}, f32[4,3,512]{2,1,0:T(4,128)S(1)}, u32[]{:S(2)}, u32[]{:S(2)}) %collective-permute-start.11) | collective-permute-done | bytes 24608 | tf_op jit(solution)/shard_map/ppermute | solution.py:878
  157.1 1.9 shard_map.209.refs_1_
  161.5 2.3 collective-permute-start.31
  166.0 2.8 %collective-permute-done.30.refs_6_ = f32[32,512]{1,0:T(8,128)S(1)} collective-permute-done((f32[32,512]{1,0:T(8,128)S(1)}, f32[32,512]{1,0:T(8,128)S(1)}, u32[]{:S(2)}, u32[]{:S(2)}) %collective-permute-start.30) | collective-permute-done | bytes 65568 | tf_op jit(solution)/shard_map/ppermute | solution.py:577
  168.8 5.8 %collective-permute-done.29.refs_4_ = f32[64,512]{1,0:T(8,128)S(1)} collective-permute-done((f32[64,512]{1,0:T(8,128)S(1)}, f32[64,512]{1,0:T(8,128)S(1)}, u32[]{:S(2)}, u32[]{:S(2)}) %collective-permute-start.29) | collective-permute-done | bytes 131104 | tf_op jit(solution)/shard_map/ppermute | solution.py:577
  174.6 2.4 collective-permute-start.32
  177.1 2.3 collective-permute-start.35
  179.3 3.4 %collective-permute-start.34 = (f32[64,512]{1,0:T(8,128)S(1)}, f32[64,512]{1,0:T(8,128)S(1)}, u32[]{:S(2)}, u32[]{:S(2)}) collective-permute-start(f32[64,512]{1,0:T(8,128)S(1)} %get-tuple-element.183.refs_5_), channel_id=1, source_target_pairs={{0,1},{1,0},{2,3},{3,2},{4,5},{5,4},{6,7},{7,6},{8,24},{9,25},{10,... | collective-permute-start | bytes 393224 | tf_op jit(solution)/shard_map/ppermute | solution.py:577
  182.7 2.9 %collective-permute-done.34.refs_6_ = f32[64,512]{1,0:T(8,128)S(1)} collective-permute-done((f32[64,512]{1,0:T(8,128)S(1)}, f32[64,512]{1,0:T(8,128)S(1)}, u32[]{:S(2)}, u32[]{:S(2)}) %collective-permute-start.34) | collective-permute-done | bytes 131104 | tf_op jit(solution)/shard_map/ppermute | solution.py:577
  185.9 3.6 %collective-permute-start.36 = (f32[512,512]{1,0:T(8,128)S(1)}, f32[512,512]{1,0:T(8,128)S(1)}, u32[]{:S(2)}, u32[]{:S(2)}) collective-permute-start(f32[512,512]{1,0:T(8,128)S(1)} %get-tuple-element.185.refs_0_), channel_id=1, source_target_pairs={{0,1},{1,0},{2,3},{3,2},{4,5},{5,4},{6,7},{7,6},{8,24},{9,25},{10,... | collective-permute-start | bytes 3145736 | tf_op jit(solution)/shard_map/ppermute | solution.py:577
  189.5 2.3 collective-permute-start.37
  192.6 1.7 collective-permute-start.38
  194.3 11.5 %collective-permute-done.38.refs_5_ = f32[128,512]{1,0:T(8,128)S(1)} collective-permute-done((f32[128,512]{1,0:T(8,128)S(1)}, f32[128,512]{1,0:T(8,128)S(1)}, u32[]{:S(2)}, u32[]{:S(2)}) %collective-permute-start.38) | collective-permute-done | bytes 262176 | tf_op jit(solution)/shard_map/ppermute | solution.py:577
  208.1 3.6 %collective-permute-start.41 = (f32[256,512]{1,0:T(8,128)S(1)}, f32[256,512]{1,0:T(8,128)S(1)}, u32[]{:S(2)}, u32[]{:S(2)}) collective-permute-start(f32[256,512]{1,0:T(8,128)S(1)} %get-tuple-element.190.refs_8_), channel_id=1, source_target_pairs={{0,2},{1,3},{2,0},{3,1},{4,6},{5,7},{6,4},{7,5},{8,10},{9,11},{10,... | collective-permute-start | bytes 1572872 | tf_op jit(solution)/shard_map/ppermute | solution.py:577
  211.7 12.2 %collective-permute-done.41.refs_2_ = f32[256,512]{1,0:T(8,128)S(1)} collective-permute-done((f32[256,512]{1,0:T(8,128)S(1)}, f32[256,512]{1,0:T(8,128)S(1)}, u32[]{:S(2)}, u32[]{:S(2)}) %collective-permute-start.41) | collective-permute-done | bytes 524320 | tf_op jit(solution)/shard_map/ppermute | solution.py:577
  224.0 4.4 %collective-permute-done.40.refs_1_ = f32[512,512]{1,0:T(8,128)S(1)} collective-permute-done((f32[512,512]{1,0:T(8,128)S(1)}, f32[512,512]{1,0:T(8,128)S(1)}, u32[]{:S(2)}, u32[]{:S(2)}) %collective-permute-start.40) | collective-permute-done | bytes 1048608 | tf_op jit(solution)/shard_map/ppermute | solution.py:577
  231.1 2.9 %collective-permute-done.44.refs_3_ = f32[512,512]{1,0:T(8,128)S(1)} collective-permute-done((f32[512,512]{1,0:T(8,128)S(1)}, f32[512,512]{1,0:T(8,128)S(1)}, u32[]{:S(2)}, u32[]{:S(2)}) %collective-permute-start.44) | collective-permute-done | bytes 1048608 | tf_op jit(solution)/shard_map/ppermute | solution.py:577
  237.3 8.7 %shard_map.218 = (f32[2048,512]{1,0:T(8,128)}, f32[512,2048]{1,0:T(8,128)}, f32[1024,512]{1,0:T(8,128)}) custom-call(f32[256,1152]{1,0:T(8,128)} %copy-done.1, f32[512,512]{1,0:T(8,128)} %copy-done.2, f32[512,512]{1,0:T(8,128)} %copy-done.4, f32[512,512]{1,0:T(8,128)} %copy-done.33, f32[512,512]{1,0:T(8,128)} %copy-done.34, f32[512,512]{1,0:T(8,128)} %copy-done.3, ...), custom_call_target="tpu_custom_call" | custom-call | flops 1 | bytes 1 | tf_op jit(solution)/shard_map/pallas_call | solution.py:780
  247.1 2.9 %collective-permute-done.51.refs_3_ = f32[256,1152]{1,0:T(8,128)S(1)} collective-permute-done((f32[256,1152]{1,0:T(8,128)}, f32[256,1152]{1,0:T(8,128)S(1)}, u32[]{:S(2)}, u32[]{:S(2)}) %collective-permute-start.51) | collective-permute-done | bytes 1179680 | tf_op jit(solution)/shard_map/ppermute | solution.py:577
  251.1 5.4 %shard_map.220 = (f32[512,1024]{1,0:T(8,128)}, f32[512,1024]{1,0:T(8,128)}, f32[32,128]{1,0:T(8,128)}, f32[1,512]{1,0:T(1,128)}, f32[4,512]{1,0:T(4,128)}, /*index=5*/f32[1,1024]{1,0:T(1,128)}, f32[1,512]{1,0:T(1,128)}) custom-call(f32[1024,512]{1,0:T(8,128)} %get-tuple-element.104.__0_._, f32[256,1152]{1,0:T(8,128)} %copy-done.1, ...), custom_call_target="tpu_custom_call" | custom-call | flops 1 | bytes 1 | tf_op jit(solution)/shard_map/pallas_call | solution.py:780
  (163 shorter events, 45.5 us)
Async XLA Ops:
  1.4 6.4 %collective-permute-start = (f32[4,3,512]{2,1,0:T(4,128)S(1)}, f32[4,3,512]{2,1,0:T(4,128)S(1)}, u32[]{:S(2)}, u32[]{:S(2)}) collective-permute-start(f32[4,3,512]{2,1,0:T(4,128)S(1)} %slice_convert_fusion), channel_id=1, source_target_pairs={{0,1},{1,2},{2,3},{3,4},{4,5},{5,6},{6,7},{8,9},{9,10},{10,11},{11... | collective-permute-start | bytes 73736 | tf_op jit(solution)/shard_map/ppermute | solution.py:807
  15.9 4.5 %collective-permute-start.1 = (f32[2,4,1024]{2,1,0:T(4,128)}, f32[2,4,1024]{2,1,0:T(4,128)S(1)}, u32[]{:S(2)}, u32[]{:S(2)}) collective-permute-start(f32[2,4,1024]{2,1,0:T(4,128)} %get-tuple-element.108), channel_id=1, source_target_pairs={{0,1},{1,0},{2,3},{3,2},{4,5},{5,4},{6,7},{7,6},{8,9},{9,8},{10,11... | collective-permute-start | bytes 98312 | tf_op jit(solution)/shard_map/ppermute | solution.py:513
  21.2 5.0 %collective-permute-start.2 = (f32[2,4,1024]{2,1,0:T(4,128)S(1)}, f32[2,4,1024]{2,1,0:T(4,128)S(1)}, u32[]{:S(2)}, u32[]{:S(2)}) collective-permute-start(f32[2,4,1024]{2,1,0:T(4,128)S(1)} %pad_maximum_fusion), channel_id=1, source_target_pairs={{0,2},{1,3},{2,0},{3,1},{4,6},{5,7},{6,4},{7,5},{8,10},{9,11},{10,... | collective-permute-start | bytes 98312 | tf_op jit(solution)/shard_map/ppermute | solution.py:513
  26.2 4.9 %collective-permute-start.3 = (f32[2,4,1024]{2,1,0:T(4,128)S(1)}, f32[2,4,1024]{2,1,0:T(4,128)S(1)}, u32[]{:S(2)}, u32[]{:S(2)}) collective-permute-start(f32[2,4,1024]{2,1,0:T(4,128)S(1)} %pad_maximum_fusion.1), channel_id=1, source_target_pairs={{0,4},{1,5},{2,6},{3,7},{4,0},{5,1},{6,2},{7,3},{8,12},{9,13},{10,... | collective-permute-start | bytes 98312 | tf_op jit(solution)/shard_map/ppermute | solution.py:513
  44.7 16.2 %collective-permute-start.5 = (f32[1024,512]{1,0:T(8,128)}, f32[1024,512]{1,0:T(8,128)S(1)}, u32[]{:S(2)}, u32[]{:S(2)}) collective-permute-start(f32[1024,512]{1,0:T(8,128)} %get-tuple-element.125), channel_id=1, source_target_pairs={{0,8},{1,9},{2,10},{3,11},{4,12},{5,13},{6,14},{7,15},{8,0},{9,1},... | collective-permute-start | bytes 6291464 | tf_op jit(solution)/shard_map/ppermute | solution.py:577
  55.7 15.1 %collective-permute-start.9 = (f32[1024,512]{1,0:T(8,128)}, f32[1024,512]{1,0:T(8,128)S(1)}, u32[]{:S(2)}, u32[]{:S(2)}) collective-permute-start(f32[1024,512]{1,0:T(8,128)} %get-tuple-element.130), channel_id=1, source_target_pairs={{0,8},{1,9},{2,10},{3,11},{4,12},{5,13},{6,14},{7,15},{8,0},{9,1},... | collective-permute-start | bytes 6291464 | tf_op jit(solution)/shard_map/ppermute | solution.py:577
  57.2 13.6 %collective-permute-start.10 = (f32[512,512]{1,0:T(8,128)}, f32[512,512]{1,0:T(8,128)S(1)}, u32[]{:S(2)}, u32[]{:S(2)}) collective-permute-start(f32[512,512]{1,0:T(8,128)} %get-tuple-element.132), channel_id=1, source_target_pairs={{0,8},{1,9},{2,10},{3,11},{4,12},{5,13},{6,14},{7,15},{8,0},{9,1},... | collective-permute-start | bytes 3145736 | tf_op jit(solution)/shard_map/ppermute | solution.py:577
  61.3 14.9 %collective-permute-start.8 = (f32[512,512]{1,0:T(8,128)S(1)}, f32[512,512]{1,0:T(8,128)S(1)}, u32[]{:S(2)}, u32[]{:S(2)}) collective-permute-start(f32[512,512]{1,0:T(8,128)S(1)} %get-tuple-element.128), channel_id=1, source_target_pairs={{0,1},{1,0},{2,3},{3,2},{4,5},{5,4},{6,7},{7,6},{8,24},{9,25},{10,... | collective-permute-start | bytes 3145736 | tf_op jit(solution)/shard_map/ppermute | solution.py:577
  66.0 4.7 %collective-permute-start.7 = (f32[4,1024]{1,0:T(4,128)S(1)}, f32[4,1024]{1,0:T(4,128)S(1)}, u32[]{:S(2)}, u32[]{:S(2)}) collective-permute-start(f32[4,1024]{1,0:T(4,128)S(1)} %fusion.6), channel_id=1, source_target_pairs={{0,4},{1,5},{2,6},{3,7},{4,0},{5,1},{6,2},{7,3},{8,12},{9,13},{10,... | collective-permute-start | bytes 49160 | tf_op jit(solution)/shard_map/ppermute | solution.py:513
  89.7 20.6 %collective-permute-start.15 = (f32[512,1152]{1,0:T(8,128)S(1)}, f32[512,1152]{1,0:T(8,128)S(1)}, u32[]{:S(2)}, u32[]{:S(2)}) collective-permute-start(f32[512,1152]{1,0:T(8,128)S(1)} %get-tuple-element.152), channel_id=1, source_target_pairs={{0,8},{1,9},{2,10},{3,11},{4,12},{5,13},{6,14},{7,15},{8,0},{9,1},... | collective-permute-start | bytes 7077896 | tf_op jit(solution)/shard_map/ppermute | solution.py:577
  89.7 20.5 %collective-permute-start.13 = (f32[512,512]{1,0:T(8,128)S(1)}, f32[512,512]{1,0:T(8,128)S(1)}, u32[]{:S(2)}, u32[]{:S(2)}) collective-permute-start(f32[512,512]{1,0:T(8,128)S(1)} %get-tuple-element.148), channel_id=1, source_target_pairs={{0,1},{1,0},{2,3},{3,2},{4,5},{5,4},{6,7},{7,6},{8,24},{9,25},{10,... | collective-permute-start | bytes 3145736 | tf_op jit(solution)/shard_map/ppermute | solution.py:577
  90.7 14.7 %collective-permute-start.14 = (f32[256,512]{1,0:T(8,128)S(1)}, f32[256,512]{1,0:T(8,128)S(1)}, u32[]{:S(2)}, u32[]{:S(2)}) collective-permute-start(f32[256,512]{1,0:T(8,128)S(1)} %get-tuple-element.150), channel_id=1, source_target_pairs={{0,2},{1,3},{2,0},{3,1},{4,6},{5,7},{6,4},{7,5},{8,10},{9,11},{10,... | collective-permute-start | bytes 1572872 | tf_op jit(solution)/shard_map/ppermute | solution.py:577
  92.3 14.9 %collective-permute-start.12 = (f32[256,512]{1,0:T(8,128)S(1)}, f32[256,512]{1,0:T(8,128)S(1)}, u32[]{:S(2)}, u32[]{:S(2)}) collective-permute-start(f32[256,512]{1,0:T(8,128)S(1)} %get-tuple-element.145.refs_0_), channel_id=1, source_target_pairs={{0,16},{1,17},{2,18},{3,19},{4,20},{5,21},{6,22},{7,23},{8,9},{9,8... | collective-permute-start | bytes 1572872 | tf_op jit(solution)/shard_map/ppermute | solution.py:577
  110.8 21.8 %collective-permute-start.19 = (f32[256,1152]{1,0:T(8,128)S(1)}, f32[256,1152]{1,0:T(8,128)S(1)}, u32[]{:S(2)}, u32[]{:S(2)}) collective-permute-start(f32[256,1152]{1,0:T(8,128)S(1)} %get-tuple-element.160), channel_id=1, source_target_pairs={{0,1},{1,0},{2,3},{3,2},{4,5},{5,4},{6,7},{7,6},{8,24},{9,25},{10,... | collective-permute-start | bytes 3538952 | tf_op jit(solution)/shard_map/ppermute | solution.py:577
  111.8 15.4 %collective-permute-start.17 = (f32[256,512]{1,0:T(8,128)S(1)}, f32[256,512]{1,0:T(8,128)S(1)}, u32[]{:S(2)}, u32[]{:S(2)}) collective-permute-start(f32[256,512]{1,0:T(8,128)S(1)} %get-tuple-element.156), channel_id=1, source_target_pairs={{0,16},{1,17},{2,18},{3,19},{4,20},{5,21},{6,22},{7,23},{8,9},{9,8... | collective-permute-start | bytes 1572872 | tf_op jit(solution)/shard_map/ppermute | solution.py:577
  113.3 13.8 %collective-permute-start.18 = (f32[128,512]{1,0:T(8,128)S(1)}, f32[128,512]{1,0:T(8,128)S(1)}, u32[]{:S(2)}, u32[]{:S(2)}) collective-permute-start(f32[128,512]{1,0:T(8,128)S(1)} %get-tuple-element.158), channel_id=1, source_target_pairs={{0,4},{1,5},{2,6},{3,7},{4,0},{5,1},{6,2},{7,3},{8,12},{9,13},{10,... | collective-permute-start | bytes 786440 | tf_op jit(solution)/shard_map/ppermute | solution.py:577
  115.9 11.3 %collective-permute-start.16 = (f32[128,512]{1,0:T(8,128)S(1)}, f32[128,512]{1,0:T(8,128)S(1)}, u32[]{:S(2)}, u32[]{:S(2)}) collective-permute-start(f32[128,512]{1,0:T(8,128)S(1)} %get-tuple-element.153.refs_0_), channel_id=1, source_target_pairs={{0,2},{1,3},{2,0},{3,1},{4,6},{5,7},{6,4},{7,5},{8,10},{9,11},{10,... | collective-permute-start | bytes 786440 | tf_op jit(solution)/shard_map/ppermute | solution.py:577
  132.8 11.1 %collective-permute-start.23 = (f32[128,1152]{1,0:T(8,128)S(1)}, f32[128,1152]{1,0:T(8,128)S(1)}, u32[]{:S(2)}, u32[]{:S(2)}) collective-permute-start(f32[128,1152]{1,0:T(8,128)S(1)} %get-tuple-element.168), channel_id=1, source_target_pairs={{0,16},{1,17},{2,18},{3,19},{4,20},{5,21},{6,22},{7,23},{8,9},{9,8... | collective-permute-start | bytes 1769480 | tf_op jit(solution)/shard_map/ppermute | solution.py:577
  133.3 10.0 %collective-permute-start.21 = (f32[128,512]{1,0:T(8,128)S(1)}, f32[128,512]{1,0:T(8,128)S(1)}, u32[]{:S(2)}, u32[]{:S(2)}) collective-permute-start(f32[128,512]{1,0:T(8,128)S(1)} %get-tuple-element.164), channel_id=1, source_target_pairs={{0,2},{1,3},{2,0},{3,1},{4,6},{5,7},{6,4},{7,5},{8,10},{9,11},{10,... | collective-permute-start | bytes 786440 | tf_op jit(solution)/shard_map/ppermute | solution.py:577
  135.3 6.4 %collective-permute-start.22 = (f32[64,512]{1,0:T(8,128)S(1)}, f32[64,512]{1,0:T(8,128)S(1)}, u32[]{:S(2)}, u32[]{:S(2)}) collective-permute-start(f32[64,512]{1,0:T(8,128)S(1)} %get-tuple-element.166), channel_id=1, source_target_pairs={{0,1},{1,0},{2,3},{3,2},{4,5},{5,4},{6,7},{7,6},{8,24},{9,25},{10,... | collective-permute-start | bytes 393224 | tf_op jit(solution)/shard_map/ppermute | solution.py:577
  135.8 7.2 %collective-permute-start.20 = (f32[64,512]{1,0:T(8,128)S(1)}, f32[64,512]{1,0:T(8,128)S(1)}, u32[]{:S(2)}, u32[]{:S(2)}) collective-permute-start(f32[64,512]{1,0:T(8,128)S(1)} %get-tuple-element.161.refs_0_), channel_id=1, source_target_pairs={{0,4},{1,5},{2,6},{3,7},{4,0},{5,1},{6,2},{7,3},{8,12},{9,13},{10,... | collective-permute-start | bytes 393224 | tf_op jit(solution)/shard_map/ppermute | solution.py:577
  144.1 16.2 %collective-permute-start.27 = (f32[64,1152]{1,0:T(8,128)S(1)}, f32[64,1152]{1,0:T(8,128)S(1)}, u32[]{:S(2)}, u32[]{:S(2)}) collective-permute-start(f32[64,1152]{1,0:T(8,128)S(1)} %get-tuple-element.175), channel_id=1, source_target_pairs={{0,2},{1,3},{2,0},{3,1},{4,6},{5,7},{6,4},{7,5},{8,10},{9,11},{10,... | collective-permute-start | bytes 884744 | tf_op jit(solution)/shard_map/ppermute | solution.py:577
  146.2 12.7 %collective-permute-start.25 = (f32[64,512]{1,0:T(8,128)S(1)}, f32[64,512]{1,0:T(8,128)S(1)}, u32[]{:S(2)}, u32[]{:S(2)}) collective-permute-start(f32[64,512]{1,0:T(8,128)S(1)} %get-tuple-element.171), channel_id=1, source_target_pairs={{0,4},{1,5},{2,6},{3,7},{4,0},{5,1},{6,2},{7,3},{8,12},{9,13},{10,... | collective-permute-start | bytes 393224 | tf_op jit(solution)/shard_map/ppermute | solution.py:577
  148.0 12.4 %collective-permute-start.24 = (f32[64,512]{1,0:T(8,128)S(1)}, f32[64,512]{1,0:T(8,128)S(1)}, u32[]{:S(2)}, u32[]{:S(2)}) collective-permute-start(f32[64,512]{1,0:T(8,128)S(1)} %get-tuple-element.169.refs_0_.refs_2_), channel_id=1, source_target_pairs={{0,4},{1,5},{2,6},{3,7},{4,0},{5,1},{6,2},{7,3},{8,12},{9,13},{10,... | collective-permute-start | bytes 393224 | tf_op jit(solution)/shard_map/ppermute | solution.py:577
  149.2 9.8 %collective-permute-start.26 = (f32[32,512]{1,0:T(8,128)S(1)}, f32[32,512]{1,0:T(8,128)S(1)}, u32[]{:S(2)}, u32[]{:S(2)}) collective-permute-start(f32[32,512]{1,0:T(8,128)S(1)} %get-tuple-element.173), channel_id=1, source_target_pairs={{0,16},{1,17},{2,18},{3,19},{4,20},{5,21},{6,22},{7,23},{8,9},{9,8... | collective-permute-start | bytes 196616 | tf_op jit(solution)/shard_map/ppermute | solution.py:577
  150.7 5.8 %collective-permute-start.11 = (f32[4,3,512]{2,1,0:T(4,128)S(1)}, f32[4,3,512]{2,1,0:T(4,128)S(1)}, u32[]{:S(2)}, u32[]{:S(2)}) collective-permute-start(f32[4,3,512]{2,1,0:T(4,128)S(1)} %get-tuple-element.143), channel_id=1, source_target_pairs={{1,0},{2,1},{3,2},{4,3},{5,4},{6,5},{7,6},{9,8},{10,9},{11,10},{12... | collective-permute-start | bytes 73736 | tf_op jit(solution)/shard_map/ppermute | solution.py:878
  161.4 13.1 %collective-permute-start.28 = (f32[128,512]{1,0:T(8,128)S(1)}, f32[128,512]{1,0:T(8,128)S(1)}, u32[]{:S(2)}, u32[]{:S(2)}) collective-permute-start(f32[128,512]{1,0:T(8,128)S(1)} %get-tuple-element.176.refs_0_.refs_1_), channel_id=1, source_target_pairs={{0,2},{1,3},{2,0},{3,1},{4,6},{5,7},{6,4},{7,5},{8,10},{9,11},{10,... | collective-permute-start | bytes 786440 | tf_op jit(solution)/shard_map/ppermute | solution.py:577
  161.5 13.0 %collective-permute-start.31 = (f32[32,1152]{1,0:T(8,128)S(1)}, f32[32,1152]{1,0:T(8,128)S(1)}, u32[]{:S(2)}, u32[]{:S(2)}) collective-permute-start(f32[32,1152]{1,0:T(8,128)S(1)} %get-tuple-element.180), channel_id=1, source_target_pairs={{0,4},{1,5},{2,6},{3,7},{4,0},{5,1},{6,2},{7,3},{8,12},{9,13},{10,... | collective-permute-start | bytes 442376 | tf_op jit(solution)/shard_map/ppermute | solution.py:577
  163.9 10.7 %collective-permute-start.29 = (f32[64,512]{1,0:T(8,128)S(1)}, f32[64,512]{1,0:T(8,128)S(1)}, u32[]{:S(2)}, u32[]{:S(2)}) collective-permute-start(f32[64,512]{1,0:T(8,128)S(1)} %get-tuple-element.177.refs_3_), channel_id=1, source_target_pairs={{0,4},{1,5},{2,6},{3,7},{4,0},{5,1},{6,2},{7,3},{8,12},{9,13},{10,... | collective-permute-start | bytes 393224 | tf_op jit(solution)/shard_map/ppermute | solution.py:577
  164.5 4.3 %collective-permute-start.30 = (f32[32,512]{1,0:T(8,128)S(1)}, f32[32,512]{1,0:T(8,128)S(1)}, u32[]{:S(2)}, u32[]{:S(2)}) collective-permute-start(f32[32,512]{1,0:T(8,128)S(1)} %get-tuple-element.178.refs_5_), channel_id=1, source_target_pairs={{0,16},{1,17},{2,18},{3,19},{4,20},{5,21},{6,22},{7,23},{8,9},{9,8... | collective-permute-start | bytes 196616 | tf_op jit(solution)/shard_map/ppermute | solution.py:577
  174.6 11.0 %collective-permute-start.32 = (f32[256,512]{1,0:T(8,128)S(1)}, f32[256,512]{1,0:T(8,128)S(1)}, u32[]{:S(2)}, u32[]{:S(2)}) collective-permute-start(f32[256,512]{1,0:T(8,128)S(1)} %get-tuple-element.181.refs_0_.refs_1_), channel_id=1, source_target_pairs={{0,16},{1,17},{2,18},{3,19},{4,20},{5,21},{6,22},{7,23},{8,9},{9,8... | collective-permute-start | bytes 1572872 | tf_op jit(solution)/shard_map/ppermute | solution.py:577
  177.1 8.6 %collective-permute-start.33 = (f32[128,512]{1,0:T(8,128)S(1)}, f32[128,512]{1,0:T(8,128)S(1)}, u32[]{:S(2)}, u32[]{:S(2)}) collective-permute-start(f32[128,512]{1,0:T(8,128)S(1)} %get-tuple-element.182.refs_3_), channel_id=1, source_target_pairs={{0,2},{1,3},{2,0},{3,1},{4,6},{5,7},{6,4},{7,5},{8,10},{9,11},{10,... | collective-permute-start | bytes 786440 | tf_op jit(solution)/shard_map/ppermute | solution.py:577
  177.1 8.6 %collective-permute-start.35 = (f32[32,1152]{1,0:T(8,128)S(1)}, f32[32,1152]{1,0:T(8,128)S(1)}, u32[]{:S(2)}, u32[]{:S(2)}) collective-permute-start(f32[32,1152]{1,0:T(8,128)S(1)} %get-tuple-element.184.refs_7_), channel_id=1, source_target_pairs={{0,4},{1,5},{2,6},{3,7},{4,0},{5,1},{6,2},{7,3},{8,12},{9,13},{10,... | collective-permute-start | bytes 442376 | tf_op jit(solution)/shard_map/ppermute | solution.py:577
  179.3 6.3 %collective-permute-start.34 = (f32[64,512]{1,0:T(8,128)S(1)}, f32[64,512]{1,0:T(8,128)S(1)}, u32[]{:S(2)}, u32[]{:S(2)}) collective-permute-start(f32[64,512]{1,0:T(8,128)S(1)} %get-tuple-element.183.refs_5_), channel_id=1, source_target_pairs={{0,1},{1,0},{2,3},{3,2},{4,5},{5,4},{6,7},{7,6},{8,24},{9,25},{10,... | collective-permute-start | bytes 393224 | tf_op jit(solution)/shard_map/ppermute | solution.py:577
  185.9 21.2 %collective-permute-start.36 = (f32[512,512]{1,0:T(8,128)S(1)}, f32[512,512]{1,0:T(8,128)S(1)}, u32[]{:S(2)}, u32[]{:S(2)}) collective-permute-start(f32[512,512]{1,0:T(8,128)S(1)} %get-tuple-element.185.refs_0_), channel_id=1, source_target_pairs={{0,1},{1,0},{2,3},{3,2},{4,5},{5,4},{6,7},{7,6},{8,24},{9,25},{10,... | collective-permute-start | bytes 3145736 | tf_op jit(solution)/shard_map/ppermute | solution.py:577
  189.5 16.3 %collective-permute-start.37 = (f32[256,512]{1,0:T(8,128)S(1)}, f32[256,512]{1,0:T(8,128)S(1)}, u32[]{:S(2)}, u32[]{:S(2)}) collective-permute-start(f32[256,512]{1,0:T(8,128)S(1)} %get-tuple-element.186.refs_2_), channel_id=1, source_target_pairs={{0,16},{1,17},{2,18},{3,19},{4,20},{5,21},{6,22},{7,23},{8,9},{9,8... | collective-permute-start | bytes 1572872 | tf_op jit(solution)/shard_map/ppermute | solution.py:577
  191.9 13.9 %collective-permute-start.39 = (f32[64,1152]{1,0:T(8,128)S(1)}, f32[64,1152]{1,0:T(8,128)S(1)}, u32[]{:S(2)}, u32[]{:S(2)}) collective-permute-start(f32[64,1152]{1,0:T(8,128)S(1)} %get-tuple-element.188.refs_6_), channel_id=1, source_target_pairs={{0,2},{1,3},{2,0},{3,1},{4,6},{5,7},{6,4},{7,5},{8,10},{9,11},{10,... | collective-permute-start | bytes 884744 | tf_op jit(solution)/shard_map/ppermute | solution.py:577
  192.6 13.2 %collective-permute-start.38 = (f32[128,512]{1,0:T(8,128)S(1)}, f32[128,512]{1,0:T(8,128)S(1)}, u32[]{:S(2)}, u32[]{:S(2)}) collective-permute-start(f32[128,512]{1,0:T(8,128)S(1)} %get-tuple-element.187.refs_4_), channel_id=1, source_target_pairs={{0,4},{1,5},{2,6},{3,7},{4,0},{5,1},{6,2},{7,3},{8,12},{9,13},{10,... | collective-permute-start | bytes 786440 | tf_op jit(solution)/shard_map/ppermute | solution.py:577
  207.4 21.0 %collective-permute-start.40 = (f32[512,512]{1,0:T(8,128)S(1)}, f32[512,512]{1,0:T(8,128)S(1)}, u32[]{:S(2)}, u32[]{:S(2)}) collective-permute-start(f32[512,512]{1,0:T(8,128)S(1)} %get-tuple-element.189.refs_0_.refs_4_), channel_id=1, source_target_pairs={{0,1},{1,0},{2,3},{3,2},{4,5},{5,4},{6,7},{7,6},{8,24},{9,25},{10,... | collective-permute-start | bytes 3145736 | tf_op jit(solution)/shard_map/ppermute | solution.py:577
  207.7 21.8 %collective-permute-start.43 = (f32[512,512]{1,0:T(8,128)S(1)}, f32[512,512]{1,0:T(8,128)S(1)}, u32[]{:S(2)}, u32[]{:S(2)}) collective-permute-start(f32[512,512]{1,0:T(8,128)S(1)} %get-tuple-element.185.refs_0_), channel_id=1, source_target_pairs={{0,8},{1,9},{2,10},{3,11},{4,12},{5,13},{6,14},{7,15},{8,0},{9,1},... | collective-permute-start | bytes 3145736 | tf_op jit(solution)/shard_map/ppermute | solution.py:577
  207.7 16.3 %collective-permute-start.42 = (f32[128,1152]{1,0:T(8,128)S(1)}, f32[128,1152]{1,0:T(8,128)S(1)}, u32[]{:S(2)}, u32[]{:S(2)}) collective-permute-start(f32[128,1152]{1,0:T(8,128)S(1)} %get-tuple-element.191.refs_3_), channel_id=1, source_target_pairs={{0,16},{1,17},{2,18},{3,19},{4,20},{5,21},{6,22},{7,23},{8,9},{9,8... | collective-permute-start | bytes 1769480 | tf_op jit(solution)/shard_map/ppermute | solution.py:577
  208.1 15.8 %collective-permute-start.41 = (f32[256,512]{1,0:T(8,128)S(1)}, f32[256,512]{1,0:T(8,128)S(1)}, u32[]{:S(2)}, u32[]{:S(2)}) collective-permute-start(f32[256,512]{1,0:T(8,128)S(1)} %get-tuple-element.190.refs_8_), channel_id=1, source_target_pairs={{0,2},{1,3},{2,0},{3,1},{4,6},{5,7},{6,4},{7,5},{8,10},{9,11},{10,... | collective-permute-start | bytes 1572872 | tf_op jit(solution)/shard_map/ppermute | solution.py:577
  228.5 17.5 %collective-permute-start.49 = (f32[256,1152]{1,0:T(8,128)S(1)}, f32[256,1152]{1,0:T(8,128)S(1)}, u32[]{:S(2)}, u32[]{:S(2)}) collective-permute-start(f32[256,1152]{1,0:T(8,128)S(1)} %get-tuple-element.192._.refs_0_), channel_id=1, source_target_pairs={{0,1},{1,0},{2,3},{3,2},{4,5},{5,4},{6,7},{7,6},{8,24},{9,25},{10,... | collective-permute-start | bytes 3538952 | tf_op jit(solution)/shard_map/ppermute | solution.py:577
  229.0 4.9 %collective-permute-start.44 = (f32[512,512]{1,0:T(8,128)S(1)}, f32[512,512]{1,0:T(8,128)S(1)}, u32[]{:S(2)}, u32[]{:S(2)}) collective-permute-start(f32[512,512]{1,0:T(8,128)S(1)} %get-tuple-element.193.refs_1_), channel_id=1, source_target_pairs={{0,8},{1,9},{2,10},{3,11},{4,12},{5,13},{6,14},{7,15},{8,0},{9,1},... | collective-permute-start | bytes 3145736 | tf_op jit(solution)/shard_map/ppermute | solution.py:577
  229.5 5.9 %collective-permute-start.45 = (f32[512,512]{1,0:T(8,128)S(1)}, f32[512,512]{1,0:T(8,128)S(1)}, u32[]{:S(2)}, u32[]{:S(2)}) collective-permute-start(f32[512,512]{1,0:T(8,128)S(1)} %get-tuple-element.189.refs_0_.refs_4_), channel_id=1, source_target_pairs={{0,8},{1,9},{2,10},{3,11},{4,12},{5,13},{6,14},{7,15},{8,0},{9,1},... | collective-permute-start | bytes 3145736 | tf_op jit(solution)/shard_map/ppermute | solution.py:577
  229.5 7.7 %collective-permute-start.46 = (f32[512,512]{1,0:T(8,128)S(1)}, f32[512,512]{1,0:T(8,128)}, u32[]{:S(2)}, u32[]{:S(2)}) collective-permute-start(f32[512,512]{1,0:T(8,128)S(1)} %get-tuple-element.194.refs_5_), channel_id=1, source_target_pairs={{0,8},{1,9},{2,10},{3,11},{4,12},{5,13},{6,14},{7,15},{8,0},{9,1},... | collective-permute-start | bytes 3145736 | tf_op jit(solution)/shard_map/ppermute | solution.py:577
  230.9 5.2 %collective-permute-start.48 = (f32[256,512]{1,0:T(8,128)S(1)}, f32[256,512]{1,0:T(8,128)S(1)}, u32[]{:S(2)}, u32[]{:S(2)}) collective-permute-start(f32[256,512]{1,0:T(8,128)S(1)} %get-tuple-element.195.refs_9_), channel_id=1, source_target_pairs={{0,8},{1,9},{2,10},{3,11},{4,12},{5,13},{6,14},{7,15},{8,0},{9,1},... | collective-permute-start | bytes 1572872 | tf_op jit(solution)/shard_map/ppermute | solution.py:577
  233.9 13.2 %collective-permute-start.50 = (f32[256,1152]{1,0:T(8,128)S(1)}, f32[256,1152]{1,0:T(8,128)S(1)}, u32[]{:S(2)}, u32[]{:S(2)}) collective-permute-start(f32[256,1152]{1,0:T(8,128)S(1)} %get-tuple-element.192._.refs_0_), channel_id=1, source_target_pairs={{0,8},{1,9},{2,10},{3,11},{4,12},{5,13},{6,14},{7,15},{8,0},{9,1},... | collective-permute-start | bytes 3538952 | tf_op jit(solution)/shard_map/ppermute | solution.py:577
  (44 other events, 375.9 us)

commit v5 on v4

--- a/solution.py
+++ b/solution.py
@@ -12,9 +12,11 @@
 VMEM = pl.BlockSpec(memory_space=pltpu.VMEM)
 SMEM = pl.BlockSpec(memory_space=pltpu.SMEM)
 ORDERS = ("xyab", "xyab", "abxy", "xyab")
+FIRST = 3
 TAIL = 5
 CHUNKS = 4
-FINISH = 56
+FINISH = 36
+HELD = 30
 WAVE = 24
 LAST = 30
 UNROLL = 2
@@ -279,7 +281,7 @@
         second_grad[...] += dot_rt(up_low, w_up[:, at])
         return carry
 
-    lax.fori_loop(0, w_down.shape[0] // block, part, 0, unroll=UNROLL)
+    lax.fori_loop(0, w_down.shape[0] // block, part, 0, unroll=min(UNROLL, w_down.shape[0] // block))
 
 
 def state_kernel(stage, scalars, ins, outs, extra, scratch):
@@ -701,9 +703,12 @@
     return first, passed
 
 
-def finish_kernel(steps, routes, total, few, _, *refs):
+def finish_kernel(steps, routes, total, few, skip, *refs):
     count = len(steps)
-    arrays, outs = refs[: 4 * count], refs[4 * count : 4 * count + total]
+    before, into = skip
+    arrays = refs[before : before + 4 * count]
+    refs = arrays + refs[before + 4 * count + into :]
+    outs = refs[4 * count : 4 * count + total]
     buffers, sems = refs[4 * count + total : 5 * count + total], refs[-1]
     even = lax.axis_index("row") % 2 == 0
     base, plans = 0, []
@@ -722,7 +727,8 @@
                         source = pair[half ^ upper_half]
                         buffer = buffers[k].at[parity, half]
                         for at, columns, output, to in routes(k, parity, half * rows, rows):
-                            plan.append((source.at[at, columns], buffer.at[at, columns], outs[output].at[to]))
+                            target = None if output is None else outs[output].at[to]
+                            plan.append((source.at[at, columns], buffer.at[at, columns], target))
                     mine = even if is_own == (parity == 0) else jnp.logical_not(even)
                     plans.append((jnp.logical_and(mine, place == upper_half), plan, base))
                     longest = max(longest, len(plan))
@@ -740,54 +746,59 @@
         def _():
             for i, (source, buffer, target) in enumerate(plan):
                 pltpu.make_async_copy(source, buffer, sems.at[0, first + i]).wait()
-                pltpu.make_async_copy(buffer, target, sems.at[1, first + i]).start()
+                if target is not None:
+                    pltpu.make_async_copy(buffer, target, sems.at[1, first + i]).start()
+
+    small = []
+    if few:
+        packed = buffers[0].at[0, 0, pl.ds(0, few), pl.ds(outs[0].shape[1], 128)]
+        small = spread_small(packed, outs[2:], refs[5 * count + total : -1], sems)
 
     for condition, plan, first in plans:
 
         @pl.when(condition)
         def _():
             for i, (source, buffer, target) in enumerate(plan):
-                pltpu.make_async_copy(buffer, target, sems.at[1, first + i]).wait()
-
-    if few:
-        spread_small(outs[2:], refs[5 * count + total :])
-
-
-def spread_small(outs, scratch):
-    packed, *targets = outs
-    tiles, *rows, sems = scratch
-    copy = pltpu.make_async_copy(packed, tiles, sems.at[0, 0])
-    copy.start()
-    copy.wait()
+                if target is not None:
+                    pltpu.make_async_copy(buffer, target, sems.at[1, first + i]).wait()
+
+    for copy in small:
+        copy.wait()
+
+
+def spread_small(tiles, targets, rows, sems):
     width = targets[0].shape[1]
     line = 0
     for row in rows:
         for r in range(row.shape[0]):
             for j in range(row.shape[1] // 128):
-                at = (line + j * 128 // width, j * 128 % width // 128)
-                source = at[1] * SUB + at[0]
+                source = j * 128 % width // 128 * SUB + line + j * 128 // width
                 row[r : r + 1, j * 128 : (j + 1) * 128] = tiles[source : source + 1, :]
             line += row.shape[1] // width
-    copies = [pltpu.make_async_copy(row, out, sems.at[1, i]) for i, (row, out) in enumerate(zip(rows, targets))]
+    last = sems.shape[1] - len(rows)
+    copies = [pltpu.make_async_copy(row, out, sems.at[1, last + i]) for i, (row, out) in enumerate(zip(rows, targets))]
     for copy in copies:
         copy.start()
-    for copy in copies:
-        copy.wait()
-
-
-def finish_call(routes, token, sums, outs, few=0):
+    return copies
+
+
+def finish_call(routes, tokens, sums, outs, few=0, into=()):
     arrays = [array for one in sums for array in (one.mine, one.received, *one.others)]
+    before = len(tokens) + len(arrays)
     return pl.pallas_call(
-        functools.partial(finish_kernel, [one.steps[0] for one in sums], routes, len(outs), few),
-        in_specs=[pl.BlockSpec(memory_space=pl.ANY)] * (1 + len(arrays)),
+        functools.partial(
+            finish_kernel, [one.steps[0] for one in sums], routes, len(outs), few, (len(tokens), len(into))
+        ),
+        in_specs=[ANY] * (before + len(into)),
         out_specs=(HBM,) * len(outs),
         out_shape=shaped(*outs),
+        input_output_aliases={before + i: i for i in range(len(into))},
         scratch_shapes=[pltpu.VMEM((2, 2) + one.mine.shape, F32) for one in sums]
         + ([pltpu.VMEM(*out) for out in outs[2:]] if few else [])
         + [pltpu.SemaphoreType.DMA((2, 48))],
         compiler_params=pltpu.CompilerParams(vmem_limit_bytes=FINISH << 20),
         cost_estimate=pl.CostEstimate(flops=1, bytes_accessed=1, transcendentals=0),
-    )(token, *arrays)
+    )(*tokens, *arrays, *into)
 
 
 def cut(first, rows, marks):
@@ -822,17 +833,17 @@
         56,
     )
     carried, levels = carry_forward(totals)
-    half_ff = ff // 2
-    mlp_pair, out_pair = ((half_ff, width), F32), ((hidden // 2, width), F32)
-    low_half, high_half, every = pl.ds(0, half_ff), pl.ds(half_ff, half_ff), pl.ds(0, width)
+    early_ff = ff * FIRST // 4
+    pair_a, pair_b, out_pair = [((size, width), F32) for size in (early_ff, ff - early_ff, hidden // 2)]
+    low_half, high_half, every = pl.ds(0, early_ff), pl.ds(early_ff, ff - early_ff), pl.ds(0, width)
     blend, low, middle, second_low, tail, second_grad, mine_a, other_a = staged_call(
         state_kernel,
         [first_len],
         [carried, subk, subs, keep, drive, cand, gate, x, w_out, gain_two, (w_up, (every, low_half)),
          (w_down, (low_half, every)), up],
         [(th, BF16), (th, BF16), (tw, F32), (tw, BF16), (tw, F32), (tw, F32)],
-        [mlp_pair, mlp_pair],
-        [((SUB, hidden), F32), ((half_ff, width), F32), ((half_ff, width), F32)],
+        [pair_a, pair_a],
+        [((SUB, hidden), F32), pair_a, pair_a],
         6 * count * width * ff,
         64,
         56,
@@ -844,8 +855,8 @@
         [second_low, up, (w_up, (every, high_half)), (w_down, (high_half, every)), tail, second_grad, middle, gain_two,
          w_out, low, keep, subk],
         [(tokens.shape, BF16), (tw, F32), ((1, width), F32), (th, F32), ((SUB, hidden), F32), ((rows, hidden), F32)],
-        [mlp_pair, mlp_pair, out_pair, out_pair],
-        [((half_ff, width), F32)] * 2 + [((hidden // 2, width), F32)] * 2,
+        [pair_b, pair_b, out_pair, out_pair],
+        [pair_b, pair_b, out_pair, out_pair],
         8 * count * width * ff,
         64,
         56,
@@ -857,7 +868,7 @@
         return wave([], [first], [passed])[1][0]
 
     returned = carry_backward(passed, levels, between)
-    token, (returned,) = wave([], [first] + early, [returned])
+    (returned,) = held([one.received for one in early], [returned])
     tile = 16
     pair = ((width, hidden + 128), F32)
     grad_tokens, sent, tail_normed, tail_middle, mine_d, other_d = staged_call(
@@ -889,19 +900,12 @@
         input_output_aliases={5: 0},
     )(tokens, tail_normed, tail_middle, received, gain_one, grad_tokens)
     late = Summed(mine_d, other_d, ORDERS[3])
-    tokens = [[tail_normed]] + [[]] * (TAIL - 3) + [[grad_tokens]]
+    tokens = [[]] * (TAIL - 2) + [[grad_tokens]]
     left = [[first], early]
-    while late.busy():
-        more = tokens.pop(0) if tokens else []
-        ended = [] if not left or left[0][0].busy() else left.pop(0)
-        running = sum(left, []) + [late]
-        token, ready = wave([token, *more], running, [one.received for one in ended])
-        for one, received in zip(ended, ready):
-            one.received = received
-            one.across()
-    def mlp_routes(k, parity, first, rows):
-        everything, plan = pl.ds(0, width), []
-        first = first + k * half_ff
+    token, _ = wave([tail_normed], [first] + early)
+    def mlp_routes(past, k, parity, first, rows):
+        everything, plan, k = pl.ds(0, width), [], k + past
+        first = first + (0, early_ff, ff)[k]
         if k == 2:
             first = first - ff
             return [(pl.ds(0, rows), everything, 2, (pl.ds(first + parity * hidden // 2, rows), everything))]
@@ -914,26 +918,41 @@
                 plan.append((inner, everything, 1, (pl.ds(at - block, size), pl.ds(block, width))))
         return plan
 
+    grad_down = grad_up = None
+    while late.busy():
+        more = tokens.pop(0) if tokens else []
+        ended = left.pop(0) if left and not left[0][0].busy() else []
+        token, ready = wave([token, *more], sum(left, []) + [late], [one.received for one in ended])
+        for one, received in zip(ended, ready):
+            one.received = received
+            one.across()
+        if ended == [first]:
+            grad_down, grad_up = finish_call(
+                functools.partial(mlp_routes, 0), [token], ended, [((ff, width), F32), ((width, ff), F32)]
+            )
+            tokens.insert(0, [grad_down])
+    for one in sum(left, []):
+        one.across()
+
     few = SUB * width // 128
 
     def gate_routes(k, parity, first, rows):
         inner, cols = pl.ds(0, rows), pl.ds(0, hidden)
         plan = [(inner, cols, parity, (pl.ds(first, rows), cols))]
         if parity == 0 and first < few:
-            least = min(rows, few - first)
-            at, all_cols = pl.ds(0, least), pl.ds(0, 128)
-            plan.append((at, pl.ds(hidden, 128), 2, (pl.ds(first, least), all_cols)))
+            plan.append((pl.ds(0, few), pl.ds(hidden, 128), None, None))
         return plan
 
     grad_down, grad_up, grad_out = finish_call(
-        mlp_routes, token, [first, *early], [((ff, width), F32), ((width, ff), F32), ((hidden, width), F32)]
+        functools.partial(mlp_routes, 1), [token], early,
+        [((ff, width), F32), ((width, ff), F32), ((hidden, width), F32)], 0, [grad_down, grad_up],
     )
     (late.received,) = held([grad_out], [late.received])
     late.across()
-    grad_z, grad_h, small, grad_gain_one, grad_conv, grad_bias, grad_gain = finish_call(
-        gate_routes, grad_out, [late],
-        [((width, hidden), F32), ((width, hidden), F32), ((SUB * width // 128, 128), F32), ((1, width), F32),
-         ((lag + 1, width), F32), ((1, hidden), F32), ((1, width), F32)],
+    grad_z, grad_h, grad_gain_one, grad_conv, grad_bias, grad_gain = finish_call(
+        gate_routes, [grad_out], [late],
+        [((width, hidden), F32), ((width, hidden), F32), ((1, width), F32), ((lag + 1, width), F32),
+         ((1, hidden), F32), ((1, width), F32)],
         few,
     )
     return (
@@ -958,6 +977,7 @@
         out_specs=(ANY,) * len(arrays),
         out_shape=shaped(*[(array.shape, F32) for array in arrays]),
         input_output_aliases={len(tokens) + i: i for i in range(len(arrays))},
+        compiler_params=pltpu.CompilerParams(vmem_limit_bytes=HELD << 20),
     )(*tokens, *arrays)
 
 

time: 257 us -> 240 us (0.934)
  waiting for transfers between devices: 113 us -> 105 us
  starting transfers between devices: 71.9 us -> 67.9 us
  Pallas kernels: 58.4 us -> 55.3 us
    ppermute x44, waiting for transfers between devices: 93.5 us -> 87 us  [exchanged(): return lax.ppermute(array, BOTH, pairs)]
    ppermute x44, starting transfers between devices: 52 us -> 47.3 us  [exchanged(): return lax.ppermute(array, BOTH, pairs)]
    pallas_call x2 -> x3, Pallas kernels: 14.1 us -> 10.3 us  [finish_call(): pl.pallas_call(functools.partial(finish_kernel, [one.steps[0] for one in...]
    unnamed x80 -> x56, local copies, waits for them, and re-layouts: 9.38 us -> 7.37 us
  transfers between devices with their start and end apart: 52 -> 52, of which waited for: 33 -> 34; matrix products, arithmetic and copies ran while one was open for 0% -> 0% of each run, Pallas kernels for 8% -> 12%
where the time goes in v5:
time: 240 us
  waiting for transfers between devices  105 us (44%)
  starting transfers between devices  67.9 us (28%)
  Pallas kernels  55.3 us (23%)
  local copies, waits for them, and re-layouts  7.37 us (3%)
  other arithmetic  2.93 us (1%)
    ppermute x44, waiting for transfers between devices, exchanged(): return lax.ppermute(array, BOTH, pairs)  87 us
    ppermute x44, starting transfers between devices, exchanged(): return lax.ppermute(array, BOTH, pairs)  47.3 us
    pallas_call x4, Pallas kernels, staged_call(): pl.pallas_call(body, in_specs=[SMEM] * n_s + [HBM] * n_i, out_specs=(HBM,...  40.8 us
    ppermute x6, starting transfers between devices, swapped(): lax.ppermute(array, axis, [(i, i ^ bit) for i in range(lax.axis_size(axis...  14.5 us
    ppermute x6, waiting for transfers between devices, swapped(): lax.ppermute(array, axis, [(i, i ^ bit) for i in range(lax.axis_size(axis...  11.9 us
    pallas_call x3, Pallas kernels, finish_call(): pl.pallas_call(functools.partial(finish_kernel, [one.steps[0] for one in...  10.3 us
    unnamed x56, local copies, waits for them, and re-layouts  7.37 us
    ppermute x1, starting transfers between devices, per_device(): lax.ppermute(tokens[:, group_len - lag:].astype(F32), 'seq', [(i, i + 1)...  4.84 us
  transfers between devices with their start and end apart: 52, of which 34 were waited for; matrix products, arithmetic and copies ran while one was open for 0% of the time, Pallas kernels for 12%

profile of v5, /device:TPU:0, one launch (start us, length us, event | category | flops | bytes accessed | tf_op | source)
XLA Modules:
  0.0 239.9 jit_solution(10910415934133244951)
XLA Ops:
  1.4 4.8 %collective-permute-start = (f32[4,3,512]{2,1,0:T(4,128)S(1)}, f32[4,3,512]{2,1,0:T(4,128)S(1)}, u32[]{:S(2)}, u32[]{:S(2)}) collective-permute-start(f32[4,3,512]{2,1,0:T(4,128)S(1)} %slice_convert_fusion), channel_id=1, source_target_pairs={{0,1},{1,2},{2,3},{3,4},{4,5},{5,6},{6,7},{8,9},{9,10},{10,11},{11... | collective-permute-start | bytes 73736 | tf_op jit(solution)/shard_map/ppermute | solution.py:818
  8.4 7.5 %shard_map.203 = (bf16[512,512]{1,0:T(8,128)(2,1)}, bf16[512,512]{1,0:T(8,128)(2,1)}, f32[512,1024]{1,0:T(8,128)}, f32[512,1024]{1,0:T(8,128)}, f32[512,1024]{1,...) custom-call(s32[4]{0:T(128)} %refs_0_.5, ...), custom_call_target="tpu_custom_call" | custom-call | flops 1073741824 | bytes 8388608 | tf_op jit(solution)/shard_map/pallas_call | solution.py:93
  15.9 2.4 collective-permute-start.1
  18.3 2.1 collective-permute-done.1
  21.2 3.1 %collective-permute-start.2 = (f32[2,4,1024]{2,1,0:T(4,128)S(1)}, f32[2,4,1024]{2,1,0:T(4,128)S(1)}, u32[]{:S(2)}, u32[]{:S(2)}) collective-permute-start(f32[2,4,1024]{2,1,0:T(4,128)S(1)} %pad_maximum_fusion), channel_id=1, source_target_pairs={{0,2},{1,3},{2,0},{3,1},{4,6},{5,7},{6,4},{7,5},{8,10},{9,11},{10,... | collective-permute-start | bytes 98312 | tf_op jit(solution)/shard_map/ppermute | solution.py:515
  24.2 1.9 collective-permute-done.2
  26.2 3.1 %collective-permute-start.3 = (f32[2,4,1024]{2,1,0:T(4,128)S(1)}, f32[2,4,1024]{2,1,0:T(4,128)S(1)}, u32[]{:S(2)}, u32[]{:S(2)}) collective-permute-start(f32[2,4,1024]{2,1,0:T(4,128)S(1)} %pad_maximum_fusion.1), channel_id=1, source_target_pairs={{0,4},{1,5},{2,6},{3,7},{4,0},{5,1},{6,2},{7,3},{8,12},{9,13},{10,... | collective-permute-start | bytes 98312 | tf_op jit(solution)/shard_map/ppermute | solution.py:515
  29.3 1.9 collective-permute-done.3
  31.8 15.7 %shard_map.204 = (bf16[512,1024]{1,0:T(8,128)(2,1)}, bf16[512,1024]{1,0:T(8,128)(2,1)}, f32[512,512]{1,0:T(8,128)}, bf16[512,512]{1,0:T(8,128)(2,1)}, f32[512,51...) custom-call(s32[4]{0:T(128)} %refs_0_.5, f32[4,1024]{1,0:T(4,128)} %add_select_fusion.2.refs_1_, ...), custom_call_target="tpu_custom_call" | custom-call | flops 3221225472 | bytes 8388608 | tf_op jit(solution)/shard_map/pallas_call | solution.py:93
  47.6 8.7 %shard_map.205 = (bf16[4,128,512]{2,1,0:T(8,128)(2,1)}, f32[512,512]{1,0:T(8,128)}, f32[1,512]{1,0:T(1,128)}, f32[512,1024]{1,0:T(8,128)}, f32[8,1024]{1,0:T(8,1...) custom-call(bf16[512,512]{1,0:T(8,128)(2,1)} %get-tuple-element.118., ...), custom_call_target="tpu_custom_call" | custom-call | flops 4294967296 | bytes 8388608 | tf_op jit(solution)/shard_map/pallas_call | solution.py:93
  57.8 3.0 %collective-permute-done.6 = f32[4,1024]{1,0:T(4,128)S(1)} collective-permute-done((f32[4,1024]{1,0:T(4,128)}, f32[4,1024]{1,0:T(4,128)S(1)}, u32[]{:S(2)}, u32[]{:S(2)}) %collective-permute-start.6) | collective-permute-done | bytes 16416 | tf_op jit(solution)/shard_map/ppermute | solution.py:515
  62.2 2.0 collective-permute-start.8
  64.1 1.8 collective-permute-done.8
  66.0 3.0 %collective-permute-start.9 = (f32[4,1024]{1,0:T(4,128)S(1)}, f32[4,1024]{1,0:T(4,128)S(1)}, u32[]{:S(2)}, u32[]{:S(2)}) collective-permute-start(f32[4,1024]{1,0:T(4,128)S(1)} %fusion.6), channel_id=1, source_target_pairs={{0,4},{1,5},{2,6},{3,7},{4,0},{5,1},{6,2},{7,3},{8,12},{9,13},{10,... | collective-permute-start | bytes 49160 | tf_op jit(solution)/shard_map/ppermute | solution.py:515
  72.2 8.9 %shard_map.208 = (bf16[4,128,512]{2,1,0:T(8,128)(2,1)}, f32[4,3,512]{2,1,0:T(4,128)S(1)}, f32[4,16,512]{2,1,0:T(8,128)S(1)}, f32[4,16,512]{2,1,0:T(8,128)S(1)}, ...) custom-call(s32[4]{0:T(128)S(1)} %copy-done.24, f32[4,1024]{1,0:T(4,128)S(1)} %shard_map.207.refs_1_, ...), custom_call_target="tpu_custom_call" | custom-call | flops 2147483648 | bytes 8388608 | tf_op jit(solution)/shard_map/pallas_call | solution.py:93
  81.2 8.3 %collective-permute-done.11.refs_2_ = f32[768,512]{1,0:T(8,128)S(1)} collective-permute-done((f32[768,512]{1,0:T(8,128)S(1)}, f32[768,512]{1,0:T(8,128)S(1)}, u32[]{:S(2)}, u32[]{:S(2)}) %collective-permute-start.11) | collective-permute-done | bytes 1572896 | tf_op jit(solution)/shard_map/ppermute | solution.py:579
  92.1 1.8 collective-permute-start.14
  93.9 9.8 %collective-permute-done.13.refs_4_ = f32[256,512]{1,0:T(8,128)S(1)} collective-permute-done((f32[256,512]{1,0:T(8,128)S(1)}, f32[256,512]{1,0:T(8,128)S(1)}, u32[]{:S(2)}, u32[]{:S(2)}) %collective-permute-start.13) | collective-permute-done | bytes 524320 | tf_op jit(solution)/shard_map/ppermute | solution.py:579
  109.6 7.4 %collective-permute-done.17.refs_4_ = f32[128,512]{1,0:T(8,128)S(1)} collective-permute-done((f32[128,512]{1,0:T(8,128)S(1)}, f32[128,512]{1,0:T(8,128)S(1)}, u32[]{:S(2)}, u32[]{:S(2)}) %collective-permute-start.17) | collective-permute-done | bytes 262176 | tf_op jit(solution)/shard_map/ppermute | solution.py:579
  117.0 4.4 %collective-permute-done.18.refs_6_ = f32[128,512]{1,0:T(8,128)S(1)} collective-permute-done((f32[128,512]{1,0:T(8,128)S(1)}, f32[128,512]{1,0:T(8,128)S(1)}, u32[]{:S(2)}, u32[]{:S(2)}) %collective-permute-start.18) | collective-permute-done | bytes 262176 | tf_op jit(solution)/shard_map/ppermute | solution.py:579
  121.4 2.0 collective-permute-done.19.refs_8_
  126.1 4.7 %collective-permute-done.21.refs_4_ = f32[64,512]{1,0:T(8,128)S(1)} collective-permute-done((f32[64,512]{1,0:T(8,128)S(1)}, f32[64,512]{1,0:T(8,128)S(1)}, u32[]{:S(2)}, u32[]{:S(2)}) %collective-permute-start.21) | collective-permute-done | bytes 131104 | tf_op jit(solution)/shard_map/ppermute | solution.py:579
  131.2 2.0 collective-permute-done.20.refs_2_
  134.1 2.0 collective-permute-start.24
  139.8 4.5 %collective-permute-done.10.received = f32[4,3,512]{2,1,0:T(4,128)S(1)} collective-permute-done((f32[4,3,512]{2,1,0:T(4,128)S(1)}, f32[4,3,512]{2,1,0:T(4,128)S(1)}, u32[]{:S(2)}, u32[]{:S(2)}) %collective-permute-start.10) | collective-permute-done | bytes 24608 | tf_op jit(solution)/shard_map/ppermute | solution.py:889
  144.9 1.9 shard_map.209.refs_1_
  149.7 2.2 collective-permute-start.31
  154.3 5.2 %collective-permute-done.29.refs_4_ = f32[32,512]{1,0:T(8,128)S(1)} collective-permute-done((f32[32,512]{1,0:T(8,128)S(1)}, f32[32,512]{1,0:T(8,128)S(1)}, u32[]{:S(2)}, u32[]{:S(2)}) %collective-permute-start.29) | collective-permute-done | bytes 65568 | tf_op jit(solution)/shard_map/ppermute | solution.py:579
  161.0 1.9 collective-permute-start.32
  163.0 2.5 %collective-permute-start.35 = (f32[32,1152]{1,0:T(8,128)S(1)}, f32[32,1152]{1,0:T(8,128)S(1)}, u32[]{:S(2)}, u32[]{:S(2)}) collective-permute-start(f32[32,1152]{1,0:T(8,128)S(1)} %get-tuple-element.184.refs_7_), channel_id=1, source_target_pairs={{0,4},{1,5},{2,6},{3,7},{4,0},{5,1},{6,2},{7,3},{8,12},{9,13},{10,... | collective-permute-start | bytes 442376 | tf_op jit(solution)/shard_map/ppermute | solution.py:579
  166.8 1.8 collective-permute-start.34
  168.6 2.7 %collective-permute-done.33.refs_4_ = f32[64,512]{1,0:T(8,128)S(1)} collective-permute-done((f32[64,512]{1,0:T(8,128)S(1)}, f32[64,512]{1,0:T(8,128)S(1)}, u32[]{:S(2)}, u32[]{:S(2)}) %collective-permute-start.33) | collective-permute-done | bytes 131104 | tf_op jit(solution)/shard_map/ppermute | solution.py:579
  171.3 1.9 collective-permute-done.34.refs_6_
  174.7 2.8 %collective-permute-start.36 = (f32[768,512]{1,0:T(8,128)S(1)}, f32[768,512]{1,0:T(8,128)S(1)}, u32[]{:S(2)}, u32[]{:S(2)}) collective-permute-start(f32[768,512]{1,0:T(8,128)S(1)} %get-tuple-element.185.refs_0_.refs_1_), channel_id=1, source_target_pairs={{0,1},{1,0},{2,3},{3,2},{4,5},{5,4},{6,7},{7,6},{8,24},{9,25},{10,... | collective-permute-start | bytes 4718600 | tf_op jit(solution)/shard_map/ppermute | solution.py:579
  178.6 2.2 collective-permute-start.37
  180.8 3.2 %collective-permute-start.38 = (f32[128,512]{1,0:T(8,128)S(1)}, f32[128,512]{1,0:T(8,128)S(1)}, u32[]{:S(2)}, u32[]{:S(2)}) collective-permute-start(f32[128,512]{1,0:T(8,128)S(1)} %get-tuple-element.187.refs_4_), channel_id=1, source_target_pairs={{0,4},{1,5},{2,6},{3,7},{4,0},{5,1},{6,2},{7,3},{8,12},{9,13},{10,... | collective-permute-start | bytes 786440 | tf_op jit(solution)/shard_map/ppermute | solution.py:579
  184.0 4.1 %collective-permute-done.37.refs_3_ = f32[128,512]{1,0:T(8,128)S(1)} collective-permute-done((f32[128,512]{1,0:T(8,128)S(1)}, f32[128,512]{1,0:T(8,128)S(1)}, u32[]{:S(2)}, u32[]{:S(2)}) %collective-permute-start.37) | collective-permute-done | bytes 262176 | tf_op jit(solution)/shard_map/ppermute | solution.py:579
  188.0 3.5 %collective-permute-done.38.refs_5_ = f32[128,512]{1,0:T(8,128)S(1)} collective-permute-done((f32[128,512]{1,0:T(8,128)S(1)}, f32[128,512]{1,0:T(8,128)S(1)}, u32[]{:S(2)}, u32[]{:S(2)}) %collective-permute-start.38) | collective-permute-done | bytes 262176 | tf_op jit(solution)/shard_map/ppermute | solution.py:579
  191.5 6.0 %collective-permute-done.36.refs_1_ = f32[768,512]{1,0:T(8,128)S(1)} collective-permute-done((f32[768,512]{1,0:T(8,128)S(1)}, f32[768,512]{1,0:T(8,128)S(1)}, u32[]{:S(2)}, u32[]{:S(2)}) %collective-permute-start.36) | collective-permute-done | bytes 1572896 | tf_op jit(solution)/shard_map/ppermute | solution.py:579
  199.3 1.7 collective-permute-start.43
  201.1 1.7 collective-permute-start.42
  202.8 4.0 %shard_map.218 = (f32[2048,512]{1,0:T(8,128)}, f32[512,2048]{1,0:T(8,128)}) custom-call(f32[256,512]{1,0:T(8,128)S(1)} %get-tuple-element.189.refs_0_.refs_1_, f32[768,512]{1,0:T(8,128)S(1)} %get-tuple-element.185.refs_0_.refs_1_, f32[768,512]{1,0:T(8,128)S(1)} %get-tuple-element.190.refs_2_, f32[768,512]{1,0:T(8,128)S(1)} %collective-permute-done.40.refs_3_, ...), custom_call_target="tpu_custom_call" | custom-call | flops 1 | bytes 1 | tf_op jit(solution)/shard_map/pallas_call | solution.py:788
  206.8 6.7 %collective-permute-done.43.refs_3_ = f32[256,512]{1,0:T(8,128)S(1)} collective-permute-done((f32[256,512]{1,0:T(8,128)S(1)}, f32[256,512]{1,0:T(8,128)S(1)}, u32[]{:S(2)}, u32[]{:S(2)}) %collective-permute-start.43) | collective-permute-done | bytes 524320 | tf_op jit(solution)/shard_map/ppermute | solution.py:579
  213.5 2.2 copy-done
  221.3 3.2 %shard_map.220 = (f32[2048,512]{1,0:T(8,128)}, f32[512,2048]{1,0:T(8,128)}, f32[1024,512]{1,0:T(8,128)}) custom-call(f32[256,1152]{1,0:T(8,128)S(1)} %get-tuple-element.194.refs_0_.refs_1_, f32[256,512]{1,0:T(8,128)S(1)} %get-tuple-element.189.refs_0_.refs_1_, ...), custom_call_target="tpu_custom_call", output_to_operand_aliasing={{0}: (9, {}), {1}: (10, {})} | custom-call | flops 1 | bytes 1 | tf_op jit(solution)/shard_map/pallas_call | solution.py:788
  224.5 7.5 %collective-permute-done.49.__1_ = f32[256,1152]{1,0:T(8,128)S(1)} collective-permute-done((f32[256,1152]{1,0:T(8,128)S(1)}, f32[256,1152]{1,0:T(8,128)S(1)}, u32[]{:S(2)}, u32[]{:S(2)}) %collective-permute-start.49) | collective-permute-done | bytes 1179680 | tf_op jit(solution)/shard_map/ppermute | solution.py:579
  233.7 2.8 %collective-permute-done.51.refs_4_ = f32[256,1152]{1,0:T(8,128)S(1)} collective-permute-done((f32[256,1152]{1,0:T(8,128)S(1)}, f32[256,1152]{1,0:T(8,128)S(1)}, u32[]{:S(2)}, u32[]{:S(2)}) %collective-permute-start.51) | collective-permute-done | bytes 1179680 | tf_op jit(solution)/shard_map/ppermute | solution.py:579
  236.5 3.2 %shard_map.222 = (f32[512,1024]{1,0:T(8,128)}, f32[512,1024]{1,0:T(8,128)}, f32[1,512]{1,0:T(1,128)}, f32[4,512]{1,0:T(4,128)}, f32[1,1024]{1,0:T(1,128)}, /*index=5*/f32[1,512]{1,0:T(1,128)}) custom-call(f32[1024,512]{1,0:T(8,128)S(1)} %copy-done.2, f32[256,1152]{1,0:T(8,128)S(1)} %get-tuple-element.194.refs_0_.refs_1_, ...), custom_call_target="tpu_custom_call" | custom-call | flops 1 | bytes 1 | tf_op jit(solution)/shard_map/pallas_call | solution.py:788
  (141 shorter events, 46.9 us)
Async XLA Ops:
  1.4 6.4 %collective-permute-start = (f32[4,3,512]{2,1,0:T(4,128)S(1)}, f32[4,3,512]{2,1,0:T(4,128)S(1)}, u32[]{:S(2)}, u32[]{:S(2)}) collective-permute-start(f32[4,3,512]{2,1,0:T(4,128)S(1)} %slice_convert_fusion), channel_id=1, source_target_pairs={{0,1},{1,2},{2,3},{3,4},{4,5},{5,6},{6,7},{8,9},{9,10},{10,11},{11... | collective-permute-start | bytes 73736 | tf_op jit(solution)/shard_map/ppermute | solution.py:818
  15.9 4.5 %collective-permute-start.1 = (f32[2,4,1024]{2,1,0:T(4,128)}, f32[2,4,1024]{2,1,0:T(4,128)S(1)}, u32[]{:S(2)}, u32[]{:S(2)}) collective-permute-start(f32[2,4,1024]{2,1,0:T(4,128)} %get-tuple-element.109), channel_id=1, source_target_pairs={{0,1},{1,0},{2,3},{3,2},{4,5},{5,4},{6,7},{7,6},{8,9},{9,8},{10,11... | collective-permute-start | bytes 98312 | tf_op jit(solution)/shard_map/ppermute | solution.py:515
  21.2 5.0 %collective-permute-start.2 = (f32[2,4,1024]{2,1,0:T(4,128)S(1)}, f32[2,4,1024]{2,1,0:T(4,128)S(1)}, u32[]{:S(2)}, u32[]{:S(2)}) collective-permute-start(f32[2,4,1024]{2,1,0:T(4,128)S(1)} %pad_maximum_fusion), channel_id=1, source_target_pairs={{0,2},{1,3},{2,0},{3,1},{4,6},{5,7},{6,4},{7,5},{8,10},{9,11},{10,... | collective-permute-start | bytes 98312 | tf_op jit(solution)/shard_map/ppermute | solution.py:515
  26.2 5.0 %collective-permute-start.3 = (f32[2,4,1024]{2,1,0:T(4,128)S(1)}, f32[2,4,1024]{2,1,0:T(4,128)S(1)}, u32[]{:S(2)}, u32[]{:S(2)}) collective-permute-start(f32[2,4,1024]{2,1,0:T(4,128)S(1)} %pad_maximum_fusion.1), channel_id=1, source_target_pairs={{0,4},{1,5},{2,6},{3,7},{4,0},{5,1},{6,2},{7,3},{8,12},{9,13},{10,... | collective-permute-start | bytes 98312 | tf_op jit(solution)/shard_map/ppermute | solution.py:515
  47.5 14.1 %collective-permute-start.7 = (f32[1536,512]{1,0:T(8,128)}, f32[1536,512]{1,0:T(8,128)S(1)}, u32[]{:S(2)}, u32[]{:S(2)}) collective-permute-start(f32[1536,512]{1,0:T(8,128)} %get-tuple-element.128), channel_id=1, source_target_pairs={{0,8},{1,9},{2,10},{3,11},{4,12},{5,13},{6,14},{7,15},{8,0},{9,1},... | collective-permute-start | bytes 9437192 | tf_op jit(solution)/shard_map/ppermute | solution.py:579
  56.3 14.4 %collective-permute-start.4 = (f32[512,512]{1,0:T(8,128)}, f32[512,512]{1,0:T(8,128)S(1)}, u32[]{:S(2)}, u32[]{:S(2)}) collective-permute-start(f32[512,512]{1,0:T(8,128)} %get-tuple-element.124), channel_id=1, source_target_pairs={{0,8},{1,9},{2,10},{3,11},{4,12},{5,13},{6,14},{7,15},{8,0},{9,1},... | collective-permute-start | bytes 3145736 | tf_op jit(solution)/shard_map/ppermute | solution.py:579
  56.8 14.0 %collective-permute-start.5 = (f32[512,512]{1,0:T(8,128)}, f32[512,512]{1,0:T(8,128)S(1)}, u32[]{:S(2)}, u32[]{:S(2)}) collective-permute-start(f32[512,512]{1,0:T(8,128)} %get-tuple-element.125), channel_id=1, source_target_pairs={{0,8},{1,9},{2,10},{3,11},{4,12},{5,13},{6,14},{7,15},{8,0},{9,1},... | collective-permute-start | bytes 3145736 | tf_op jit(solution)/shard_map/ppermute | solution.py:579
  56.9 3.9 %collective-permute-start.6 = (f32[4,1024]{1,0:T(4,128)}, f32[4,1024]{1,0:T(4,128)S(1)}, u32[]{:S(2)}, u32[]{:S(2)}) collective-permute-start(f32[4,1024]{1,0:T(4,128)} %get-tuple-element.126), channel_id=1, source_target_pairs={{0,1},{1,0},{2,3},{3,2},{4,5},{5,4},{6,7},{7,6},{8,9},{9,8},{10,11... | collective-permute-start | bytes 49160 | tf_op jit(solution)/shard_map/ppermute | solution.py:515
  62.2 3.8 %collective-permute-start.8 = (f32[4,1024]{1,0:T(4,128)S(1)}, f32[4,1024]{1,0:T(4,128)S(1)}, u32[]{:S(2)}, u32[]{:S(2)}) collective-permute-start(f32[4,1024]{1,0:T(4,128)S(1)} %get-tuple-element.129), channel_id=1, source_target_pairs={{0,2},{1,3},{2,0},{3,1},{4,6},{5,7},{6,4},{7,5},{8,10},{9,11},{10,... | collective-permute-start | bytes 49160 | tf_op jit(solution)/shard_map/ppermute | solution.py:515
  66.0 4.7 %collective-permute-start.9 = (f32[4,1024]{1,0:T(4,128)S(1)}, f32[4,1024]{1,0:T(4,128)S(1)}, u32[]{:S(2)}, u32[]{:S(2)}) collective-permute-start(f32[4,1024]{1,0:T(4,128)S(1)} %fusion.6), channel_id=1, source_target_pairs={{0,4},{1,5},{2,6},{3,7},{4,0},{5,1},{6,2},{7,3},{8,12},{9,13},{10,... | collective-permute-start | bytes 49160 | tf_op jit(solution)/shard_map/ppermute | solution.py:515
  69.0 20.4 %collective-permute-start.11 = (f32[768,512]{1,0:T(8,128)S(1)}, f32[768,512]{1,0:T(8,128)S(1)}, u32[]{:S(2)}, u32[]{:S(2)}) collective-permute-start(f32[768,512]{1,0:T(8,128)S(1)} %get-tuple-element.142), channel_id=1, source_target_pairs={{0,1},{1,0},{2,3},{3,2},{4,5},{5,4},{6,7},{7,6},{8,24},{9,25},{10,... | collective-permute-start | bytes 4718600 | tf_op jit(solution)/shard_map/ppermute | solution.py:579
  81.1 22.9 %collective-permute-start.15 = (f32[512,1152]{1,0:T(8,128)S(1)}, f32[512,1152]{1,0:T(8,128)S(1)}, u32[]{:S(2)}, u32[]{:S(2)}) collective-permute-start(f32[512,1152]{1,0:T(8,128)S(1)} %get-tuple-element.152), channel_id=1, source_target_pairs={{0,8},{1,9},{2,10},{3,11},{4,12},{5,13},{6,14},{7,15},{8,0},{9,1},... | collective-permute-start | bytes 7077896 | tf_op jit(solution)/shard_map/ppermute | solution.py:579
  89.9 14.1 %collective-permute-start.12 = (f32[384,512]{1,0:T(8,128)S(1)}, f32[384,512]{1,0:T(8,128)S(1)}, u32[]{:S(2)}, u32[]{:S(2)}) collective-permute-start(f32[384,512]{1,0:T(8,128)S(1)} %get-tuple-element.145.refs_0_), channel_id=1, source_target_pairs={{0,16},{1,17},{2,18},{3,19},{4,20},{5,21},{6,22},{7,23},{8,9},{9,8... | collective-permute-start | bytes 2359304 | tf_op jit(solution)/shard_map/ppermute | solution.py:579
  91.5 12.2 %collective-permute-start.13 = (f32[256,512]{1,0:T(8,128)S(1)}, f32[256,512]{1,0:T(8,128)S(1)}, u32[]{:S(2)}, u32[]{:S(2)}) collective-permute-start(f32[256,512]{1,0:T(8,128)S(1)} %get-tuple-element.148), channel_id=1, source_target_pairs={{0,1},{1,0},{2,3},{3,2},{4,5},{5,4},{6,7},{7,6},{8,24},{9,25},{10,... | collective-permute-start | bytes 1572872 | tf_op jit(solution)/shard_map/ppermute | solution.py:579
  92.1 11.6 %collective-permute-start.14 = (f32[256,512]{1,0:T(8,128)S(1)}, f32[256,512]{1,0:T(8,128)S(1)}, u32[]{:S(2)}, u32[]{:S(2)}) collective-permute-start(f32[256,512]{1,0:T(8,128)S(1)} %get-tuple-element.150), channel_id=1, source_target_pairs={{0,2},{1,3},{2,0},{3,1},{4,6},{5,7},{6,4},{7,5},{8,10},{9,11},{10,... | collective-permute-start | bytes 1572872 | tf_op jit(solution)/shard_map/ppermute | solution.py:579
  104.5 18.9 %collective-permute-start.19 = (f32[256,1152]{1,0:T(8,128)S(1)}, f32[256,1152]{1,0:T(8,128)S(1)}, u32[]{:S(2)}, u32[]{:S(2)}) collective-permute-start(f32[256,1152]{1,0:T(8,128)S(1)} %get-tuple-element.160), channel_id=1, source_target_pairs={{0,1},{1,0},{2,3},{3,2},{4,5},{5,4},{6,7},{7,6},{8,24},{9,25},{10,... | collective-permute-start | bytes 3538952 | tf_op jit(solution)/shard_map/ppermute | solution.py:579
  106.0 15.4 %collective-permute-start.16 = (f32[192,512]{1,0:T(8,128)S(1)}, f32[192,512]{1,0:T(8,128)S(1)}, u32[]{:S(2)}, u32[]{:S(2)}) collective-permute-start(f32[192,512]{1,0:T(8,128)S(1)} %get-tuple-element.153.refs_0_), channel_id=1, source_target_pairs={{0,2},{1,3},{2,0},{3,1},{4,6},{5,7},{6,4},{7,5},{8,10},{9,11},{10,... | collective-permute-start | bytes 1179656 | tf_op jit(solution)/shard_map/ppermute | solution.py:579
  107.7 9.2 %collective-permute-start.17 = (f32[128,512]{1,0:T(8,128)S(1)}, f32[128,512]{1,0:T(8,128)S(1)}, u32[]{:S(2)}, u32[]{:S(2)}) collective-permute-start(f32[128,512]{1,0:T(8,128)S(1)} %get-tuple-element.156), channel_id=1, source_target_pairs={{0,16},{1,17},{2,18},{3,19},{4,20},{5,21},{6,22},{7,23},{8,9},{9,8... | collective-permute-start | bytes 786440 | tf_op jit(solution)/shard_map/ppermute | solution.py:579
  109.3 12.1 %collective-permute-start.18 = (f32[128,512]{1,0:T(8,128)S(1)}, f32[128,512]{1,0:T(8,128)S(1)}, u32[]{:S(2)}, u32[]{:S(2)}) collective-permute-start(f32[128,512]{1,0:T(8,128)S(1)} %get-tuple-element.158), channel_id=1, source_target_pairs={{0,4},{1,5},{2,6},{3,7},{4,0},{5,1},{6,2},{7,3},{8,12},{9,13},{10,... | collective-permute-start | bytes 786440 | tf_op jit(solution)/shard_map/ppermute | solution.py:579
  123.6 9.9 %collective-permute-start.23 = (f32[128,1152]{1,0:T(8,128)S(1)}, f32[128,1152]{1,0:T(8,128)S(1)}, u32[]{:S(2)}, u32[]{:S(2)}) collective-permute-start(f32[128,1152]{1,0:T(8,128)S(1)} %get-tuple-element.168), channel_id=1, source_target_pairs={{0,16},{1,17},{2,18},{3,19},{4,20},{5,21},{6,22},{7,23},{8,9},{9,8... | collective-permute-start | bytes 1769480 | tf_op jit(solution)/shard_map/ppermute | solution.py:579
  124.1 9.1 %collective-permute-start.20 = (f32[96,512]{1,0:T(8,128)S(1)}, f32[96,512]{1,0:T(8,128)S(1)}, u32[]{:S(2)}, u32[]{:S(2)}) collective-permute-start(f32[96,512]{1,0:T(8,128)S(1)} %get-tuple-element.161.refs_0_), channel_id=1, source_target_pairs={{0,4},{1,5},{2,6},{3,7},{4,0},{5,1},{6,2},{7,3},{8,12},{9,13},{10,... | collective-permute-start | bytes 589832 | tf_op jit(solution)/shard_map/ppermute | solution.py:579
  124.7 6.2 %collective-permute-start.21 = (f32[64,512]{1,0:T(8,128)S(1)}, f32[64,512]{1,0:T(8,128)S(1)}, u32[]{:S(2)}, u32[]{:S(2)}) collective-permute-start(f32[64,512]{1,0:T(8,128)S(1)} %get-tuple-element.164), channel_id=1, source_target_pairs={{0,2},{1,3},{2,0},{3,1},{4,6},{5,7},{6,4},{7,5},{8,10},{9,11},{10,... | collective-permute-start | bytes 393224 | tf_op jit(solution)/shard_map/ppermute | solution.py:579
  125.0 6.2 %collective-permute-start.22 = (f32[64,512]{1,0:T(8,128)S(1)}, f32[64,512]{1,0:T(8,128)S(1)}, u32[]{:S(2)}, u32[]{:S(2)}) collective-permute-start(f32[64,512]{1,0:T(8,128)S(1)} %get-tuple-element.166), channel_id=1, source_target_pairs={{0,1},{1,0},{2,3},{3,2},{4,5},{5,4},{6,7},{7,6},{8,24},{9,25},{10,... | collective-permute-start | bytes 393224 | tf_op jit(solution)/shard_map/ppermute | solution.py:579
  133.7 14.3 %collective-permute-start.27 = (f32[64,1152]{1,0:T(8,128)S(1)}, f32[64,1152]{1,0:T(8,128)S(1)}, u32[]{:S(2)}, u32[]{:S(2)}) collective-permute-start(f32[64,1152]{1,0:T(8,128)S(1)} %get-tuple-element.175), channel_id=1, source_target_pairs={{0,2},{1,3},{2,0},{3,1},{4,6},{5,7},{6,4},{7,5},{8,10},{9,11},{10,... | collective-permute-start | bytes 884744 | tf_op jit(solution)/shard_map/ppermute | solution.py:579
  134.1 13.9 %collective-permute-start.24 = (f32[96,512]{1,0:T(8,128)S(1)}, f32[96,512]{1,0:T(8,128)S(1)}, u32[]{:S(2)}, u32[]{:S(2)}) collective-permute-start(f32[96,512]{1,0:T(8,128)S(1)} %get-tuple-element.169.refs_0_.refs_2_), channel_id=1, source_target_pairs={{0,4},{1,5},{2,6},{3,7},{4,0},{5,1},{6,2},{7,3},{8,12},{9,13},{10,... | collective-permute-start | bytes 589832 | tf_op jit(solution)/shard_map/ppermute | solution.py:579
  136.1 11.8 %collective-permute-start.25 = (f32[32,512]{1,0:T(8,128)S(1)}, f32[32,512]{1,0:T(8,128)S(1)}, u32[]{:S(2)}, u32[]{:S(2)}) collective-permute-start(f32[32,512]{1,0:T(8,128)S(1)} %get-tuple-element.171), channel_id=1, source_target_pairs={{0,4},{1,5},{2,6},{3,7},{4,0},{5,1},{6,2},{7,3},{8,12},{9,13},{10,... | collective-permute-start | bytes 196616 | tf_op jit(solution)/shard_map/ppermute | solution.py:579
  137.0 11.0 %collective-permute-start.26 = (f32[32,512]{1,0:T(8,128)S(1)}, f32[32,512]{1,0:T(8,128)S(1)}, u32[]{:S(2)}, u32[]{:S(2)}) collective-permute-start(f32[32,512]{1,0:T(8,128)S(1)} %get-tuple-element.173), channel_id=1, source_target_pairs={{0,16},{1,17},{2,18},{3,19},{4,20},{5,21},{6,22},{7,23},{8,9},{9,8... | collective-permute-start | bytes 196616 | tf_op jit(solution)/shard_map/ppermute | solution.py:579
  138.5 5.8 %collective-permute-start.10 = (f32[4,3,512]{2,1,0:T(4,128)S(1)}, f32[4,3,512]{2,1,0:T(4,128)S(1)}, u32[]{:S(2)}, u32[]{:S(2)}) collective-permute-start(f32[4,3,512]{2,1,0:T(4,128)S(1)} %get-tuple-element.139), channel_id=1, source_target_pairs={{1,0},{2,1},{3,2},{4,3},{5,4},{6,5},{7,6},{9,8},{10,9},{11,10},{12... | collective-permute-start | bytes 73736 | tf_op jit(solution)/shard_map/ppermute | solution.py:889
  149.1 11.8 %collective-permute-start.28 = (f32[192,512]{1,0:T(8,128)S(1)}, f32[192,512]{1,0:T(8,128)S(1)}, u32[]{:S(2)}, u32[]{:S(2)}) collective-permute-start(f32[192,512]{1,0:T(8,128)S(1)} %get-tuple-element.176.refs_0_.refs_1_), channel_id=1, source_target_pairs={{0,2},{1,3},{2,0},{3,1},{4,6},{5,7},{6,4},{7,5},{8,10},{9,11},{10,... | collective-permute-start | bytes 1179656 | tf_op jit(solution)/shard_map/ppermute | solution.py:579
  149.7 9.8 %collective-permute-start.31 = (f32[32,1152]{1,0:T(8,128)S(1)}, f32[32,1152]{1,0:T(8,128)S(1)}, u32[]{:S(2)}, u32[]{:S(2)}) collective-permute-start(f32[32,1152]{1,0:T(8,128)S(1)} %get-tuple-element.180), channel_id=1, source_target_pairs={{0,4},{1,5},{2,6},{3,7},{4,0},{5,1},{6,2},{7,3},{8,12},{9,13},{10,... | collective-permute-start | bytes 442376 | tf_op jit(solution)/shard_map/ppermute | solution.py:579
  151.9 7.6 %collective-permute-start.29 = (f32[32,512]{1,0:T(8,128)S(1)}, f32[32,512]{1,0:T(8,128)S(1)}, u32[]{:S(2)}, u32[]{:S(2)}) collective-permute-start(f32[32,512]{1,0:T(8,128)S(1)} %get-tuple-element.177.refs_3_), channel_id=1, source_target_pairs={{0,4},{1,5},{2,6},{3,7},{4,0},{5,1},{6,2},{7,3},{8,12},{9,13},{10,... | collective-permute-start | bytes 196616 | tf_op jit(solution)/shard_map/ppermute | solution.py:579
  152.6 6.9 %collective-permute-start.30 = (f32[32,512]{1,0:T(8,128)S(1)}, f32[32,512]{1,0:T(8,128)S(1)}, u32[]{:S(2)}, u32[]{:S(2)}) collective-permute-start(f32[32,512]{1,0:T(8,128)S(1)} %get-tuple-element.178.refs_5_), channel_id=1, source_target_pairs={{0,16},{1,17},{2,18},{3,19},{4,20},{5,21},{6,22},{7,23},{8,9},{9,8... | collective-permute-start | bytes 196616 | tf_op jit(solution)/shard_map/ppermute | solution.py:579
  161.0 13.5 %collective-permute-start.32 = (f32[384,512]{1,0:T(8,128)S(1)}, f32[384,512]{1,0:T(8,128)S(1)}, u32[]{:S(2)}, u32[]{:S(2)}) collective-permute-start(f32[384,512]{1,0:T(8,128)S(1)} %get-tuple-element.181.refs_0_.refs_1_), channel_id=1, source_target_pairs={{0,16},{1,17},{2,18},{3,19},{4,20},{5,21},{6,22},{7,23},{8,9},{9,8... | collective-permute-start | bytes 2359304 | tf_op jit(solution)/shard_map/ppermute | solution.py:579
  163.0 10.3 %collective-permute-start.35 = (f32[32,1152]{1,0:T(8,128)S(1)}, f32[32,1152]{1,0:T(8,128)S(1)}, u32[]{:S(2)}, u32[]{:S(2)}) collective-permute-start(f32[32,1152]{1,0:T(8,128)S(1)} %get-tuple-element.184.refs_7_), channel_id=1, source_target_pairs={{0,4},{1,5},{2,6},{3,7},{4,0},{5,1},{6,2},{7,3},{8,12},{9,13},{10,... | collective-permute-start | bytes 442376 | tf_op jit(solution)/shard_map/ppermute | solution.py:579
  165.4 5.9 %collective-permute-start.33 = (f32[64,512]{1,0:T(8,128)S(1)}, f32[64,512]{1,0:T(8,128)S(1)}, u32[]{:S(2)}, u32[]{:S(2)}) collective-permute-start(f32[64,512]{1,0:T(8,128)S(1)} %get-tuple-element.182.refs_3_), channel_id=1, source_target_pairs={{0,2},{1,3},{2,0},{3,1},{4,6},{5,7},{6,4},{7,5},{8,10},{9,11},{10,... | collective-permute-start | bytes 393224 | tf_op jit(solution)/shard_map/ppermute | solution.py:579
  166.8 6.4 %collective-permute-start.34 = (f32[64,512]{1,0:T(8,128)S(1)}, f32[64,512]{1,0:T(8,128)S(1)}, u32[]{:S(2)}, u32[]{:S(2)}) collective-permute-start(f32[64,512]{1,0:T(8,128)S(1)} %get-tuple-element.183.refs_5_), channel_id=1, source_target_pairs={{0,1},{1,0},{2,3},{3,2},{4,5},{5,4},{6,7},{7,6},{8,24},{9,25},{10,... | collective-permute-start | bytes 393224 | tf_op jit(solution)/shard_map/ppermute | solution.py:579
  174.7 22.8 %collective-permute-start.36 = (f32[768,512]{1,0:T(8,128)S(1)}, f32[768,512]{1,0:T(8,128)S(1)}, u32[]{:S(2)}, u32[]{:S(2)}) collective-permute-start(f32[768,512]{1,0:T(8,128)S(1)} %get-tuple-element.185.refs_0_.refs_1_), channel_id=1, source_target_pairs={{0,1},{1,0},{2,3},{3,2},{4,5},{5,4},{6,7},{7,6},{8,24},{9,25},{10,... | collective-permute-start | bytes 4718600 | tf_op jit(solution)/shard_map/ppermute | solution.py:579
  177.4 14.1 %collective-permute-start.39 = (f32[64,1152]{1,0:T(8,128)S(1)}, f32[64,1152]{1,0:T(8,128)S(1)}, u32[]{:S(2)}, u32[]{:S(2)}) collective-permute-start(f32[64,1152]{1,0:T(8,128)S(1)} %get-tuple-element.188.refs_6_), channel_id=1, source_target_pairs={{0,2},{1,3},{2,0},{3,1},{4,6},{5,7},{6,4},{7,5},{8,10},{9,11},{10,... | collective-permute-start | bytes 884744 | tf_op jit(solution)/shard_map/ppermute | solution.py:579
  178.6 9.4 %collective-permute-start.37 = (f32[128,512]{1,0:T(8,128)S(1)}, f32[128,512]{1,0:T(8,128)S(1)}, u32[]{:S(2)}, u32[]{:S(2)}) collective-permute-start(f32[128,512]{1,0:T(8,128)S(1)} %get-tuple-element.186.refs_2_), channel_id=1, source_target_pairs={{0,16},{1,17},{2,18},{3,19},{4,20},{5,21},{6,22},{7,23},{8,9},{9,8... | collective-permute-start | bytes 786440 | tf_op jit(solution)/shard_map/ppermute | solution.py:579
  180.8 10.7 %collective-permute-start.38 = (f32[128,512]{1,0:T(8,128)S(1)}, f32[128,512]{1,0:T(8,128)S(1)}, u32[]{:S(2)}, u32[]{:S(2)}) collective-permute-start(f32[128,512]{1,0:T(8,128)S(1)} %get-tuple-element.187.refs_4_), channel_id=1, source_target_pairs={{0,4},{1,5},{2,6},{3,7},{4,0},{5,1},{6,2},{7,3},{8,12},{9,13},{10,... | collective-permute-start | bytes 786440 | tf_op jit(solution)/shard_map/ppermute | solution.py:579
  184.0 18.9 %collective-permute-start.40 = (f32[768,512]{1,0:T(8,128)S(1)}, f32[768,512]{1,0:T(8,128)S(1)}, u32[]{:S(2)}, u32[]{:S(2)}) collective-permute-start(f32[768,512]{1,0:T(8,128)S(1)} %get-tuple-element.185.refs_0_.refs_1_), channel_id=1, source_target_pairs={{0,8},{1,9},{2,10},{3,11},{4,12},{5,13},{6,14},{7,15},{8,0},{9,1},... | collective-permute-start | bytes 4718600 | tf_op jit(solution)/shard_map/ppermute | solution.py:579
  197.6 5.2 %collective-permute-start.41 = (f32[768,512]{1,0:T(8,128)S(1)}, f32[768,512]{1,0:T(8,128)S(1)}, u32[]{:S(2)}, u32[]{:S(2)}) collective-permute-start(f32[768,512]{1,0:T(8,128)S(1)} %get-tuple-element.190.refs_2_), channel_id=1, source_target_pairs={{0,8},{1,9},{2,10},{3,11},{4,12},{5,13},{6,14},{7,15},{8,0},{9,1},... | collective-permute-start | bytes 4718600 | tf_op jit(solution)/shard_map/ppermute | solution.py:579
  197.7 15.8 %collective-permute-start.44 = (f32[128,1152]{1,0:T(8,128)S(1)}, f32[128,1152]{1,0:T(8,128)S(1)}, u32[]{:S(2)}, u32[]{:S(2)}) collective-permute-start(f32[128,1152]{1,0:T(8,128)S(1)} %get-tuple-element.193.refs_4_), channel_id=1, source_target_pairs={{0,16},{1,17},{2,18},{3,19},{4,20},{5,21},{6,22},{7,23},{8,9},{9,8... | collective-permute-start | bytes 1769480 | tf_op jit(solution)/shard_map/ppermute | solution.py:579
  199.3 14.2 %collective-permute-start.43 = (f32[256,512]{1,0:T(8,128)S(1)}, f32[256,512]{1,0:T(8,128)S(1)}, u32[]{:S(2)}, u32[]{:S(2)}) collective-permute-start(f32[256,512]{1,0:T(8,128)S(1)} %get-tuple-element.192.refs_5_), channel_id=1, source_target_pairs={{0,2},{1,3},{2,0},{3,1},{4,6},{5,7},{6,4},{7,5},{8,10},{9,11},{10,... | collective-permute-start | bytes 1572872 | tf_op jit(solution)/shard_map/ppermute | solution.py:579
  201.1 12.4 %collective-permute-start.42 = (f32[256,512]{1,0:T(8,128)S(1)}, f32[256,512]{1,0:T(8,128)S(1)}, u32[]{:S(2)}, u32[]{:S(2)}) collective-permute-start(f32[256,512]{1,0:T(8,128)S(1)} %get-tuple-element.189.refs_0_.refs_1_), channel_id=1, source_target_pairs={{0,1},{1,0},{2,3},{3,2},{4,5},{5,4},{6,7},{7,6},{8,24},{9,25},{10,... | collective-permute-start | bytes 1572872 | tf_op jit(solution)/shard_map/ppermute | solution.py:579
  215.8 16.3 %collective-permute-start.49 = (f32[256,1152]{1,0:T(8,128)S(1)}, f32[256,1152]{1,0:T(8,128)S(1)}, u32[]{:S(2)}, u32[]{:S(2)}) collective-permute-start(f32[256,1152]{1,0:T(8,128)S(1)} %get-tuple-element.194.refs_0_.refs_1_), channel_id=1, source_target_pairs={{0,1},{1,0},{2,3},{3,2},{4,5},{5,4},{6,7},{7,6},{8,24},{9,25},{10,... | collective-permute-start | bytes 3538952 | tf_op jit(solution)/shard_map/ppermute | solution.py:579
  217.7 3.6 %collective-permute-start.48 = (f32[256,512]{1,0:T(8,128)S(1)}, f32[256,512]{1,0:T(8,128)S(1)}, u32[]{:S(2)}, u32[]{:S(2)}) collective-permute-start(f32[256,512]{1,0:T(8,128)S(1)} %get-tuple-element.196.refs_6_), channel_id=1, source_target_pairs={{0,8},{1,9},{2,10},{3,11},{4,12},{5,13},{6,14},{7,15},{8,0},{9,1},... | collective-permute-start | bytes 1572872 | tf_op jit(solution)/shard_map/ppermute | solution.py:579
  219.0 14.6 %collective-permute-start.50 = (f32[256,1152]{1,0:T(8,128)S(1)}, f32[256,1152]{1,0:T(8,128)S(1)}, u32[]{:S(2)}, u32[]{:S(2)}) collective-permute-start(f32[256,1152]{1,0:T(8,128)S(1)} %get-tuple-element.194.refs_0_.refs_1_), channel_id=1, source_target_pairs={{0,8},{1,9},{2,10},{3,11},{4,12},{5,13},{6,14},{7,15},{8,0},{9,1},... | collective-permute-start | bytes 3538952 | tf_op jit(solution)/shard_map/ppermute | solution.py:579
  (32 other events, 248.5 us)
